TPU v7x, 256 devices: a whole 4x4x8 slice. The times are simulated.
256 devices in a mesh: ex: 32 (over y, z), tp: 8 (over x, core).
Axes of the slice: x: 4, y: 4, z: 8, core: 2. Of those that a mesh axis runs over, the one named last changes fastest.
Arguments:
- down_matrix_feeds: bfloat16 [32768, 28672], P('ex', 'tp'), may hold values from -6 to 6
- result_slope_matrix: bfloat16 [32768, 8192], P('ex', 'tp'), may hold values from -6 to 6
- feed_sketch_factor: bfloat16 [28672, 64], P('tp'), may hold values from -0.03125 to 0.03125
- result_slope_factor: bfloat16 [8192, 64], P('tp'), may hold values from -0.0625 to 0.0625
- heldout_slope_entries: bfloat16 [2048, 4096], P('ex', 'tp'), may hold values from -0.01171875 to 0.01171875
- objective_of_sample: int32 [512], P('ex'), may hold values from 0 to 2047
- kept_choice_flags: int32 [2048], replicated, may hold values 0 or 1
- token_sample_position: int32 [32, 1024], P('ex'), may hold values from 0 to 15, never falling along the last dimension, each value on 1 to 128 neighbouring positions
Outputs:
- sample_affinity: float32 [512, 2048], P('ex')
- totals: float32 [2048], P('ex')
Inputs may be any that keep to these rules, and one draw needn't show every extreme that they name: `token_sample_position`: each row runs from 0 to 15 without falling; each example has 1 to 128 tokens, and one of each row has exactly 128.
All inputs are finite; a program needn't handle non-finite values.
Results may differ from a plain program's by a relative error of at most 0.0031.
Values may be sent and summed in bfloat16 or wider, within the bound.
No kernel may reach another device: no remote copies, remote signals or barrier semaphores. Data moves between devices by JAX's collectives and lax.ppermute only.
A program may use at most 128 MiB of HBM per device.

v0:
```python
import jax
import jax.numpy as jnp
from jax import lax
from jax.sharding import PartitionSpec as P


def score_rows(examples_part, candidates_part):
    return lax.dot_general(
        examples_part, candidates_part, (((1,), (1,)), ((), ())), preferred_element_type=jnp.float32
    )


def per_device(
    down_matrix_feeds,
    result_slope_matrix,
    feed_sketch_factor,
    result_slope_factor,
    heldout_slope_entries,
    objective_of_sample,
    kept_choice_flags,
    token_sample_position,
):
    tok_rows = down_matrix_feeds.shape[0]
    examples = objective_of_sample.shape[0]
    objective_choice_slot = kept_choice_flags.shape[0]
    in_part = jnp.dot(down_matrix_feeds, feed_sketch_factor, preferred_element_type=jnp.float32)
    out_part = jnp.dot(result_slope_matrix, result_slope_factor, preferred_element_type=jnp.float32)
    labels = lax.broadcasted_iota(jnp.int32, (examples, tok_rows), 0)
    onehot = (token_sample_position[0][None, :] == labels).astype(jnp.float32)
    left_side, out_full = lax.psum((in_part, out_part), "tp")
    local_valid = lax.all_gather(heldout_slope_entries, "tp", axis=1, tiled=True)
    weighted = onehot[:, None, :] * left_side.T[None, :, :]
    grads = jnp.einsum("eit,tj->eij", weighted, out_full, precision=lax.Precision.HIGHEST)
    per_example = grads.reshape(examples, -1).astype(jnp.bfloat16)
    sample_affinity = score_rows(per_example, lax.all_gather(local_valid, "ex", axis=0, tiled=True))
    sample_affinity = sample_affinity * kept_choice_flags.astype(jnp.float32)[None, :]
    columns = lax.broadcasted_iota(jnp.int32, (examples, objective_choice_slot), 1)
    chosen = (objective_of_sample[:, None] == columns).astype(jnp.float32)
    partial_totals = jnp.sum(chosen * sample_affinity, axis=0)
    totals = lax.psum_scatter(partial_totals, "ex", scatter_dimension=0, tiled=True)
    return (sample_affinity, totals)


def solution(mesh):
    placed = (
        P("ex", "tp"),
        P("ex", "tp"),
        P("tp", None),
        P("tp", None),
        P("ex", "tp"),
        P("ex"),
        P(),
        P("ex", None),
    )
    return jax.shard_map(
        per_device, mesh=mesh, in_specs=placed, out_specs=(P("ex", None), P("ex")), check_vma=False
    )
```

profile of v0, /device:TPU:2, one launch (start us, length us, event | category | flops | bytes accessed | tf_op | source)
XLA Modules:
  0.0 267.1 jit_solution(271592909221365448)
XLA Ops:
  8.0 0.0 copy-start
  8.0 0.0 copy-start.5
  8.0 0.0 copy-start.1
  8.0 0.0 copy-start.2
  8.0 0.0 copy-start.3
  8.1 0.0 copy-start.4
  8.1 0.0 all-reduce.4.cloned.1.call-start
  8.1 1.5 copy-done
  9.6 2.4 fusion.10
  12.0 6.3 %fusion.9 = f32[64,1024]{1,0:T(8,128)} fusion(bf16[3584,64]{0,1:T(8,128)(2,1)} %param.10, bf16[1024,3584]{1,0:T(8,128)(2,1)} %param.8), kind=kOutput, calls=%fused_computation.11 | convolution fusion | flops 469762048 | bytes 8060928 | tf_op jit(solution)/shard_map/dot_general | solution.py:26
  18.3 0.0 all-reduce.4.cloned.1.call-update
  18.3 0.0 all-gather.2.cloned.1.call-start
  18.4 0.0 copy-done.1
  18.4 14.3 %all_gather.6 = bf16[64,4096]{1,0:T(8,128)(2,1)} all-gather(bf16[64,512]{1,0:T(8,128)(2,1)S(1)} %copy-done.1), channel_id=1, replica_groups=mesh['ex'=32,'tp'=8] {'tp'}, dimensions={1}, use_global_device_ids=true | all-gather | bytes 589824 | tf_op jit(solution)/shard_map/all_gather | solution.py:31
  32.7 0.0 all-gather.2.cloned.1.call-update
  32.7 0.0 copy-done.2
  32.7 0.0 copy-done.5
  32.7 0.6 dynamic-slice
  34.0 0.0 copy-done.3
  34.0 51.8 %all-reduce.4.cloned.1.call-done = (f32[64,1024]{1,0:T(8,128)}, f32[1024,64]{0,1:T(8,128)}) async-done(((f32[64,1024]{1,0:T(8,128)}, f32[1024,64]{0,1:T(8,128)}), (f32[64,1024]{1,0:T(8,128)}, f32[1024,64]{0,1:T(8,128)})) %all-reduce.4.cloned.1.call-update) | async-done | bytes 524304 | tf_op jit(solution)/shard_map/psum | solution.py:30
  85.8 4.4 %fusion.4 = bf16[16,64,64]{2,1,0:T(8,128)(2,1)S(1)} fusion(f32[64,1024]{1,0:T(8,128)} %get-tuple-element.2, f32[16,1024]{1,0:T(8,128)S(1)} %fusion.8, f32[1024,64]{0,1:T(8,128)} %get-tuple-element.3), kind=kOutput, calls=%fused_computation.5 | convolution fusion | flops 806420480 | bytes 720896 | tf_op jit(solution)/shard_map/eit,tj->eij/dot_general | solution.py:33
  90.2 0.3 convert_element_type.19
  90.5 85.3 %all-gather.2.cloned.1.call-done = bf16[2048,4096]{1,0:T(8,128)(2,1)} async-done(((bf16[64,4096]{1,0:T(8,128)(2,1)}), bf16[2048,4096]{1,0:T(8,128)(2,1)}) %all-gather.2.cloned.1.call-update) | async-done | bytes 16777232 | tf_op jit(solution)/shard_map/all_gather | solution.py:35
  175.8 0.0 copy-done.4
  175.8 10.9 %select_reduce_fusion = (f32[2048]{0:T(1024)S(1)}, f32[16,2048]{1,0:T(8,128)}) fusion(s32[16]{0:T(128)S(1)} %copy-done.4, f32[2048]{0:T(1024)S(1)} %convert_element_type.20, bf16[16,4096]{1,0:T(8,128)(2,1)S(1)} %convert_element_type.19, bf16[2048,4096]{1,0:T(8,128)(2,1)} %all-gather.2.cloned.1.call-done), kind=kOutput, calls=%fused_computation.7 | convolution fusion | flops 268564480 | bytes 17055808 | tf_op jit(solution)/shard_map/dot_general | solution.py:8
  186.7 72.3 %all-reduce = f32[2048]{0:T(1024)S(1)} all-reduce(f32[2048]{0:T(1024)S(1)} %get-tuple-element.4), channel_id=2, replica_groups=mesh['ex'=32,'tp'=8] {'ex'}, use_global_device_ids=true, to_apply=%region_3.0.clone | all-reduce | flops 2048 | bytes 16384
  259.0 0.6 dynamic-slice.1
  (2 shorter events, 0.0 us)
Async XLA Ops:
  8.0 1.6 copy-start
  8.0 24.7 %copy-start.5 = (u32[256]{0:T(256)S(1)}, u32[256]{0:T(256)}, u32[]{:S(2)}) copy-start(u32[256]{0:T(256)} %constant.7) | copy-start | bytes 3076
  8.0 10.3 %copy-start.1 = (bf16[64,512]{1,0:T(8,128)(2,1)S(1)}, bf16[64,512]{1,0:T(8,128)(2,1)}, u32[]{:S(2)}) copy-start(bf16[64,512]{1,0:T(8,128)(2,1)} %param.12) | copy-start | bytes 196612
  8.0 24.7 %copy-start.2 = (s32[2048]{0:T(1024)S(1)}, s32[2048]{0:T(1024)}, u32[]{:S(2)}) copy-start(s32[2048]{0:T(1024)} %param.14) | copy-start | bytes 24580
  8.0 25.9 %copy-start.3 = (s32[1,1024]{1,0:T(1,128)S(1)}, s32[1,1024]{1,0:T(1,128)}, u32[]{:S(2)}) copy-start(s32[1,1024]{1,0:T(1,128)} %param.15) | copy-start | bytes 12292
  8.1 167.8 %copy-start.4 = (s32[16]{0:T(128)S(1)}, s32[16]{0:T(128)}, u32[]{:S(2)}) copy-start(s32[16]{0:T(128)} %param.13) | copy-start | bytes 196
  8.1 77.7 %all-reduce.4.cloned.1.call-start = ((), (), s32[]{:S(2)}) async-start(), calls=%async_computation.1 | async-start | bytes 1048576 | tf_op jit(solution)/shard_map/psum | solution.py:30
  18.3 157.5 %all-gather.2.cloned.1.call-start = ((), (), s32[]{:S(2)}) async-start(), calls=%async_computation | async-start | bytes 17301504 | tf_op jit(solution)/shard_map/all_gather | solution.py:35
Sparse Core Ops, SparseCore 0:
  18.4 67.3 all-reduce.3
Sparse Core Ops, SparseCore 1:
  32.8 143.0 all-gather.1
where the time goes:
time: 267 us
  waiting for transfers between devices  137 us (51%)
  blocking collectives  86.6 us (32%)
  matrix products  23.9 us (9%)
  between operations  16.3 us (6%)
  local copies, waits for them, and re-layouts  3.01 us (1%)
    all_gather x1, waiting for transfers between devices, per_device(): lax.all_gather(local_valid, 'ex', axis=0, tiled=True)  85.3 us
    unnamed x1, blocking collectives  72.3 us
    psum x1, waiting for transfers between devices, per_device(): left_side, out_full = lax.psum((in_part, out_part), 'tp')  51.8 us
    all_gather x1, blocking collectives, per_device(): lax.all_gather(heldout_slope_entries, 'tp', axis=1, tiled=True)  14.3 us
    dot_general x1, matrix products, score_rows(): lax.dot_general(examples_part, candidates_part, (((1,), (1,)), ((), ())),...  10.9 us
    dot_general x1, matrix products, per_device(): jnp.dot(down_matrix_feeds, feed_sketch_factor, preferred_element_type=jnp...  6.28 us
  transfers between devices with their start and end apart: 2, of which 2 were waited for; matrix products, arithmetic and copies ran while one was open for 2% of the time, Pallas kernels for 0%

commit v1 on v0

v1 whole, which is shorter than its diff:
```python
import jax
import jax.numpy as jnp
from jax import lax
from jax.sharding import PartitionSpec as P

NY, NZ, NX = 4, 8, 4
F32, BF16 = jnp.float32, jnp.bfloat16


def tp_swap(value, bits):
    return lax.ppermute(value, "tp", [(i, i ^ bits) for i in range(2 * NX)])


def y_swap(value, bits):
    return lax.ppermute(value, "ex", [(i, i ^ (bits * NZ)) for i in range(NY * NZ)])


def z_shift(value, step):
    return lax.ppermute(
        value, "ex", [(y * NZ + z, y * NZ + (z + step) % NZ) for y in range(NY) for z in range(NZ)]
    )


def split_two(value):
    high = lax.reduce_precision(value, 8, 7)
    return high.astype(BF16), (value - high).astype(BF16)


def pick(pair, index):
    return jnp.where(index == 0, pair[0], pair[1])


def per_device(
    down_matrix_feeds,
    result_slope_matrix,
    feed_sketch_factor,
    result_slope_factor,
    heldout_slope_entries,
    objective_of_sample,
    kept_choice_flags,
    token_sample_position,
):
    tokens = down_matrix_feeds.shape[0]
    rank = feed_sketch_factor.shape[1]
    examples = objective_of_sample.shape[0]
    choices = kept_choice_flags.shape[0]
    own_choices = heldout_slope_entries.shape[0]
    tp, ex = lax.axis_index("tp"), lax.axis_index("ex")
    x, core, y, z = tp // 2, tp % 2, ex // NZ, ex % NZ

    held = jnp.stack([heldout_slope_entries] + [y_swap(heldout_slope_entries, d) for d in (1, 2, 3)])
    up = down = held
    blocks = {0: held}
    for step in range(1, NZ // 2 + 1):
        up = z_shift(up, 1)
        blocks[step] = up
        if step < NZ // 2:
            down = z_shift(down, -1)
            blocks[NZ - step] = down

    nt = (((0,), (1,)), ((), ()))
    in_part = lax.dot_general(feed_sketch_factor, down_matrix_feeds, nt, preferred_element_type=F32)
    out_part = lax.dot_general(result_slope_factor, result_slope_matrix, nt, preferred_element_type=F32)

    rows = rank // (2 * NX)
    in_cores = in_part.reshape(NX, 2, rows, tokens)
    in_cores = (in_cores[:, 0].reshape(NX * rows, tokens), in_cores[:, 1].reshape(NX * rows, tokens))
    out_cores = (out_part[: rank // 2], out_part[rank // 2 :])
    both = [jnp.concatenate([i, o], 0) for i, o in zip(in_cores, out_cores)]
    mine = pick(both, core) + tp_swap(pick(both, 1 - core), 1)
    in_chip, out_chip = mine[: NX * rows].reshape(NX, rows, tokens), mine[NX * rows :]
    out_sent = out_chip.astype(BF16)
    in_own = lax.dynamic_index_in_dim(in_chip, x, 0, False)
    got = []
    for d in (1, 2, 3):
        part = lax.dynamic_index_in_dim(in_chip, x ^ d, 0, False)
        got.append(tp_swap(jnp.concatenate([*split_two(part), out_sent], 0), 2 * d).astype(F32))
    in_sum = in_own + sum(g[:rows] + g[rows : 2 * rows] for g in got)
    out_half = out_chip + sum(g[2 * rows :] for g in got)
    out_other = tp_swap(out_half, 1)
    out_sum = jnp.where(core == 0, jnp.concatenate([out_half, out_other], 0), jnp.concatenate([out_other, out_half], 0))

    labels = lax.broadcasted_iota(jnp.int32, (examples, tokens), 0)
    onehot = (token_sample_position[0][None, :] == labels).astype(F32)
    weighted = (onehot[:, None, :] * in_sum[None, :, :]).reshape(examples * rows, tokens)
    grads = lax.dot_general(
        weighted, out_sum, (((1,), (1,)), ((), ())), precision=lax.Precision.HIGHEST, preferred_element_type=F32
    )
    per_example = jnp.concatenate(split_two(grads.reshape(examples, rows * rank)), 0)

    scores = []
    for k in range(NZ):
        block = blocks[k].reshape(NY * own_choices, -1)
        s = lax.dot_general(per_example, block, (((1,), (1,)), ((), ())), preferred_element_type=F32)
        scores.append((s[:examples] + s[examples:]).reshape(examples, NY, 1, own_choices))
    scores = scores[::-1]
    shift = z + 1
    for bit in (1, 2, 4):
        turned = [scores[(m - bit) % NZ] for m in range(NZ)]
        scores = [jnp.where((shift & bit) != 0, t, s) for t, s in zip(turned, scores)]
    scores = jnp.concatenate(scores, 2)
    for bit in (1, 2):
        turned = jnp.concatenate([scores[:, m ^ bit : (m ^ bit) + 1] for m in range(NY)], 1)
        scores = jnp.where((y & bit) != 0, turned, scores)
    scores = scores.reshape(examples, choices)

    halves = (scores[:, : choices // 2], scores[:, choices // 2 :])
    mine = pick(halves, core) + tp_swap(pick(halves, 1 - core), 1)
    mine = (mine + tp_swap(mine, 2)) + (tp_swap(mine, 4) + tp_swap(mine, 6))
    other = tp_swap(mine, 1)
    flags = kept_choice_flags.astype(F32)[None, :]
    sample_affinity = flags * jnp.where(
        core == 0, jnp.concatenate([mine, other], 1), jnp.concatenate([other, mine], 1)
    )

    columns = lax.broadcasted_iota(jnp.int32, (examples, choices), 1)
    chosen = (objective_of_sample[:, None] == columns).astype(F32)
    partial_totals = jnp.sum(chosen * sample_affinity, axis=0).reshape(NY * NZ, own_choices)
    totals = jnp.sum(lax.all_to_all(partial_totals, "ex", 0, 0, tiled=True), axis=0)
    return (sample_affinity, totals)


def solution(mesh):
    placed = (
        P("ex", "tp"),
        P("ex", "tp"),
        P("tp", None),
        P("tp", None),
        P("ex", "tp"),
        P("ex"),
        P(),
        P("ex", None),
    )
    return jax.shard_map(
        per_device, mesh=mesh, in_specs=placed, out_specs=(P("ex", None), P("ex")), check_vma=False
    )
```

time: 267 us -> 89.1 us (0.33)
  the two profiles are of different devices: /device:TPU:2 before, /device:TPU:1 now
where the time goes in v1:
time: 89.1 us; the launch traced here: 88.8 us
  starting transfers between devices  32.2 us (36%)
  waiting for transfers between devices  21.8 us (24%)
  blocking collectives  14.8 us (17%)
  matrix products  11.2 us (13%)
  other arithmetic  6.02 us (7%)
  local copies, waits for them, and re-layouts  1.57 us (2%)
  between operations  1.05 us (1%)
    ppermute x10, starting transfers between devices, tp_swap(): return lax.ppermute(value, 'tp', [(i, i ^ bits) for i in range(2 * NX)])  17.6 us
    all_to_all x1, blocking collectives, per_device(): lax.all_to_all(partial_totals, 'ex', 0, 0, tiled=True)  14.8 us
    ppermute x7, waiting for transfers between devices, z_shift(): lax.ppermute(value, 'ex', [(y * NZ + z, y * NZ + (z + step) % NZ) for y i...  11.4 us
    ppermute x7, starting transfers between devices, z_shift(): lax.ppermute(value, 'ex', [(y * NZ + z, y * NZ + (z + step) % NZ) for y i...  11.3 us
    ppermute x10, waiting for transfers between devices, tp_swap(): return lax.ppermute(value, 'tp', [(i, i ^ bits) for i in range(2 * NX)])  7.57 us
    dot_general x1, matrix products, per_device(): lax.dot_general(feed_sketch_factor, down_matrix_feeds, nt, preferred_elem...  5.68 us
    dot_general x8, matrix products, per_device(): lax.dot_general(per_example, block, (((1,), (1,)), ((), ())), preferred_e...  4.23 us
    ppermute x3, starting transfers between devices, y_swap(): lax.ppermute(value, 'ex', [(i, i ^ bits * NZ) for i in range(NY * NZ)])  3.28 us
  transfers between devices with their start and end apart: 20, of which 12 were waited for; matrix products, arithmetic and copies ran while one was open for 10% of the time, Pallas kernels for 0%

profile of v1, /device:TPU:1, one launch (start us, length us, event | category | flops | bytes accessed | tf_op | source)
XLA Modules:
  0.0 88.8 jit_solution(11361041773541963994)
XLA Ops:
  0.7 5.7 %fusion.35 = f32[64,1024]{1,0:T(8,128)S(1)} fusion(bf16[3584,64]{0,1:T(8,128)(2,1)} %param.10, bf16[1024,3584]{1,0:T(8,128)(2,1)} %param.8), kind=kOutput, calls=%fused_computation.109 | convolution fusion | flops 469762048 | bytes 8060928 | tf_op jit(solution)/shard_map/dot_general | solution.py:62
  7.3 3.3 %collective-permute-start = (f32[64,1024]{1,0:T(8,128)S(1)}, f32[64,1024]{1,0:T(8,128)}, u32[]{:S(2)}, u32[]{:S(2)}) collective-permute-start(f32[64,1024]{1,0:T(8,128)S(1)} %fusion.10), channel_id=1, source_target_pairs={{0,1},{1,0},{2,3},{3,2},{4,5},{5,4},{6,7},{7,6},{8,9},{9,8},{10,11... | collective-permute-start | bytes 786440 | tf_op jit(solution)/shard_map/ppermute | solution.py:11
  10.6 1.5 %collective-permute-start.7 = (bf16[64,512]{1,0:T(8,128)(2,1)S(1)}, bf16[64,512]{1,0:T(8,128)(2,1)S(1)}, u32[]{:S(2)}, u32[]{:S(2)}) collective-permute-start(bf16[64,512]{1,0:T(8,128)(2,1)S(1)} %copy-done.2), channel_id=1, source_target_pairs={{0,192},{8,200},{16,208},{24,216},{32,224},{40,232},{48,240},{56,2... | collective-permute-start | bytes 196616 | tf_op jit(solution)/shard_map/ppermute | solution.py:15
  12.1 1.8 %collective-permute-start.6 = (bf16[64,512]{1,0:T(8,128)(2,1)S(1)}, bf16[64,512]{1,0:T(8,128)(2,1)S(1)}, u32[]{:S(2)}, u32[]{:S(2)}) collective-permute-start(bf16[64,512]{1,0:T(8,128)(2,1)S(1)} %copy-done.2), channel_id=1, source_target_pairs={{0,128},{8,136},{16,144},{24,152},{32,160},{40,168},{48,176},{56,1... | collective-permute-start | bytes 196616 | tf_op jit(solution)/shard_map/ppermute | solution.py:15
  14.3 1.0 %collective-permute-done.7 = bf16[64,512]{1,0:T(8,128)(2,1)S(1)} collective-permute-done((bf16[64,512]{1,0:T(8,128)(2,1)S(1)}, bf16[64,512]{1,0:T(8,128)(2,1)S(1)}, u32[]{:S(2)}, u32[]{:S(2)}) %collective-permute-start.7) | collective-permute-done | bytes 65568 | tf_op jit(solution)/shard_map/ppermute | solution.py:15
  15.3 1.4 %collective-permute-done.6 = bf16[64,512]{1,0:T(8,128)(2,1)S(1)} collective-permute-done((bf16[64,512]{1,0:T(8,128)(2,1)S(1)}, bf16[64,512]{1,0:T(8,128)(2,1)S(1)}, u32[]{:S(2)}, u32[]{:S(2)}) %collective-permute-start.6) | collective-permute-done | bytes 65568 | tf_op jit(solution)/shard_map/ppermute | solution.py:15
  16.8 1.7 %collective-permute-start.11 = (bf16[4,64,512]{2,1,0:T(8,128)(2,1)S(1)}, bf16[4,64,512]{2,1,0:T(8,128)(2,1)}, u32[]{:S(2)}, u32[]{:S(2)}) collective-permute-start(bf16[4,64,512]{2,1,0:T(8,128)(2,1)S(1)} %pad_maximum_fusion.2), channel_id=1, source_target_pairs={{0,8},{8,16},{16,24},{24,32},{32,40},{40,48},{48,56},{56,0},{64,72... | collective-permute-start | bytes 786440 | tf_op jit(solution)/shard_map/ppermute | solution.py:19
  18.5 4.0 %collective-permute-start.8 = (bf16[4,64,512]{2,1,0:T(8,128)(2,1)S(1)}, bf16[4,64,512]{2,1,0:T(8,128)(2,1)S(1)}, u32[]{:S(2)}, u32[]{:S(2)}) collective-permute-start(bf16[4,64,512]{2,1,0:T(8,128)(2,1)S(1)} %pad_maximum_fusion.2), channel_id=1, source_target_pairs={{0,56},{8,0},{16,8},{24,16},{32,24},{40,32},{48,40},{56,48},{64,12... | collective-permute-start | bytes 786440 | tf_op jit(solution)/shard_map/ppermute | solution.py:19
  22.5 1.0 %select_add_fusion = f32[64,1024]{1,0:T(8,128)S(1)} fusion(f32[64,1024]{1,0:T(8,128)} %collective-permute-done, f32[32,1024]{1,0:T(8,128)S(1)} %get-tuple-element.23, f32[32,1024]{1,0:T(8,128)S(1)} %get-tuple-element.21, f32[32,1024]{1,0:T(8,128)S(1)} %get-tuple-element.22, f32[32,1024]{1,0:T(8,128)S(1)} %get-tuple-element.20, pred[]{:T(512)S(6)} %eq.35), kind=kLoop, calls=%fused_computation.15 | loop fusion | flops 262144 | bytes 1048577 | tf_op jit(solution)/shard_map/add | solution.py:70
  23.6 1.3 %collective-permute-start.1 = (bf16[48,1024]{1,0:T(8,128)(2,1)S(1)}, bf16[48,1024]{1,0:T(8,128)(2,1)}, u32[]{:S(2)}, u32[]{:S(2)}) collective-permute-start(bf16[48,1024]{1,0:T(8,128)(2,1)S(1)} %get-tuple-element.36), channel_id=1, source_target_pairs={{0,2},{1,3},{2,0},{3,1},{4,6},{5,7},{6,4},{7,5},{8,10},{9,11},{10,... | collective-permute-start | bytes 294920 | tf_op jit(solution)/shard_map/ppermute | solution.py:11
  24.9 2.4 %collective-permute-start.2 = (bf16[48,1024]{1,0:T(8,128)(2,1)S(1)}, bf16[48,1024]{1,0:T(8,128)(2,1)}, u32[]{:S(2)}, u32[]{:S(2)}) collective-permute-start(bf16[48,1024]{1,0:T(8,128)(2,1)S(1)} %get-tuple-element.37), channel_id=1, source_target_pairs={{0,4},{1,5},{2,6},{3,7},{4,0},{5,1},{6,2},{7,3},{8,12},{9,13},{10,... | collective-permute-start | bytes 294920 | tf_op jit(solution)/shard_map/ppermute | solution.py:11
  27.7 2.7 %collective-permute-start.9 = (bf16[4,64,512]{2,1,0:T(8,128)(2,1)S(1)}, bf16[4,64,512]{2,1,0:T(8,128)(2,1)}, u32[]{:S(2)}, u32[]{:S(2)}) collective-permute-start(bf16[4,64,512]{2,1,0:T(8,128)(2,1)S(1)} %collective-permute-done.8), channel_id=1, source_target_pairs={{0,56},{8,0},{16,8},{24,16},{32,24},{40,32},{48,40},{56,48},{64,12... | collective-permute-start | bytes 786440 | tf_op jit(solution)/shard_map/ppermute | solution.py:19
  30.4 0.9 %convert_element_type.52 = f32[48,1024]{1,0:T(8,128)S(1)} convert(bf16[48,1024]{1,0:T(8,128)(2,1)} %collective-permute-done.1) | non-fusion elementwise | flops 49152 | bytes 294912 | tf_op jit(solution)/shard_map/convert_element_type | solution.py:77
  31.3 0.9 %convert_element_type.55 = f32[48,1024]{1,0:T(8,128)S(1)} convert(bf16[48,1024]{1,0:T(8,128)(2,1)} %collective-permute-done.2) | non-fusion elementwise | flops 49152 | bytes 294912 | tf_op jit(solution)/shard_map/convert_element_type | solution.py:77
  32.2 1.2 %collective-permute-done.3 = bf16[48,1024]{1,0:T(8,128)(2,1)} collective-permute-done((bf16[48,1024]{1,0:T(8,128)(2,1)S(1)}, bf16[48,1024]{1,0:T(8,128)(2,1)}, u32[]{:S(2)}, u32[]{:S(2)}) %collective-permute-start.3) | collective-permute-done | bytes 98336 | tf_op jit(solution)/shard_map/ppermute | solution.py:11
  33.4 0.9 %convert_element_type.58 = f32[48,1024]{1,0:T(8,128)S(1)} convert(bf16[48,1024]{1,0:T(8,128)(2,1)} %collective-permute-done.3) | non-fusion elementwise | flops 49152 | bytes 294912 | tf_op jit(solution)/shard_map/convert_element_type | solution.py:77
  34.3 2.6 %collective-permute-start.4 = (f32[32,1024]{1,0:T(8,128)S(1)}, f32[32,1024]{1,0:T(8,128)S(1)}, u32[]{:S(2)}, u32[]{:S(2)}) collective-permute-start(f32[32,1024]{1,0:T(8,128)S(1)} %fusion.11), channel_id=1, source_target_pairs={{0,1},{1,0},{2,3},{3,2},{4,5},{5,4},{6,7},{7,6},{8,9},{9,8},{10,11... | collective-permute-start | bytes 393224 | tf_op jit(solution)/shard_map/ppermute | solution.py:11
  37.0 1.0 %collective-permute-done.4 = f32[32,1024]{1,0:T(8,128)S(1)} collective-permute-done((f32[32,1024]{1,0:T(8,128)S(1)}, f32[32,1024]{1,0:T(8,128)S(1)}, u32[]{:S(2)}, u32[]{:S(2)}) %collective-permute-start.4) | collective-permute-done | bytes 131104 | tf_op jit(solution)/shard_map/ppermute | solution.py:11
  38.7 1.2 %fusion.25 = f32[32,256]{1,0:T(8,128)S(1)} fusion(bf16[256,512]{1,0:T(8,128)(2,1)} %bitcast.19, bf16[16,512]{1,0:T(8,128)(2,1)S(1)} %get-tuple-element.40, bf16[16,512]{1,0:T(8,128)(2,1)S(1)} %get-tuple-element.39), kind=kOutput, calls=%fused_computation.100 | convolution fusion | flops 8454144 | bytes 327680 | tf_op jit(solution)/shard_map/dot_general | solution.py:94
  40.2 1.1 %fusion.26 = f32[32,256]{1,0:T(8,128)S(1)} fusion(bf16[256,512]{1,0:T(8,128)(2,1)} %bitcast.18, bf16[16,512]{1,0:T(8,128)(2,1)S(1)} %get-tuple-element.40, bf16[16,512]{1,0:T(8,128)(2,1)S(1)} %get-tuple-element.39), kind=kOutput, calls=%fused_computation.101 | convolution fusion | flops 8454144 | bytes 327680 | tf_op jit(solution)/shard_map/dot_general | solution.py:94
  41.4 2.7 %collective-permute-start.10 = (bf16[4,64,512]{2,1,0:T(8,128)(2,1)}, bf16[4,64,512]{2,1,0:T(8,128)(2,1)S(1)}, u32[]{:S(2)}, u32[]{:S(2)}) collective-permute-start(bf16[4,64,512]{2,1,0:T(8,128)(2,1)} %collective-permute-done.9), channel_id=1, source_target_pairs={{0,56},{8,0},{16,8},{24,16},{32,24},{40,32},{48,40},{56,48},{64,12... | collective-permute-start | bytes 786440 | tf_op jit(solution)/shard_map/ppermute | solution.py:19
  44.1 1.2 %fusion.30 = f32[32,256]{1,0:T(8,128)S(1)} fusion(bf16[256,512]{1,0:T(8,128)(2,1)} %bitcast.14, bf16[16,512]{1,0:T(8,128)(2,1)S(1)} %get-tuple-element.40, bf16[16,512]{1,0:T(8,128)(2,1)S(1)} %get-tuple-element.39), kind=kOutput, calls=%fused_computation.105 | convolution fusion | flops 8454144 | bytes 327680 | tf_op jit(solution)/shard_map/dot_general | solution.py:94
  45.3 3.9 %collective-permute-done.13 = bf16[4,64,512]{2,1,0:T(8,128)(2,1)S(1)} collective-permute-done((bf16[4,64,512]{2,1,0:T(8,128)(2,1)}, bf16[4,64,512]{2,1,0:T(8,128)(2,1)S(1)}, u32[]{:S(2)}, u32[]{:S(2)}) %collective-permute-start.13) | collective-permute-done | bytes 262176 | tf_op jit(solution)/shard_map/ppermute | solution.py:19
  49.6 7.4 %collective-permute-done.14 = bf16[4,64,512]{2,1,0:T(8,128)(2,1)S(1)} collective-permute-done((bf16[4,64,512]{2,1,0:T(8,128)(2,1)S(1)}, bf16[4,64,512]{2,1,0:T(8,128)(2,1)S(1)}, u32[]{:S(2)}, u32[]{:S(2)}) %collective-permute-start.14) | collective-permute-done | bytes 262176 | tf_op jit(solution)/shard_map/ppermute | solution.py:19
  59.4 2.2 %collective-permute-start.15 = (f32[16,1024]{1,0:T(8,128)S(1)}, f32[16,1024]{1,0:T(8,128)S(1)}, u32[]{:S(2)}, u32[]{:S(2)}) collective-permute-start(f32[16,1024]{1,0:T(8,128)S(1)} %slice_select_fusion), channel_id=1, source_target_pairs={{0,1},{1,0},{2,3},{3,2},{4,5},{5,4},{6,7},{7,6},{8,9},{9,8},{10,11... | collective-permute-start | bytes 196616 | tf_op jit(solution)/shard_map/ppermute | solution.py:11
  61.6 0.9 %collective-permute-done.15 = f32[16,1024]{1,0:T(8,128)S(1)} collective-permute-done((f32[16,1024]{1,0:T(8,128)S(1)}, f32[16,1024]{1,0:T(8,128)S(1)}, u32[]{:S(2)}, u32[]{:S(2)}) %collective-permute-start.15) | collective-permute-done | bytes 65568 | tf_op jit(solution)/shard_map/ppermute | solution.py:11
  62.6 2.3 %collective-permute-start.18 = (f32[16,1024]{1,0:T(8,128)S(1)}, f32[16,1024]{1,0:T(8,128)S(1)}, u32[]{:S(2)}, u32[]{:S(2)}) collective-permute-start(f32[16,1024]{1,0:T(8,128)S(1)} %select_add_fusion.1), channel_id=1, source_target_pairs={{0,6},{1,7},{2,4},{3,5},{4,2},{5,3},{6,0},{7,1},{8,14},{9,15},{10,... | collective-permute-start | bytes 196616 | tf_op jit(solution)/shard_map/ppermute | solution.py:11
  64.9 1.0 %collective-permute-start.16 = (f32[16,1024]{1,0:T(8,128)S(1)}, f32[16,1024]{1,0:T(8,128)S(1)}, u32[]{:S(2)}, u32[]{:S(2)}) collective-permute-start(f32[16,1024]{1,0:T(8,128)S(1)} %select_add_fusion.1), channel_id=1, source_target_pairs={{0,2},{1,3},{2,0},{3,1},{4,6},{5,7},{6,4},{7,5},{8,10},{9,11},{10,... | collective-permute-start | bytes 196616 | tf_op jit(solution)/shard_map/ppermute | solution.py:11
  65.9 1.1 %collective-permute-done.18 = f32[16,1024]{1,0:T(8,128)S(1)} collective-permute-done((f32[16,1024]{1,0:T(8,128)S(1)}, f32[16,1024]{1,0:T(8,128)S(1)}, u32[]{:S(2)}, u32[]{:S(2)}) %collective-permute-start.18) | collective-permute-done | bytes 65568 | tf_op jit(solution)/shard_map/ppermute | solution.py:11
  67.0 2.6 %collective-permute-done.17 = f32[16,1024]{1,0:T(8,128)S(1)} collective-permute-done((f32[16,1024]{1,0:T(8,128)S(1)}, f32[16,1024]{1,0:T(8,128)S(1)}, u32[]{:S(2)}, u32[]{:S(2)}) %collective-permute-start.17) | collective-permute-done | bytes 65568 | tf_op jit(solution)/shard_map/ppermute | solution.py:11
  69.5 2.2 %collective-permute-start.19 = (f32[16,1024]{1,0:T(8,128)S(1)}, f32[16,1024]{1,0:T(8,128)S(1)}, u32[]{:S(2)}, u32[]{:S(2)}) collective-permute-start(f32[16,1024]{1,0:T(8,128)S(1)} %add_add_fusion), channel_id=1, source_target_pairs={{0,1},{1,0},{2,3},{3,2},{4,5},{5,4},{6,7},{7,6},{8,9},{9,8},{10,11... | collective-permute-start | bytes 196616 | tf_op jit(solution)/shard_map/ppermute | solution.py:11
  73.4 14.8 %all_to_all.9 = f32[32,1,64]{2,1,0:T(1,128)S(1)} all-to-all(f32[32,1,64]{2,1,0:T(1,128)S(1)} %all_to_all.6), channel_id=1, replica_groups=mesh['ex'=32,'tp'=8] {'ex'}, dimensions={0} | all-to-all | bytes 16384 | tf_op jit(solution)/shard_map/all_to_all | solution.py:119
  (81 shorter events, 7.9 us)
Async XLA Ops:
  0.6 5.8 %copy-start = (bf16[1024,1024]{1,0:T(8,128)(2,1)S(1)}, bf16[1024,1024]{1,0:T(8,128)(2,1)}, u32[]{:S(2)}) copy-start(bf16[1024,1024]{1,0:T(8,128)(2,1)} %param.9) | copy-start | bytes 6291460
  0.6 5.8 %copy-start.1 = (bf16[1024,64]{0,1:T(8,128)(2,1)S(1)}, bf16[1024,64]{0,1:T(8,128)(2,1)}, u32[]{:S(2)}) copy-start(bf16[1024,64]{0,1:T(8,128)(2,1)} %param.11) | copy-start | bytes 393220
  0.7 9.9 %copy-start.2 = (bf16[64,512]{1,0:T(8,128)(2,1)S(1)}, bf16[64,512]{1,0:T(8,128)(2,1)}, u32[]{:S(2)}) copy-start(bf16[64,512]{1,0:T(8,128)(2,1)} %param.12) | copy-start | bytes 196612
  0.7 26.9 %copy-start.4 = (s32[1,1024]{1,0:T(1,128)S(1)}, s32[1,1024]{1,0:T(1,128)}, u32[]{:S(2)}) copy-start(s32[1,1024]{1,0:T(1,128)} %param.15) | copy-start | bytes 12292
  7.3 64.5 %copy-start.3 = (s32[2048]{0:T(1024)S(1)}, s32[2048]{0:T(1024)}, u32[]{:S(2)}) copy-start(s32[2048]{0:T(1024)} %param.14) | copy-start | bytes 24580
  7.3 65.4 %copy-start.5 = (s32[16]{0:T(128)S(1)}, s32[16]{0:T(128)}, u32[]{:S(2)}) copy-start(s32[16]{0:T(128)} %param.13) | copy-start | bytes 196
  7.3 15.2 %collective-permute-start = (f32[64,1024]{1,0:T(8,128)S(1)}, f32[64,1024]{1,0:T(8,128)}, u32[]{:S(2)}, u32[]{:S(2)}) collective-permute-start(f32[64,1024]{1,0:T(8,128)S(1)} %fusion.10), channel_id=1, source_target_pairs={{0,1},{1,0},{2,3},{3,2},{4,5},{5,4},{6,7},{7,6},{8,9},{9,8},{10,11... | collective-permute-start | bytes 786440 | tf_op jit(solution)/shard_map/ppermute | solution.py:11
  10.6 3.7 %collective-permute-start.5 = (bf16[64,512]{1,0:T(8,128)(2,1)S(1)}, bf16[64,512]{1,0:T(8,128)(2,1)S(1)}, u32[]{:S(2)}, u32[]{:S(2)}) collective-permute-start(bf16[64,512]{1,0:T(8,128)(2,1)S(1)} %copy-done.2), channel_id=1, source_target_pairs={{0,64},{8,72},{16,80},{24,88},{32,96},{40,104},{48,112},{56,120},{... | collective-permute-start | bytes 196616 | tf_op jit(solution)/shard_map/ppermute | solution.py:15
  10.6 4.7 %collective-permute-start.7 = (bf16[64,512]{1,0:T(8,128)(2,1)S(1)}, bf16[64,512]{1,0:T(8,128)(2,1)S(1)}, u32[]{:S(2)}, u32[]{:S(2)}) collective-permute-start(bf16[64,512]{1,0:T(8,128)(2,1)S(1)} %copy-done.2), channel_id=1, source_target_pairs={{0,192},{8,200},{16,208},{24,216},{32,224},{40,232},{48,240},{56,2... | collective-permute-start | bytes 196616 | tf_op jit(solution)/shard_map/ppermute | solution.py:15
  12.1 4.6 %collective-permute-start.6 = (bf16[64,512]{1,0:T(8,128)(2,1)S(1)}, bf16[64,512]{1,0:T(8,128)(2,1)S(1)}, u32[]{:S(2)}, u32[]{:S(2)}) collective-permute-start(bf16[64,512]{1,0:T(8,128)(2,1)S(1)} %copy-done.2), channel_id=1, source_target_pairs={{0,128},{8,136},{16,144},{24,152},{32,160},{40,168},{48,176},{56,1... | collective-permute-start | bytes 196616 | tf_op jit(solution)/shard_map/ppermute | solution.py:15
  16.8 10.8 %collective-permute-start.11 = (bf16[4,64,512]{2,1,0:T(8,128)(2,1)S(1)}, bf16[4,64,512]{2,1,0:T(8,128)(2,1)}, u32[]{:S(2)}, u32[]{:S(2)}) collective-permute-start(bf16[4,64,512]{2,1,0:T(8,128)(2,1)S(1)} %pad_maximum_fusion.2), channel_id=1, source_target_pairs={{0,8},{8,16},{16,24},{24,32},{32,40},{40,48},{48,56},{56,0},{64,72... | collective-permute-start | bytes 786440 | tf_op jit(solution)/shard_map/ppermute | solution.py:19
  18.5 9.2 %collective-permute-start.8 = (bf16[4,64,512]{2,1,0:T(8,128)(2,1)S(1)}, bf16[4,64,512]{2,1,0:T(8,128)(2,1)S(1)}, u32[]{:S(2)}, u32[]{:S(2)}) collective-permute-start(bf16[4,64,512]{2,1,0:T(8,128)(2,1)S(1)} %pad_maximum_fusion.2), channel_id=1, source_target_pairs={{0,56},{8,0},{16,8},{24,16},{32,24},{40,32},{48,40},{56,48},{64,12... | collective-permute-start | bytes 786440 | tf_op jit(solution)/shard_map/ppermute | solution.py:19
  23.6 6.8 %collective-permute-start.1 = (bf16[48,1024]{1,0:T(8,128)(2,1)S(1)}, bf16[48,1024]{1,0:T(8,128)(2,1)}, u32[]{:S(2)}, u32[]{:S(2)}) collective-permute-start(bf16[48,1024]{1,0:T(8,128)(2,1)S(1)} %get-tuple-element.36), channel_id=1, source_target_pairs={{0,2},{1,3},{2,0},{3,1},{4,6},{5,7},{6,4},{7,5},{8,10},{9,11},{10,... | collective-permute-start | bytes 294920 | tf_op jit(solution)/shard_map/ppermute | solution.py:11
  24.9 6.4 %collective-permute-start.2 = (bf16[48,1024]{1,0:T(8,128)(2,1)S(1)}, bf16[48,1024]{1,0:T(8,128)(2,1)}, u32[]{:S(2)}, u32[]{:S(2)}) collective-permute-start(bf16[48,1024]{1,0:T(8,128)(2,1)S(1)} %get-tuple-element.37), channel_id=1, source_target_pairs={{0,4},{1,5},{2,6},{3,7},{4,0},{5,1},{6,2},{7,3},{8,12},{9,13},{10,... | collective-permute-start | bytes 294920 | tf_op jit(solution)/shard_map/ppermute | solution.py:11
  27.3 6.0 %collective-permute-start.3 = (bf16[48,1024]{1,0:T(8,128)(2,1)S(1)}, bf16[48,1024]{1,0:T(8,128)(2,1)}, u32[]{:S(2)}, u32[]{:S(2)}) collective-permute-start(bf16[48,1024]{1,0:T(8,128)(2,1)S(1)} %get-tuple-element.38), channel_id=1, source_target_pairs={{0,6},{1,7},{2,4},{3,5},{4,2},{5,3},{6,0},{7,1},{8,14},{9,15},{10,... | collective-permute-start | bytes 294920 | tf_op jit(solution)/shard_map/ppermute | solution.py:11
  27.6 12.5 %collective-permute-start.12 = (bf16[4,64,512]{2,1,0:T(8,128)(2,1)}, bf16[4,64,512]{2,1,0:T(8,128)(2,1)}, u32[]{:S(2)}, u32[]{:S(2)}) collective-permute-start(bf16[4,64,512]{2,1,0:T(8,128)(2,1)} %collective-permute-done.11), channel_id=1, source_target_pairs={{0,8},{8,16},{16,24},{24,32},{32,40},{40,48},{48,56},{56,0},{64,72... | collective-permute-start | bytes 786440 | tf_op jit(solution)/shard_map/ppermute | solution.py:19
  27.7 13.7 %collective-permute-start.9 = (bf16[4,64,512]{2,1,0:T(8,128)(2,1)S(1)}, bf16[4,64,512]{2,1,0:T(8,128)(2,1)}, u32[]{:S(2)}, u32[]{:S(2)}) collective-permute-start(bf16[4,64,512]{2,1,0:T(8,128)(2,1)S(1)} %collective-permute-done.8), channel_id=1, source_target_pairs={{0,56},{8,0},{16,8},{24,16},{32,24},{40,32},{48,40},{56,48},{64,12... | collective-permute-start | bytes 786440 | tf_op jit(solution)/shard_map/ppermute | solution.py:19
  34.3 3.6 %collective-permute-start.4 = (f32[32,1024]{1,0:T(8,128)S(1)}, f32[32,1024]{1,0:T(8,128)S(1)}, u32[]{:S(2)}, u32[]{:S(2)}) collective-permute-start(f32[32,1024]{1,0:T(8,128)S(1)} %fusion.11), channel_id=1, source_target_pairs={{0,1},{1,0},{2,3},{3,2},{4,5},{5,4},{6,7},{7,6},{8,9},{9,8},{10,11... | collective-permute-start | bytes 393224 | tf_op jit(solution)/shard_map/ppermute | solution.py:11
  40.1 9.0 %collective-permute-start.13 = (bf16[4,64,512]{2,1,0:T(8,128)(2,1)}, bf16[4,64,512]{2,1,0:T(8,128)(2,1)S(1)}, u32[]{:S(2)}, u32[]{:S(2)}) collective-permute-start(bf16[4,64,512]{2,1,0:T(8,128)(2,1)} %collective-permute-done.12), channel_id=1, source_target_pairs={{0,8},{8,16},{16,24},{24,32},{32,40},{40,48},{48,56},{56,0},{64,72... | collective-permute-start | bytes 786440 | tf_op jit(solution)/shard_map/ppermute | solution.py:19
  41.4 8.1 %collective-permute-start.10 = (bf16[4,64,512]{2,1,0:T(8,128)(2,1)}, bf16[4,64,512]{2,1,0:T(8,128)(2,1)S(1)}, u32[]{:S(2)}, u32[]{:S(2)}) collective-permute-start(bf16[4,64,512]{2,1,0:T(8,128)(2,1)} %collective-permute-done.9), channel_id=1, source_target_pairs={{0,56},{8,0},{16,8},{24,16},{32,24},{40,32},{48,40},{56,48},{64,12... | collective-permute-start | bytes 786440 | tf_op jit(solution)/shard_map/ppermute | solution.py:19
  49.1 7.8 %collective-permute-start.14 = (bf16[4,64,512]{2,1,0:T(8,128)(2,1)S(1)}, bf16[4,64,512]{2,1,0:T(8,128)(2,1)S(1)}, u32[]{:S(2)}, u32[]{:S(2)}) collective-permute-start(bf16[4,64,512]{2,1,0:T(8,128)(2,1)S(1)} %collective-permute-done.13), channel_id=1, source_target_pairs={{0,8},{8,16},{16,24},{24,32},{32,40},{40,48},{48,56},{56,0},{64,72... | collective-permute-start | bytes 786440 | tf_op jit(solution)/shard_map/ppermute | solution.py:19
  59.4 3.1 %collective-permute-start.15 = (f32[16,1024]{1,0:T(8,128)S(1)}, f32[16,1024]{1,0:T(8,128)S(1)}, u32[]{:S(2)}, u32[]{:S(2)}) collective-permute-start(f32[16,1024]{1,0:T(8,128)S(1)} %slice_select_fusion), channel_id=1, source_target_pairs={{0,1},{1,0},{2,3},{3,2},{4,5},{5,4},{6,7},{7,6},{8,9},{9,8},{10,11... | collective-permute-start | bytes 196616 | tf_op jit(solution)/shard_map/ppermute | solution.py:11
  62.6 4.4 %collective-permute-start.18 = (f32[16,1024]{1,0:T(8,128)S(1)}, f32[16,1024]{1,0:T(8,128)S(1)}, u32[]{:S(2)}, u32[]{:S(2)}) collective-permute-start(f32[16,1024]{1,0:T(8,128)S(1)} %select_add_fusion.1), channel_id=1, source_target_pairs={{0,6},{1,7},{2,4},{3,5},{4,2},{5,3},{6,0},{7,1},{8,14},{9,15},{10,... | collective-permute-start | bytes 196616 | tf_op jit(solution)/shard_map/ppermute | solution.py:11
  64.9 4.6 %collective-permute-start.17 = (f32[16,1024]{1,0:T(8,128)S(1)}, f32[16,1024]{1,0:T(8,128)S(1)}, u32[]{:S(2)}, u32[]{:S(2)}) collective-permute-start(f32[16,1024]{1,0:T(8,128)S(1)} %select_add_fusion.1), channel_id=1, source_target_pairs={{0,4},{1,5},{2,6},{3,7},{4,0},{5,1},{6,2},{7,3},{8,12},{9,13},{10,... | collective-permute-start | bytes 196616 | tf_op jit(solution)/shard_map/ppermute | solution.py:11
  64.9 4.6 %collective-permute-start.16 = (f32[16,1024]{1,0:T(8,128)S(1)}, f32[16,1024]{1,0:T(8,128)S(1)}, u32[]{:S(2)}, u32[]{:S(2)}) collective-permute-start(f32[16,1024]{1,0:T(8,128)S(1)} %select_add_fusion.1), channel_id=1, source_target_pairs={{0,2},{1,3},{2,0},{3,1},{4,6},{5,7},{6,4},{7,5},{8,10},{9,11},{10,... | collective-permute-start | bytes 196616 | tf_op jit(solution)/shard_map/ppermute | solution.py:11
  69.5 3.1 %collective-permute-start.19 = (f32[16,1024]{1,0:T(8,128)S(1)}, f32[16,1024]{1,0:T(8,128)S(1)}, u32[]{:S(2)}, u32[]{:S(2)}) collective-permute-start(f32[16,1024]{1,0:T(8,128)S(1)} %add_add_fusion), channel_id=1, source_target_pairs={{0,1},{1,0},{2,3},{3,2},{4,5},{5,4},{6,7},{7,6},{8,9},{9,8},{10,11... | collective-permute-start | bytes 196616 | tf_op jit(solution)/shard_map/ppermute | solution.py:11

commit v2 on v0

v2 whole, which is shorter than its diff:
```python
import jax
import jax.numpy as jnp
from jax import lax
from jax.experimental import pallas as pl
from jax.experimental.pallas import tpu as pltpu
from jax.sharding import Mesh
from jax.sharding import PartitionSpec as P

NY, NZ, NX, NC = 4, 8, 4, 2
SIZES = dict(y=NY, z=NZ, x=NX, core=NC)
RANK, TOK, E_DEV, C_DEV, K_DEV, CHOICES = 64, 1024, 16, 64, 512, 2048
ROWS = RANK // (NX * NC)
HALF = RANK // 2
E_ALL, C_ALL = NY * E_DEV, NZ * C_DEV
C_HALF = C_ALL // 2
F32, BF16, I32 = jnp.float32, jnp.bfloat16, jnp.int32
NT = (((1,), (1,)), ((), ()))
VMEM_LIMIT = 48 * 1024 * 1024


def swap(value, axis, bits):
    return lax.ppermute(value, axis, [(i, i ^ bits) for i in range(SIZES[axis])])


def shaped(*dims, dtype=F32):
    return jax.ShapeDtypeStruct(dims, dtype)


def call(body, outs, *args, scratch=()):
    return pl.pallas_call(
        body,
        out_shape=outs,
        scratch_shapes=scratch,
        compiler_params=pltpu.CompilerParams(vmem_limit_bytes=VMEM_LIMIT),
    )(*args)


def project_body(x_ref, y_ref, w_in_ref, w_out_ref, keep_ref, send_ref):
    core = lax.axis_index("core")
    low = lax.dot_general(w_in_ref[...], x_ref[...], NT, preferred_element_type=F32)
    out = lax.dot_general(w_out_ref[...], y_ref[...], NT, preferred_element_type=F32)
    for c in range(NC):
        part = [low[(NC * j + c) * ROWS : (NC * j + c + 1) * ROWS] for j in range(NX)]
        part = jnp.concatenate(part + [out[c * HALF : (c + 1) * HALF]], 0)

        @pl.when(core == c)
        def _():
            keep_ref[...] = part

        @pl.when(core != c)
        def _():
            send_ref[...] = part


def project(x, y, w_in, w_out):
    block = 256
    whole = lambda a: pl.BlockSpec(a.shape, lambda i: (0, 0))
    out = pl.BlockSpec((RANK, block), lambda i: (0, i))
    return pl.pallas_call(
        project_body,
        grid=(TOK // block,),
        in_specs=[
            pl.BlockSpec((block, x.shape[1]), lambda i: (i, 0)),
            pl.BlockSpec((block, y.shape[1]), lambda i: (i, 0)),
            whole(w_in),
            whole(w_out),
        ],
        out_specs=[out, out],
        out_shape=[shaped(RANK, TOK), shaped(RANK, TOK)],
        compiler_params=pltpu.CompilerParams(vmem_limit_bytes=VMEM_LIMIT),
    )(x, y, w_in, w_out)


def halves_of(value):
    high = value.astype(BF16)
    return high, (value - high.astype(F32)).astype(BF16)


def spread_body(keep_ref, got_ref, s1_ref, s2_ref, s3_ref, in_ref, out_ref):
    x = lax.axis_index("x")
    for d, ref in ((1, s1_ref), (2, s2_ref), (3, s3_ref), (0, None)):
        at = pl.ds(pl.multiple_of((x ^ d) * ROWS, ROWS), ROWS)
        part = keep_ref[at, :] + got_ref[at, :]
        if ref is None:
            in_ref[...] = part
        else:
            ref[: 2 * ROWS] = jnp.concatenate(halves_of(part), 0)
    out = keep_ref[NX * ROWS :] + got_ref[NX * ROWS :]
    out_ref[...] = out
    for ref in (s1_ref, s2_ref, s3_ref):
        ref[2 * ROWS :] = out.astype(BF16)


def outer_body(in_ref, g1_ref, g2_ref, g3_ref, mine_ref, other_ref, where_ref, goal_ref, p_ref):
    core = lax.axis_index("core")
    low = in_ref[...]
    for ref in (g1_ref, g2_ref, g3_ref):
        g = ref[: 2 * ROWS].astype(F32)
        low = low + (g[:ROWS] + g[ROWS:])
    mine, other = mine_ref[...], other_ref[...]
    out = jnp.concatenate([jnp.where(core == 0, mine, other), jnp.where(core == 0, other, mine)], 0)
    onehot = lax.broadcasted_iota(I32, (E_DEV, TOK), 0) == where_ref[...]
    weighted = jnp.concatenate([jnp.where(onehot, low[i : i + 1], 0.0) for i in range(ROWS)], 0)
    grads = lax.dot_general(weighted, out, NT, precision=lax.Precision.HIGHEST, preferred_element_type=F32)
    flat = jnp.concatenate([grads[i * E_DEV : (i + 1) * E_DEV] for i in range(ROWS)], 1)
    high, low = halves_of(flat)
    goal = jnp.broadcast_to(goal_ref[...], (E_DEV, 128))
    p_ref[:E_DEV, :K_DEV] = high
    p_ref[E_DEV:, :K_DEV] = low
    p_ref[:E_DEV, K_DEV:] = (goal >> 4).astype(F32).astype(BF16)
    p_ref[E_DEV:, K_DEV:] = (goal & 15).astype(F32).astype(BF16)


def score_body(p0, p1, p2, p3, h_ref, keep_ref, send_ref, goal_ref, held):
    core, z = lax.axis_index("core"), lax.axis_index("z")
    for m, bits in enumerate((0, 4, 2, 6, 1, 5, 3, 7)):
        held[pl.ds(pl.multiple_of((z ^ bits) * C_DEV, C_DEV), C_DEV), :] = h_ref[m]
    ps = [p[...] for p in (p0, p1, p2, p3)]
    left = jnp.concatenate([p[:E_DEV, :K_DEV] for p in ps] + [p[E_DEV:, :K_DEV] for p in ps], 0)
    score = lax.dot_general(left, held[...], NT, preferred_element_type=F32)
    score = score[:E_ALL] + score[E_ALL:]
    first, second = score[:, :C_HALF], score[:, C_HALF:]
    keep_ref[...] = jnp.where(core == 0, first, second)
    send_ref[...] = jnp.where(core == 0, second, first)
    goal = [p[:E_DEV, K_DEV:].astype(F32) * 16.0 + p[E_DEV:, K_DEV:].astype(F32) for p in ps]
    goal_ref[...] = jnp.concatenate(goal, 0)


def total_body(a0, a1, a2, a3, goal_ref, flag_ref, s0, s1, s2, s3, slots_ref):
    core, y = lax.axis_index("core"), lax.axis_index("y")
    score = (a0[...] + a1[...]) + (a2[...] + a3[...])
    score = score * flag_ref[pl.ds(y * NC + core, 1), :]
    for d, ref in enumerate((s0, s1, s2, s3)):
        ref[...] = score[d * E_DEV : (d + 1) * E_DEV]
    first = ((y * NC + core) * C_HALF).astype(F32)
    goal = goal_ref[...] - first
    lane = lax.broadcasted_iota(I32, (E_ALL, 128), 1).astype(F32)
    sums = [
        jnp.sum(jnp.where(goal == lane + 128.0 * j, score[:, 128 * j : 128 * (j + 1)], 0.0), 0, keepdims=True)
        for j in range(C_HALF // 128)
    ]
    slots_ref[...] = jnp.zeros_like(slots_ref)
    for j in range(C_HALF // C_DEV):
        piece = sums[j // 2][:, (j % 2) * C_DEV : (j % 2 + 1) * C_DEV]
        for c in range(NC):
            slots_ref[pl.ds((core * (NZ // NC) + j) * NC + c, 1), 0, :] = piece


def lay_body(mine_ref, other_ref, out_ref):
    core, y = lax.axis_index("core"), lax.axis_index("y")
    for d in range(NY):
        for part, ref in ((core, mine_ref), (1 - core, other_ref)):
            at = pl.multiple_of((y ^ d) * C_ALL + part * C_HALF, C_HALF)
            out_ref[:, pl.ds(at, C_HALF)] = ref[d * E_DEV : (d + 1) * E_DEV, :]


def per_device(
    down_matrix_feeds,
    result_slope_matrix,
    feed_sketch_factor,
    result_slope_factor,
    heldout_slope_entries,
    objective_of_sample,
    kept_choice_flags,
    token_sample_position,
):
    held = heldout_slope_entries[None]
    for bits in (4, 2, 1):
        held = jnp.concatenate([held, swap(held, "z", bits)], 0)

    keep, send = project(
        down_matrix_feeds, result_slope_matrix, feed_sketch_factor.T, result_slope_factor.T
    )
    sent = shaped(6 * ROWS, TOK, dtype=BF16)
    s1, s2, s3, in_own, out_chip = call(
        spread_body,
        [sent, sent, sent, shaped(ROWS, TOK), shaped(HALF, TOK)],
        keep,
        swap(send, "core", 1),
    )
    got = [swap(s, "x", d) for d, s in ((1, s1), (2, s2), (3, s3))]
    out_half = out_chip + sum(g[2 * ROWS :].astype(F32) for g in got)
    packed = call(
        outer_body,
        shaped(2 * E_DEV, K_DEV + 128, dtype=BF16),
        in_own,
        *got,
        out_half,
        swap(out_half, "core", 1),
        token_sample_position,
        objective_of_sample[:, None],
    )
    packs = [packed] + [swap(packed, "y", d) for d in (1, 2, 3)]

    half = shaped(E_ALL, C_HALF)
    keep, send, goal = call(
        score_body,
        [half, half, shaped(E_ALL, 128)],
        *packs,
        held,
        scratch=[pltpu.VMEM((C_ALL, K_DEV), BF16)],
    )
    mine = keep + swap(send, "core", 1)
    flags = kept_choice_flags.astype(F32).reshape(NY * NC, C_HALF)
    piece = shaped(E_DEV, C_HALF)
    *pieces, slots = call(
        total_body,
        [piece] * NY + [shaped(NZ * NC, 1, C_DEV)],
        mine,
        *[swap(mine, "x", d) for d in (1, 2, 3)],
        goal,
        flags,
    )
    mine = jnp.concatenate([pieces[0]] + [swap(pieces[d], "y", d) for d in (1, 2, 3)], 0)
    totals = jnp.sum(lax.all_to_all(slots, ("z", "core"), 0, 0, tiled=True), axis=(0, 1))
    sample_affinity = call(lay_body, shaped(E_DEV, CHOICES), mine, swap(mine, "core", 1))
    return (sample_affinity, totals)


def solution(mesh):
    ex, tp = ("y", "z"), ("x", "core")
    chips = Mesh(mesh.devices.reshape(NY, NZ, NX, NC), ("y", "z", "x", "core"))
    placed = (
        P(ex, tp),
        P(ex, tp),
        P(tp, None),
        P(tp, None),
        P(ex, tp),
        P(ex),
        P(),
        P(ex, None),
    )
    return jax.shard_map(
        per_device, mesh=chips, in_specs=placed, out_specs=(P(ex, None), P(ex)), check_vma=False
    )
```

time: 267 us -> 71.4 us (0.27)
  the two profiles are of different devices: /device:TPU:2 before, /device:TPU:1 now
where the time goes in v2:
time: 71.4 us; the launch traced here: 71.1 us
  starting transfers between devices  32.1 us (45%)
  waiting for transfers between devices  16.2 us (23%)
  blocking collectives  10.1 us (14%)
  Pallas kernels  7.62 us (11%)
  local copies, waits for them, and re-layouts  3.63 us (5%)
  between operations  0.77 us (1%)
    ppermute x19, starting transfers between devices, swap(): lax.ppermute(value, axis, [(i, i ^ bits) for i in range(SIZES[axis])])  32.1 us
    ppermute x19, waiting for transfers between devices, swap(): lax.ppermute(value, axis, [(i, i ^ bits) for i in range(SIZES[axis])])  16.2 us
    all_to_all x1, blocking collectives, per_device(): lax.all_to_all(slots, ('z', 'core'), 0, 0, tiled=True)  10.1 us
    pallas_call x1, Pallas kernels, project(): pl.pallas_call(project_body, grid=(TOK // block,), in_specs=[pl.BlockSpec...  5.78 us
    unnamed x17, local copies, waits for them, and re-layouts  3.54 us
    pallas_call x5, Pallas kernels, call(): pl.pallas_call(body, out_shape=outs, scratch_shapes=scratch, compiler_par...  1.85 us
  transfers between devices with their start and end apart: 19, of which 11 were waited for; matrix products, arithmetic and copies ran while one was open for 1% of the time, Pallas kernels for 9%

profile of v2, /device:TPU:1, one launch (start us, length us, event | category | flops | bytes accessed | tf_op | source)
XLA Modules:
  0.0 71.1 jit_solution(15272322940983007208)
XLA Ops:
  0.7 7.8 %collective-permute-start.8 = (bf16[1,64,512]{2,1,0:T(8,128)(2,1)}, bf16[1,64,512]{2,1,0:T(8,128)(2,1)S(1)}, u32[]{:S(2)}, u32[]{:S(2)}) collective-permute-start(bf16[1,64,512]{2,1,0:T(8,128)(2,1)} %bitcast.6), channel_id=1, source_target_pairs={{0,32},{8,40},{16,48},{24,56},{32,0},{40,8},{48,16},{56,24},{1,33}... | collective-permute-start | bytes 196616 | tf_op jit(solution)/shard_map/ppermute | solution.py:22
  8.5 1.6 %copy-done = bf16[1024,1024]{1,0:T(8,128)(2,1)S(1)} copy-done((bf16[1024,1024]{1,0:T(8,128)(2,1)S(1)}, bf16[1024,1024]{1,0:T(8,128)(2,1)}, u32[]{:S(2)}) %copy-start) | copy-done | bytes 2097176
  10.1 1.0 %copy-done.1 = bf16[3584,64]{0,1:T(8,128)(2,1)S(1)} copy-done((bf16[3584,64]{0,1:T(8,128)(2,1)S(1)}, bf16[3584,64]{0,1:T(8,128)(2,1)}, u32[]{:S(2)}) %copy-start.1) | copy-done | bytes 458776
  11.1 0.9 %copy-done.2 = bf16[1024,64]{0,1:T(8,128)(2,1)S(1)} copy-done((bf16[1024,64]{0,1:T(8,128)(2,1)S(1)}, bf16[1024,64]{0,1:T(8,128)(2,1)}, u32[]{:S(2)}) %copy-start.2) | copy-done | bytes 131096
  12.0 5.8 %shard_map.95 = (f32[64,1024]{1,0:T(8,128)S(1)}, f32[64,1024]{1,0:T(8,128)S(1)}) custom-call(bf16[1024,3584]{1,0:T(8,128)(2,1)} %x_ref.1, bf16[1024,1024]{1,0:T(8,128)(2,1)S(1)} %copy-done, bf16[64,3584]{1,0:T(8,128)(2,1)S(1)} %bitcast.4, bf16[64,1024]{1,0:T(8,128)(2,1)S(1)} %bitcast.5), custom_call_target="tpu_custom_call" | custom-call | tf_op jit(solution)/shard_map/pallas_call | solution.py:59
  17.8 1.0 %collective-permute-start = (f32[64,1024]{1,0:T(8,128)S(1)}, f32[64,1024]{1,0:T(8,128)S(1)}, u32[]{:S(2)}, u32[]{:S(2)}) collective-permute-start(f32[64,1024]{1,0:T(8,128)S(1)} %get-tuple-element.18), channel_id=1, source_target_pairs={{0,1},{1,0},{2,3},{3,2},{4,5},{5,4},{6,7},{7,6},{8,9},{9,8},{10,11... | collective-permute-start | bytes 786440 | tf_op jit(solution)/shard_map/ppermute | solution.py:22
  18.8 1.3 %collective-permute-start.9 = (bf16[2,64,512]{2,1,0:T(8,128)(2,1)S(1)}, bf16[2,64,512]{2,1,0:T(8,128)(2,1)S(1)}, u32[]{:S(2)}, u32[]{:S(2)}) collective-permute-start(bf16[2,64,512]{2,1,0:T(8,128)(2,1)S(1)} %pad_maximum_fusion.2), channel_id=1, source_target_pairs={{0,16},{8,24},{16,0},{24,8},{32,48},{40,56},{48,32},{56,40},{1,17}... | collective-permute-start | bytes 393224 | tf_op jit(solution)/shard_map/ppermute | solution.py:22
  20.2 1.3 %collective-permute-start.1 = (bf16[48,1024]{1,0:T(8,128)(2,1)S(1)}, bf16[48,1024]{1,0:T(8,128)(2,1)S(1)}, u32[]{:S(2)}, u32[]{:S(2)}) collective-permute-start(bf16[48,1024]{1,0:T(8,128)(2,1)S(1)} %get-tuple-element.20), channel_id=1, source_target_pairs={{0,2},{2,0},{4,6},{6,4},{1,3},{3,1},{5,7},{7,5},{8,10},{10,8},{12,... | collective-permute-start | bytes 294920 | tf_op jit(solution)/shard_map/ppermute | solution.py:22
  21.5 2.4 %collective-permute-start.2 = (bf16[48,1024]{1,0:T(8,128)(2,1)S(1)}, bf16[48,1024]{1,0:T(8,128)(2,1)S(1)}, u32[]{:S(2)}, u32[]{:S(2)}) collective-permute-start(bf16[48,1024]{1,0:T(8,128)(2,1)S(1)} %get-tuple-element.21), channel_id=1, source_target_pairs={{0,4},{2,6},{4,0},{6,2},{1,5},{3,7},{5,1},{7,3},{8,12},{10,14},{12... | collective-permute-start | bytes 294920 | tf_op jit(solution)/shard_map/ppermute | solution.py:22
  24.1 3.6 %collective-permute-done.9 = bf16[2,64,512]{2,1,0:T(8,128)(2,1)S(1)} collective-permute-done((bf16[2,64,512]{2,1,0:T(8,128)(2,1)S(1)}, bf16[2,64,512]{2,1,0:T(8,128)(2,1)S(1)}, u32[]{:S(2)}, u32[]{:S(2)}) %collective-permute-start.9) | collective-permute-done | bytes 131104 | tf_op jit(solution)/shard_map/ppermute | solution.py:22
  27.9 0.8 %collective-permute-done.2.g2_ref = bf16[48,1024]{1,0:T(8,128)(2,1)S(1)} collective-permute-done((bf16[48,1024]{1,0:T(8,128)(2,1)S(1)}, bf16[48,1024]{1,0:T(8,128)(2,1)S(1)}, u32[]{:S(2)}, u32[]{:S(2)}) %collective-permute-start.2) | collective-permute-done | bytes 98336 | tf_op jit(solution)/shard_map/ppermute | solution.py:22
  28.6 2.6 %collective-permute-done.3.g3_ref = bf16[48,1024]{1,0:T(8,128)(2,1)S(1)} collective-permute-done((bf16[48,1024]{1,0:T(8,128)(2,1)S(1)}, bf16[48,1024]{1,0:T(8,128)(2,1)S(1)}, u32[]{:S(2)}, u32[]{:S(2)}) %collective-permute-start.3) | collective-permute-done | bytes 98336 | tf_op jit(solution)/shard_map/ppermute | solution.py:22
  31.2 0.7 collective-permute-start.4
  32.0 0.9 %collective-permute-done.4.other_ref = f32[32,1024]{1,0:T(8,128)S(1)} collective-permute-done((f32[32,1024]{1,0:T(8,128)S(1)}, f32[32,1024]{1,0:T(8,128)S(1)}, u32[]{:S(2)}, u32[]{:S(2)}) %collective-permute-start.4) | collective-permute-done | bytes 131104 | tf_op jit(solution)/shard_map/ppermute | solution.py:22
  32.9 0.7 shard_map.97.p0
  33.6 1.4 %collective-permute-start.5 = (bf16[32,640]{1,0:T(8,128)(2,1)S(1)}, bf16[32,640]{1,0:T(8,128)(2,1)S(1)}, u32[]{:S(2)}, u32[]{:S(2)}) collective-permute-start(bf16[32,640]{1,0:T(8,128)(2,1)S(1)} %shard_map.97.p0), channel_id=1, source_target_pairs={{0,64},{64,0},{128,192},{192,128},{1,65},{65,1},{129,193},{193,129... | collective-permute-start | bytes 122888 | tf_op jit(solution)/shard_map/ppermute | solution.py:22
  35.0 2.6 %collective-permute-start.6 = (bf16[32,640]{1,0:T(8,128)(2,1)S(1)}, bf16[32,640]{1,0:T(8,128)(2,1)S(1)}, u32[]{:S(2)}, u32[]{:S(2)}) collective-permute-start(bf16[32,640]{1,0:T(8,128)(2,1)S(1)} %shard_map.97.p0), channel_id=1, source_target_pairs={{0,128},{64,192},{128,0},{192,64},{1,129},{65,193},{129,1},{193,65... | collective-permute-start | bytes 122888 | tf_op jit(solution)/shard_map/ppermute | solution.py:22
  37.7 1.8 %collective-permute-done.6.p2 = bf16[32,640]{1,0:T(8,128)(2,1)S(1)} collective-permute-done((bf16[32,640]{1,0:T(8,128)(2,1)S(1)}, bf16[32,640]{1,0:T(8,128)(2,1)S(1)}, u32[]{:S(2)}, u32[]{:S(2)}) %collective-permute-start.6) | collective-permute-done | bytes 40992 | tf_op jit(solution)/shard_map/ppermute | solution.py:22
  39.5 2.2 %collective-permute-done.7.p3 = bf16[32,640]{1,0:T(8,128)(2,1)S(1)} collective-permute-done((bf16[32,640]{1,0:T(8,128)(2,1)S(1)}, bf16[32,640]{1,0:T(8,128)(2,1)S(1)}, u32[]{:S(2)}, u32[]{:S(2)}) %collective-permute-start.7) | collective-permute-done | bytes 40992 | tf_op jit(solution)/shard_map/ppermute | solution.py:22
  42.0 2.2 %collective-permute-start.11 = (f32[64,256]{1,0:T(8,128)S(1)}, f32[64,256]{1,0:T(8,128)S(1)}, u32[]{:S(2)}, u32[]{:S(2)}) collective-permute-start(f32[64,256]{1,0:T(8,128)S(1)} %get-tuple-element.25), channel_id=1, source_target_pairs={{0,1},{1,0},{2,3},{3,2},{4,5},{5,4},{6,7},{7,6},{8,9},{9,8},{10,11... | collective-permute-start | bytes 196616 | tf_op jit(solution)/shard_map/ppermute | solution.py:22
  44.2 0.9 %collective-permute-done.11 = f32[64,256]{1,0:T(8,128)S(1)} collective-permute-done((f32[64,256]{1,0:T(8,128)S(1)}, f32[64,256]{1,0:T(8,128)S(1)}, u32[]{:S(2)}, u32[]{:S(2)}) %collective-permute-start.11) | collective-permute-done | bytes 65568 | tf_op jit(solution)/shard_map/ppermute | solution.py:22
  45.2 1.5 %collective-permute-start.13 = (f32[64,256]{1,0:T(8,128)S(1)}, f32[64,256]{1,0:T(8,128)S(1)}, u32[]{:S(2)}, u32[]{:S(2)}) collective-permute-start(f32[64,256]{1,0:T(8,128)S(1)} %add.15.a0), channel_id=1, source_target_pairs={{0,4},{2,6},{4,0},{6,2},{1,5},{3,7},{5,1},{7,3},{8,12},{10,14},{12... | collective-permute-start | bytes 196616 | tf_op jit(solution)/shard_map/ppermute | solution.py:22
  46.7 2.4 %collective-permute-start.14 = (f32[64,256]{1,0:T(8,128)S(1)}, f32[64,256]{1,0:T(8,128)S(1)}, u32[]{:S(2)}, u32[]{:S(2)}) collective-permute-start(f32[64,256]{1,0:T(8,128)S(1)} %add.15.a0), channel_id=1, source_target_pairs={{0,6},{2,4},{4,2},{6,0},{1,7},{3,5},{5,3},{7,1},{8,14},{10,12},{12... | collective-permute-start | bytes 196616 | tf_op jit(solution)/shard_map/ppermute | solution.py:22
  49.0 0.8 %collective-permute-done.13.a2 = f32[64,256]{1,0:T(8,128)S(1)} collective-permute-done((f32[64,256]{1,0:T(8,128)S(1)}, f32[64,256]{1,0:T(8,128)S(1)}, u32[]{:S(2)}, u32[]{:S(2)}) %collective-permute-start.13) | collective-permute-done | bytes 65568 | tf_op jit(solution)/shard_map/ppermute | solution.py:22
  49.9 1.5 %collective-permute-done.14.a3 = f32[64,256]{1,0:T(8,128)S(1)} collective-permute-done((f32[64,256]{1,0:T(8,128)S(1)}, f32[64,256]{1,0:T(8,128)S(1)}, u32[]{:S(2)}, u32[]{:S(2)}) %collective-permute-start.14) | collective-permute-done | bytes 65568 | tf_op jit(solution)/shard_map/ppermute | solution.py:22
  51.5 1.1 %collective-permute-start.16 = (f32[16,256]{1,0:T(8,128)S(1)}, f32[16,256]{1,0:T(8,128)S(1)}, u32[]{:S(2)}, u32[]{:S(2)}) collective-permute-start(f32[16,256]{1,0:T(8,128)S(1)} %get-tuple-element.29), channel_id=1, source_target_pairs={{0,128},{64,192},{128,0},{192,64},{1,129},{65,193},{129,1},{193,65... | collective-permute-start | bytes 49160 | tf_op jit(solution)/shard_map/ppermute | solution.py:22
  52.6 2.7 %collective-permute-start.17 = (f32[16,256]{1,0:T(8,128)S(1)}, f32[16,256]{1,0:T(8,128)S(1)}, u32[]{:S(2)}, u32[]{:S(2)}) collective-permute-start(f32[16,256]{1,0:T(8,128)S(1)} %get-tuple-element.30), channel_id=1, source_target_pairs={{0,192},{64,128},{128,64},{192,0},{1,193},{65,129},{129,65},{193,1... | collective-permute-start | bytes 49160 | tf_op jit(solution)/shard_map/ppermute | solution.py:22
  55.7 0.8 %collective-permute-done.17 = f32[16,256]{1,0:T(8,128)S(1)} collective-permute-done((f32[16,256]{1,0:T(8,128)S(1)}, f32[16,256]{1,0:T(8,128)S(1)}, u32[]{:S(2)}, u32[]{:S(2)}) %collective-permute-start.17) | collective-permute-done | bytes 16416 | tf_op jit(solution)/shard_map/ppermute | solution.py:22
  56.5 3.3 %collective-permute-start.18 = (f32[64,256]{1,0:T(8,128)S(1)}, f32[64,256]{1,0:T(8,128)S(1)}, u32[]{:S(2)}, u32[]{:S(2)}) collective-permute-start(f32[64,256]{1,0:T(8,128)S(1)} %constant_dynamic-update-slice_fusion.mine_ref), channel_id=1, source_target_pairs={{0,1},{1,0},{2,3},{3,2},{4,5},{5,4},{6,7},{7,6},{8,9},{9,8},{10,11... | collective-permute-start | bytes 196616 | tf_op jit(solution)/shard_map/ppermute | solution.py:22
  59.8 10.1 %all_to_all.5 = f32[16,1,64]{2,1,0:T(1,128)S(1)} all-to-all(f32[16,1,64]{2,1,0:T(1,128)S(1)} %get-tuple-element.31), channel_id=1, replica_groups=mesh['y'=4,'z'=8,'x'=4,'core'=2] {'z','core'}, dimensions={0} | all-to-all | bytes 8192 | tf_op jit(solution)/shard_map/all_to_all | solution.py:215
  69.9 0.5 reduce_sum.9
  70.5 0.7 shard_map.100
  (40 shorter events, 1.6 us)
Async XLA Ops:
  0.6 31.3 %copy-start.6 = (s32[16]{0:T(128)S(1)}, s32[16]{0:T(128)}, u32[]{:S(2)}) copy-start(s32[16]{0:T(128)} %param.13) | copy-start | bytes 196
  0.6 32.2 %copy-start.3 = (s32[1,1024]{1,0:T(1,128)S(1)}, s32[1,1024]{1,0:T(1,128)}, u32[]{:S(2)}) copy-start(s32[1,1024]{1,0:T(1,128)} %where_ref.1) | copy-start | bytes 12292
  0.7 18.1 %collective-permute-start.8 = (bf16[1,64,512]{2,1,0:T(8,128)(2,1)}, bf16[1,64,512]{2,1,0:T(8,128)(2,1)S(1)}, u32[]{:S(2)}, u32[]{:S(2)}) collective-permute-start(bf16[1,64,512]{2,1,0:T(8,128)(2,1)} %bitcast.6), channel_id=1, source_target_pairs={{0,32},{8,40},{16,48},{24,56},{32,0},{40,8},{48,16},{56,24},{1,33}... | collective-permute-start | bytes 196616 | tf_op jit(solution)/shard_map/ppermute | solution.py:22
  8.5 1.6 %copy-start = (bf16[1024,1024]{1,0:T(8,128)(2,1)S(1)}, bf16[1024,1024]{1,0:T(8,128)(2,1)}, u32[]{:S(2)}) copy-start(bf16[1024,1024]{1,0:T(8,128)(2,1)} %y_ref.1) | copy-start | bytes 6291460
  10.1 1.0 %copy-start.1 = (bf16[3584,64]{0,1:T(8,128)(2,1)S(1)}, bf16[3584,64]{0,1:T(8,128)(2,1)}, u32[]{:S(2)}) copy-start(bf16[3584,64]{0,1:T(8,128)(2,1)} %param.10) | copy-start | bytes 1376260
  11.1 0.9 %copy-start.2 = (bf16[1024,64]{0,1:T(8,128)(2,1)S(1)}, bf16[1024,64]{0,1:T(8,128)(2,1)}, u32[]{:S(2)}) copy-start(bf16[1024,64]{0,1:T(8,128)(2,1)} %param.11) | copy-start | bytes 393220
  12.0 6.8 %copy-start.4 = (bf16[64,512]{1,0:T(8,128)(2,1)S(1)}, bf16[64,512]{1,0:T(8,128)(2,1)}, u32[]{:S(2)}) copy-start(bf16[64,512]{1,0:T(8,128)(2,1)} %param.12) | copy-start | bytes 196612
  12.0 37.0 %copy-start.5 = (s32[2048]{0:T(1024)S(1)}, s32[2048]{0:T(1024)}, u32[]{:S(2)}) copy-start(s32[2048]{0:T(1024)} %param.14) | copy-start | bytes 24580
  17.8 2.3 %collective-permute-start = (f32[64,1024]{1,0:T(8,128)S(1)}, f32[64,1024]{1,0:T(8,128)S(1)}, u32[]{:S(2)}, u32[]{:S(2)}) collective-permute-start(f32[64,1024]{1,0:T(8,128)S(1)} %get-tuple-element.18), channel_id=1, source_target_pairs={{0,1},{1,0},{2,3},{3,2},{4,5},{5,4},{6,7},{7,6},{8,9},{9,8},{10,11... | collective-permute-start | bytes 786440 | tf_op jit(solution)/shard_map/ppermute | solution.py:22
  18.8 8.9 %collective-permute-start.9 = (bf16[2,64,512]{2,1,0:T(8,128)(2,1)S(1)}, bf16[2,64,512]{2,1,0:T(8,128)(2,1)S(1)}, u32[]{:S(2)}, u32[]{:S(2)}) collective-permute-start(bf16[2,64,512]{2,1,0:T(8,128)(2,1)S(1)} %pad_maximum_fusion.2), channel_id=1, source_target_pairs={{0,16},{8,24},{16,0},{24,8},{32,48},{40,56},{48,32},{56,40},{1,17}... | collective-permute-start | bytes 393224 | tf_op jit(solution)/shard_map/ppermute | solution.py:22
  20.2 7.7 %collective-permute-start.1 = (bf16[48,1024]{1,0:T(8,128)(2,1)S(1)}, bf16[48,1024]{1,0:T(8,128)(2,1)S(1)}, u32[]{:S(2)}, u32[]{:S(2)}) collective-permute-start(bf16[48,1024]{1,0:T(8,128)(2,1)S(1)} %get-tuple-element.20), channel_id=1, source_target_pairs={{0,2},{2,0},{4,6},{6,4},{1,3},{3,1},{5,7},{7,5},{8,10},{10,8},{12,... | collective-permute-start | bytes 294920 | tf_op jit(solution)/shard_map/ppermute | solution.py:22
  21.5 7.2 %collective-permute-start.2 = (bf16[48,1024]{1,0:T(8,128)(2,1)S(1)}, bf16[48,1024]{1,0:T(8,128)(2,1)S(1)}, u32[]{:S(2)}, u32[]{:S(2)}) collective-permute-start(bf16[48,1024]{1,0:T(8,128)(2,1)S(1)} %get-tuple-element.21), channel_id=1, source_target_pairs={{0,4},{2,6},{4,0},{6,2},{1,5},{3,7},{5,1},{7,3},{8,12},{10,14},{12... | collective-permute-start | bytes 294920 | tf_op jit(solution)/shard_map/ppermute | solution.py:22
  23.9 7.3 %collective-permute-start.3 = (bf16[48,1024]{1,0:T(8,128)(2,1)S(1)}, bf16[48,1024]{1,0:T(8,128)(2,1)S(1)}, u32[]{:S(2)}, u32[]{:S(2)}) collective-permute-start(bf16[48,1024]{1,0:T(8,128)(2,1)S(1)} %get-tuple-element.22), channel_id=1, source_target_pairs={{0,6},{2,4},{4,2},{6,0},{1,7},{3,5},{5,3},{7,1},{8,14},{10,12},{12... | collective-permute-start | bytes 294920 | tf_op jit(solution)/shard_map/ppermute | solution.py:22
  27.8 9.8 %collective-permute-start.10 = (bf16[4,64,512]{2,1,0:T(8,128)(2,1)S(1)}, bf16[4,64,512]{2,1,0:T(8,128)(2,1)S(1)}, u32[]{:S(2)}, u32[]{:S(2)}) collective-permute-start(bf16[4,64,512]{2,1,0:T(8,128)(2,1)S(1)} %pad_maximum_fusion.1), channel_id=1, source_target_pairs={{0,8},{8,0},{16,24},{24,16},{32,40},{40,32},{48,56},{56,48},{1,9},... | collective-permute-start | bytes 786440 | tf_op jit(solution)/shard_map/ppermute | solution.py:22
  31.2 1.6 %collective-permute-start.4 = (f32[32,1024]{1,0:T(8,128)S(1)}, f32[32,1024]{1,0:T(8,128)S(1)}, u32[]{:S(2)}, u32[]{:S(2)}) collective-permute-start(f32[32,1024]{1,0:T(8,128)S(1)} %add_add_fusion.mine_ref), channel_id=1, source_target_pairs={{0,1},{1,0},{2,3},{3,2},{4,5},{5,4},{6,7},{7,6},{8,9},{9,8},{10,11... | collective-permute-start | bytes 393224 | tf_op jit(solution)/shard_map/ppermute | solution.py:22
  33.6 4.1 %collective-permute-start.5 = (bf16[32,640]{1,0:T(8,128)(2,1)S(1)}, bf16[32,640]{1,0:T(8,128)(2,1)S(1)}, u32[]{:S(2)}, u32[]{:S(2)}) collective-permute-start(bf16[32,640]{1,0:T(8,128)(2,1)S(1)} %shard_map.97.p0), channel_id=1, source_target_pairs={{0,64},{64,0},{128,192},{192,128},{1,65},{65,1},{129,193},{193,129... | collective-permute-start | bytes 122888 | tf_op jit(solution)/shard_map/ppermute | solution.py:22
  35.0 4.5 %collective-permute-start.6 = (bf16[32,640]{1,0:T(8,128)(2,1)S(1)}, bf16[32,640]{1,0:T(8,128)(2,1)S(1)}, u32[]{:S(2)}, u32[]{:S(2)}) collective-permute-start(bf16[32,640]{1,0:T(8,128)(2,1)S(1)} %shard_map.97.p0), channel_id=1, source_target_pairs={{0,128},{64,192},{128,0},{192,64},{1,129},{65,193},{129,1},{193,65... | collective-permute-start | bytes 122888 | tf_op jit(solution)/shard_map/ppermute | solution.py:22
  37.6 4.1 %collective-permute-start.7 = (bf16[32,640]{1,0:T(8,128)(2,1)S(1)}, bf16[32,640]{1,0:T(8,128)(2,1)S(1)}, u32[]{:S(2)}, u32[]{:S(2)}) collective-permute-start(bf16[32,640]{1,0:T(8,128)(2,1)S(1)} %shard_map.97.p0), channel_id=1, source_target_pairs={{0,192},{64,128},{128,64},{192,0},{1,193},{65,129},{129,65},{193,1... | collective-permute-start | bytes 122888 | tf_op jit(solution)/shard_map/ppermute | solution.py:22
  42.0 3.1 %collective-permute-start.11 = (f32[64,256]{1,0:T(8,128)S(1)}, f32[64,256]{1,0:T(8,128)S(1)}, u32[]{:S(2)}, u32[]{:S(2)}) collective-permute-start(f32[64,256]{1,0:T(8,128)S(1)} %get-tuple-element.25), channel_id=1, source_target_pairs={{0,1},{1,0},{2,3},{3,2},{4,5},{5,4},{6,7},{7,6},{8,9},{9,8},{10,11... | collective-permute-start | bytes 196616 | tf_op jit(solution)/shard_map/ppermute | solution.py:22
  45.1 4.0 %collective-permute-start.12 = (f32[64,256]{1,0:T(8,128)S(1)}, f32[64,256]{1,0:T(8,128)S(1)}, u32[]{:S(2)}, u32[]{:S(2)}) collective-permute-start(f32[64,256]{1,0:T(8,128)S(1)} %add.15.a0), channel_id=1, source_target_pairs={{0,2},{2,0},{4,6},{6,4},{1,3},{3,1},{5,7},{7,5},{8,10},{10,8},{12,... | collective-permute-start | bytes 196616 | tf_op jit(solution)/shard_map/ppermute | solution.py:22
  45.2 4.7 %collective-permute-start.13 = (f32[64,256]{1,0:T(8,128)S(1)}, f32[64,256]{1,0:T(8,128)S(1)}, u32[]{:S(2)}, u32[]{:S(2)}) collective-permute-start(f32[64,256]{1,0:T(8,128)S(1)} %add.15.a0), channel_id=1, source_target_pairs={{0,4},{2,6},{4,0},{6,2},{1,5},{3,7},{5,1},{7,3},{8,12},{10,14},{12... | collective-permute-start | bytes 196616 | tf_op jit(solution)/shard_map/ppermute | solution.py:22
  46.7 4.7 %collective-permute-start.14 = (f32[64,256]{1,0:T(8,128)S(1)}, f32[64,256]{1,0:T(8,128)S(1)}, u32[]{:S(2)}, u32[]{:S(2)}) collective-permute-start(f32[64,256]{1,0:T(8,128)S(1)} %add.15.a0), channel_id=1, source_target_pairs={{0,6},{2,4},{4,2},{6,0},{1,7},{3,5},{5,3},{7,1},{8,14},{10,12},{12... | collective-permute-start | bytes 196616 | tf_op jit(solution)/shard_map/ppermute | solution.py:22
  51.5 3.9 %collective-permute-start.15 = (f32[16,256]{1,0:T(8,128)S(1)}, f32[16,256]{1,0:T(8,128)S(1)}, u32[]{:S(2)}, u32[]{:S(2)}) collective-permute-start(f32[16,256]{1,0:T(8,128)S(1)} %get-tuple-element.28), channel_id=1, source_target_pairs={{0,64},{64,0},{128,192},{192,128},{1,65},{65,1},{129,193},{193,129... | collective-permute-start | bytes 49160 | tf_op jit(solution)/shard_map/ppermute | solution.py:22
  51.5 4.2 %collective-permute-start.16 = (f32[16,256]{1,0:T(8,128)S(1)}, f32[16,256]{1,0:T(8,128)S(1)}, u32[]{:S(2)}, u32[]{:S(2)}) collective-permute-start(f32[16,256]{1,0:T(8,128)S(1)} %get-tuple-element.29), channel_id=1, source_target_pairs={{0,128},{64,192},{128,0},{192,64},{1,129},{65,193},{129,1},{193,65... | collective-permute-start | bytes 49160 | tf_op jit(solution)/shard_map/ppermute | solution.py:22
  52.6 3.9 %collective-permute-start.17 = (f32[16,256]{1,0:T(8,128)S(1)}, f32[16,256]{1,0:T(8,128)S(1)}, u32[]{:S(2)}, u32[]{:S(2)}) collective-permute-start(f32[16,256]{1,0:T(8,128)S(1)} %get-tuple-element.30), channel_id=1, source_target_pairs={{0,192},{64,128},{128,64},{192,0},{1,193},{65,129},{129,65},{193,1... | collective-permute-start | bytes 49160 | tf_op jit(solution)/shard_map/ppermute | solution.py:22
  56.5 13.9 %collective-permute-start.18 = (f32[64,256]{1,0:T(8,128)S(1)}, f32[64,256]{1,0:T(8,128)S(1)}, u32[]{:S(2)}, u32[]{:S(2)}) collective-permute-start(f32[64,256]{1,0:T(8,128)S(1)} %constant_dynamic-update-slice_fusion.mine_ref), channel_id=1, source_target_pairs={{0,1},{1,0},{2,3},{3,2},{4,5},{5,4},{6,7},{7,6},{8,9},{9,8},{10,11... | collective-permute-start | bytes 196616 | tf_op jit(solution)/shard_map/ppermute | solution.py:22

commit v3 on v2

v3 whole, which is shorter than its diff:
```python
import jax
import jax.numpy as jnp
from jax import lax
from jax.experimental import pallas as pl
from jax.experimental.pallas import tpu as pltpu
from jax.sharding import Mesh
from jax.sharding import PartitionSpec as P

NY, NZ, NX, NC = 4, 8, 4, 2
SIZES = dict(y=NY, z=NZ, x=NX, core=NC)
RANK, TOK, E_DEV, C_DEV, K_DEV, CHOICES = 64, 1024, 16, 64, 512, 2048
ROWS = RANK // (NX * NC)
HALF = RANK // 2
E_ALL, C_ALL = NY * E_DEV, NZ * C_DEV
C_HALF = C_ALL // 2
F32, BF16, I32, I16 = jnp.float32, jnp.bfloat16, jnp.int32, jnp.int16
NT = (((1,), (1,)), ((), ()))
CHUNK = 512
VMEM_LIMIT = 48 * 1024 * 1024


def swap(value, axis, bits):
    return lax.ppermute(value, axis, [(i, i ^ bits) for i in range(SIZES[axis])])


def shaped(*dims, dtype=F32):
    return jax.ShapeDtypeStruct(dims, dtype)


def call(body, outs, *args, scratch=()):
    return pl.pallas_call(
        body,
        out_shape=outs,
        scratch_shapes=scratch,
        compiler_params=pltpu.CompilerParams(vmem_limit_bytes=VMEM_LIMIT),
    )(*args)


def project_body(x_hbm, y_hbm, w_in_hbm, w_out_hbm, keep_ref, send_ref, parts, w_in, w_out, low, out, sems):
    core = lax.axis_index("core")
    steps = [(y_hbm, w_out, out, k) for k in range(y_hbm.shape[1] // CHUNK)]
    steps += [(x_hbm, w_in, low, k) for k in range(x_hbm.shape[1] // CHUNK)]
    copies = [
        pltpu.make_async_copy(src.at[:, pl.ds(k * CHUNK, CHUNK)], parts.at[n], sems.at[n])
        for n, (src, _, _, k) in enumerate(steps)
    ]
    copy_out = pltpu.make_async_copy(w_out_hbm, w_out, sems.at[len(steps)])
    copy_in = pltpu.make_async_copy(w_in_hbm, w_in, sems.at[len(steps) + 1])
    copy_out.start()
    copies[0].start()
    copy_in.start()
    for copy in copies[1:]:
        copy.start()
    copy_out.wait()
    for n, (src, weights, total, k) in enumerate(steps):
        copies[n].wait()
        if src is x_hbm and k == 0:
            copy_in.wait()
        part = lax.dot_general(
            weights[:, k * CHUNK : (k + 1) * CHUNK], parts[n], NT, preferred_element_type=F32
        )
        if k == 0:
            total[...] = part
        else:
            total[...] += part
    for c in range(NC):
        part = [low[(NC * j + c) * ROWS : (NC * j + c + 1) * ROWS] for j in range(NX)]
        part = jnp.concatenate(part + [out[c * HALF : (c + 1) * HALF]], 0)

        @pl.when(core == c)
        def _():
            keep_ref[...] = part

        @pl.when(core != c)
        def _():
            send_ref[...] = part


def project(x, y, w_in, w_out):
    steps = (x.shape[1] + y.shape[1]) // CHUNK
    args = [pltpu.with_memory_space_constraint(a, pltpu.HBM) for a in (x, y, w_in, w_out)]
    return pl.pallas_call(
        project_body,
        in_specs=[pl.BlockSpec(memory_space=pltpu.HBM)] * 4,
        out_shape=[shaped(RANK, TOK), shaped(RANK, TOK)],
        scratch_shapes=[
            pltpu.VMEM((steps, TOK, CHUNK), BF16),
            pltpu.VMEM(w_in.shape, BF16),
            pltpu.VMEM(w_out.shape, BF16),
            pltpu.VMEM((RANK, TOK), F32),
            pltpu.VMEM((RANK, TOK), F32),
            pltpu.SemaphoreType.DMA((steps + 2,)),
        ],
        compiler_params=pltpu.CompilerParams(vmem_limit_bytes=VMEM_LIMIT),
    )(*args)


def coded(value):
    top = jnp.maximum(jnp.max(jnp.abs(value), 0, keepdims=True), 1e-30)
    power = jnp.clip(jnp.floor(jnp.log2(top)) - 13.0, -100.0, 100.0)
    return jnp.round(value / jnp.exp2(power)), power


def spread_body(keep_ref, got_ref, s1_ref, s2_ref, s3_ref, in_ref, out_ref):
    x = lax.axis_index("x")
    out = keep_ref[NX * ROWS :] + got_ref[NX * ROWS :]
    out_ref[...] = out
    out_code, out_power = coded(out)
    line = lax.broadcasted_iota(I32, (ROWS, TOK), 0)
    for d, ref in ((1, s1_ref), (2, s2_ref), (3, s3_ref), (0, None)):
        at = pl.ds(pl.multiple_of((x ^ d) * ROWS, ROWS), ROWS)
        part = keep_ref[at, :] + got_ref[at, :]
        if ref is None:
            in_ref[...] = part
        else:
            code, power = coded(part)
            powers = jnp.where(line == 0, power, out_power)
            ref[...] = jnp.concatenate([code, out_code, powers], 0).astype(I32).astype(I16)


def add_body(in_ref, out_ref, g1_ref, g2_ref, g3_ref, low_ref, half_ref):
    low, half = in_ref[...], out_ref[...]
    for ref in (g1_ref, g2_ref, g3_ref):
        got = ref[...].astype(I32).astype(F32)
        powers = jnp.exp2(got[ROWS + HALF :])
        low = low + got[:ROWS] * powers[:1]
        half = half + got[ROWS : ROWS + HALF] * powers[1:2]
    low_ref[...] = low
    half_ref[...] = half


def outer_body(in_ref, mine_ref, other_ref, where_ref, goal_ref, p_ref):
    core = lax.axis_index("core")
    low, mine, other = in_ref[...], mine_ref[...], other_ref[...]
    out = jnp.concatenate([jnp.where(core == 0, mine, other), jnp.where(core == 0, other, mine)], 0)
    onehot = lax.broadcasted_iota(I32, (E_DEV, TOK), 0) == where_ref[...]
    weighted = jnp.concatenate([jnp.where(onehot, low[i : i + 1], 0.0) for i in range(ROWS)], 0)
    grads = lax.dot_general(weighted, out, NT, precision=lax.Precision.HIGHEST, preferred_element_type=F32)
    flat = [grads[i * E_DEV : (i + 1) * E_DEV] for i in range(ROWS)]
    goal = jnp.broadcast_to(goal_ref[...], (E_DEV, 128))
    goal = jnp.where(lax.broadcasted_iota(I32, (E_DEV, 128), 1) < 64, goal >> 4, goal & 15)
    p_ref[...] = jnp.concatenate(flat + [goal.astype(F32)], 1).astype(BF16)


def score_body(p0, p1, p2, p3, h_ref, keep_ref, send_ref, goal_ref, held):
    core, z = lax.axis_index("core"), lax.axis_index("z")
    for m, bits in enumerate((0, 4, 2, 6, 1, 5, 3, 7)):
        held[pl.ds(pl.multiple_of((z ^ bits) * C_DEV, C_DEV), C_DEV), :] = h_ref[m]
    ps = [p[...] for p in (p0, p1, p2, p3)]
    left = jnp.concatenate([p[:, :K_DEV] for p in ps], 0)
    score = lax.dot_general(left, held[...], NT, preferred_element_type=F32)
    first, second = score[:, :C_HALF], score[:, C_HALF:]
    keep_ref[...] = jnp.where(core == 0, first, second)
    send_ref[...] = jnp.where(core == 0, second, first)
    goal = jnp.concatenate([p[:, K_DEV:] for p in ps], 0).astype(F32)
    goal_ref[...] = jnp.broadcast_to(goal[:, :1] * 16.0 + goal[:, 64:65], (E_ALL, 128))


def total_body(a0, a1, a2, a3, goal_ref, flag_ref, s0, s1, s2, s3, slots_ref):
    core, y = lax.axis_index("core"), lax.axis_index("y")
    score = (a0[...] + a1[...]) + (a2[...] + a3[...])
    score = score * flag_ref[pl.ds(y * NC + core, 1), :]
    for d, ref in enumerate((s0, s1, s2, s3)):
        ref[...] = score[d * E_DEV : (d + 1) * E_DEV]
    first = ((y * NC + core) * C_HALF).astype(F32)
    goal = goal_ref[...] - first
    lane = lax.broadcasted_iota(I32, (E_ALL, 128), 1).astype(F32)
    sums = [
        jnp.sum(jnp.where(goal == lane + 128.0 * j, score[:, 128 * j : 128 * (j + 1)], 0.0), 0, keepdims=True)
        for j in range(C_HALF // 128)
    ]
    slots_ref[...] = jnp.zeros_like(slots_ref)
    for j in range(C_HALF // C_DEV):
        piece = sums[j // 2][:, (j % 2) * C_DEV : (j % 2 + 1) * C_DEV]
        slots_ref[pl.ds(core * (NZ // NC) + j, 1), 0, :] = piece


def join_body(s0, s1, s2, s3, slots_ref, out_ref):
    for d, ref in enumerate((s0, s1, s2, s3)):
        out_ref[d * E_DEV : (d + 1) * E_DEV] = ref[...]
    total = jnp.sum(slots_ref[...], 0)
    total = jnp.concatenate([total, jnp.zeros((1, C_HALF - C_DEV), F32)], 1)
    out_ref[E_ALL:] = jnp.broadcast_to(total, (8, C_HALF))


def lay_body(mine_ref, other_ref, out_ref, total_ref):
    core, y = lax.axis_index("core"), lax.axis_index("y")
    for d in range(NY):
        for part, ref in ((core, mine_ref), (1 - core, other_ref)):
            at = pl.multiple_of((y ^ d) * C_ALL + part * C_HALF, C_HALF)
            out_ref[:, pl.ds(at, C_HALF)] = ref[d * E_DEV : (d + 1) * E_DEV, :]
    total_ref[...] = mine_ref[E_ALL : E_ALL + 1, :C_DEV] + other_ref[E_ALL : E_ALL + 1, :C_DEV]


def per_device(
    down_matrix_feeds,
    result_slope_matrix,
    feed_sketch_factor,
    result_slope_factor,
    heldout_slope_entries,
    objective_of_sample,
    kept_choice_flags,
    token_sample_position,
):
    held = heldout_slope_entries[None]
    for bits in (4, 2, 1):
        held = jnp.concatenate([held, swap(held, "z", bits)], 0)

    keep, send = project(
        down_matrix_feeds, result_slope_matrix, feed_sketch_factor.T, result_slope_factor.T
    )
    sent = shaped(2 * ROWS + HALF, TOK, dtype=I16)
    low, half = shaped(ROWS, TOK), shaped(HALF, TOK)
    s1, s2, s3, in_own, out_chip = call(
        spread_body, [sent, sent, sent, low, half], keep, swap(send, "core", 1)
    )
    got = [swap(s, "x", d) for d, s in ((1, s1), (2, s2), (3, s3))]
    in_sum, out_half = call(add_body, [low, half], in_own, out_chip, *got)
    packed = call(
        outer_body,
        shaped(E_DEV, K_DEV + 128, dtype=BF16),
        in_sum,
        out_half,
        swap(out_half, "core", 1),
        token_sample_position,
        objective_of_sample[:, None],
    )
    packs = [packed] + [swap(packed, "y", d) for d in (1, 2, 3)]

    half = shaped(E_ALL, C_HALF)
    keep, send, goal = call(
        score_body,
        [half, half, shaped(E_ALL, 128)],
        *packs,
        held,
        scratch=[pltpu.VMEM((C_ALL, K_DEV), BF16)],
    )
    mine = keep + swap(send, "core", 1)
    flags = kept_choice_flags.astype(F32).reshape(NY * NC, C_HALF)
    piece = shaped(E_DEV, C_HALF)
    *pieces, slots = call(
        total_body,
        [piece] * NY + [shaped(NZ, 1, C_DEV)],
        mine,
        *[swap(mine, "x", d) for d in (1, 2, 3)],
        goal,
        flags,
    )
    back = [pieces[0]] + [swap(pieces[d], "y", d) for d in (1, 2, 3)]
    slots = lax.all_to_all(slots, "z", 0, 0, tiled=True)
    mine = call(join_body, shaped(E_ALL + 8, C_HALF), *back, slots)
    sample_affinity, totals = call(
        lay_body, [shaped(E_DEV, CHOICES), shaped(1, C_DEV)], mine, swap(mine, "core", 1)
    )
    return (sample_affinity, totals[0])


def solution(mesh):
    ex, tp = ("y", "z"), ("x", "core")
    chips = Mesh(mesh.devices.reshape(NY, NZ, NX, NC), ("y", "z", "x", "core"))
    placed = (
        P(ex, tp),
        P(ex, tp),
        P(tp, None),
        P(tp, None),
        P(ex, tp),
        P(ex),
        P(),
        P(ex, None),
    )
    return jax.shard_map(
        per_device, mesh=chips, in_specs=placed, out_specs=(P(ex, None), P(ex)), check_vma=False
    )
```

time: 71.4 us -> 75.1 us (1.052)
  starting transfers between devices: 32.1 us -> 35.8 us
  local copies, waits for them, and re-layouts: 3.63 us -> 0.11 us
  blocking collectives: 10.1 us -> 12.3 us
  waiting for transfers between devices: 16.2 us -> 18.3 us
  Pallas kernels: 7.62 us -> 6.73 us
    ppermute x19, starting transfers between devices: 32.1 us -> 35.8 us  [swap(): lax.ppermute(value, axis, [(i, i ^ bits) for i in range(SIZES[axis])])]
    unnamed x17 -> x8, local copies, waits for them, and re-layouts: 3.54 us -> 0.02 us
    all_to_all x1, blocking collectives: 10.1 us -> 12.3 us  [per_device(): slots = lax.all_to_all(slots, 'z', 0, 0, tiled=True)]
    ppermute x19, waiting for transfers between devices: 16.2 us -> 18.3 us  [swap(): lax.ppermute(value, axis, [(i, i ^ bits) for i in range(SIZES[axis])])]
    pallas_call x1, Pallas kernels: 5.78 us -> 4.75 us  [project(): pl.pallas_call(project_body, in_specs=[pl.BlockSpec(memory_space=pltpu.HB...]
    concatenate x3, other arithmetic: 0.1 us -> 0.93 us  [per_device(): held = jnp.concatenate([held, swap(held, 'z', bits)], 0)]
    pallas_call x5 -> x7, Pallas kernels: 1.85 us -> 1.99 us  [call(): pl.pallas_call(body, out_shape=outs, scratch_shapes=scratch, compiler_par...]
  transfers between devices with their start and end apart: 19 -> 19, of which waited for: 11 -> 12; matrix products, arithmetic and copies ran while one was open for 1% -> 0% of each run, Pallas kernels for 9% -> 7%
where the time goes in v3:
time: 75.1 us; the launch traced here: 75 us
  starting transfers between devices  35.8 us (48%)
  waiting for transfers between devices  18.3 us (24%)
  blocking collectives  12.3 us (16%)
  Pallas kernels  6.73 us (9%)
  other arithmetic  0.95 us (1%)
    ppermute x19, starting transfers between devices, swap(): lax.ppermute(value, axis, [(i, i ^ bits) for i in range(SIZES[axis])])  35.8 us
    ppermute x19, waiting for transfers between devices, swap(): lax.ppermute(value, axis, [(i, i ^ bits) for i in range(SIZES[axis])])  18.3 us
    all_to_all x1, blocking collectives, per_device(): slots = lax.all_to_all(slots, 'z', 0, 0, tiled=True)  12.3 us
    pallas_call x1, Pallas kernels, project(): pl.pallas_call(project_body, in_specs=[pl.BlockSpec(memory_space=pltpu.HB...  4.75 us
    pallas_call x7, Pallas kernels, call(): pl.pallas_call(body, out_shape=outs, scratch_shapes=scratch, compiler_par...  1.99 us
  transfers between devices with their start and end apart: 19, of which 12 were waited for; matrix products, arithmetic and copies ran while one was open for 0% of the time, Pallas kernels for 7%

profile of v3, /device:TPU:1, one launch (start us, length us, event | category | flops | bytes accessed | tf_op | source)
XLA Modules:
  0.0 75.0 jit_solution(9930650546047323841)
XLA Ops:
  0.7 7.8 %collective-permute-start.8 = (bf16[1,64,512]{2,1,0:T(8,128)(2,1)}, bf16[1,64,512]{2,1,0:T(8,128)(2,1)S(1)}, u32[]{:S(2)}, u32[]{:S(2)}) collective-permute-start(bf16[1,64,512]{2,1,0:T(8,128)(2,1)} %bitcast.5), channel_id=1, source_target_pairs={{0,32},{8,40},{16,48},{24,56},{32,0},{40,8},{48,16},{56,24},{1,33}... | collective-permute-start | bytes 196616 | tf_op jit(solution)/shard_map/ppermute | solution.py:23
  8.5 2.0 %collective-permute-done.8 = bf16[1,64,512]{2,1,0:T(8,128)(2,1)S(1)} collective-permute-done((bf16[1,64,512]{2,1,0:T(8,128)(2,1)}, bf16[1,64,512]{2,1,0:T(8,128)(2,1)S(1)}, u32[]{:S(2)}, u32[]{:S(2)}) %collective-permute-start.8) | collective-permute-done | bytes 65568 | tf_op jit(solution)/shard_map/ppermute | solution.py:23
  10.5 0.9 %pad_maximum_fusion.2 = bf16[2,64,512]{2,1,0:T(8,128)(2,1)S(1)} fusion(bf16[1,64,512]{2,1,0:T(8,128)(2,1)S(1)} %collective-permute-done.8, bf16[1,64,512]{2,1,0:T(8,128)(2,1)} %bitcast.6), kind=kLoop, calls=%fused_computation.2 | loop fusion | flops 65536 | bytes 262144 | tf_op jit(solution)/shard_map/concatenate | solution.py:207
  11.3 1.4 %collective-permute-start.9 = (bf16[2,64,512]{2,1,0:T(8,128)(2,1)S(1)}, bf16[2,64,512]{2,1,0:T(8,128)(2,1)S(1)}, u32[]{:S(2)}, u32[]{:S(2)}) collective-permute-start(bf16[2,64,512]{2,1,0:T(8,128)(2,1)S(1)} %pad_maximum_fusion.2), channel_id=1, source_target_pairs={{0,16},{8,24},{16,0},{24,8},{32,48},{40,56},{48,32},{56,40},{1,17}... | collective-permute-start | bytes 393224 | tf_op jit(solution)/shard_map/ppermute | solution.py:23
  12.8 4.7 %shard_map.95 = (f32[64,1024]{1,0:T(8,128)S(1)}, f32[64,1024]{1,0:T(8,128)S(1)}) custom-call(bf16[1024,3584]{1,0:T(8,128)(2,1)} %x_hbm.1, bf16[1024,1024]{1,0:T(8,128)(2,1)} %y_hbm.1, bf16[64,3584]{1,0:T(8,128)(2,1)} %bitcast.9, bf16[64,1024]{1,0:T(8,128)(2,1)} %bitcast.10), custom_call_target="tpu_custom_call" | custom-call | tf_op jit(solution)/shard_map/pallas_call | solution.py:82
  17.5 3.3 %collective-permute-start = (f32[64,1024]{1,0:T(8,128)S(1)}, f32[64,1024]{1,0:T(8,128)S(1)}, u32[]{:S(2)}, u32[]{:S(2)}) collective-permute-start(f32[64,1024]{1,0:T(8,128)S(1)} %get-tuple-element.22), channel_id=1, source_target_pairs={{0,1},{1,0},{2,3},{3,2},{4,5},{5,4},{6,7},{7,6},{8,9},{9,8},{10,11... | collective-permute-start | bytes 786440 | tf_op jit(solution)/shard_map/ppermute | solution.py:23
  20.8 0.6 collective-permute-start.10
  21.5 0.5 collective-permute-done.got_ref
  22.1 1.3 %collective-permute-start.1 = (s16[48,1024]{1,0:T(8,128)(2,1)S(1)}, s16[48,1024]{1,0:T(8,128)(2,1)S(1)}, u32[]{:S(2)}, u32[]{:S(2)}) collective-permute-start(s16[48,1024]{1,0:T(8,128)(2,1)S(1)} %get-tuple-element.25), channel_id=1, source_target_pairs={{0,2},{2,0},{4,6},{6,4},{1,3},{3,1},{5,7},{7,5},{8,10},{10,8},{12,... | collective-permute-start | bytes 294920 | tf_op jit(solution)/shard_map/ppermute | solution.py:23
  23.4 2.4 %collective-permute-start.2 = (s16[48,1024]{1,0:T(8,128)(2,1)S(1)}, s16[48,1024]{1,0:T(8,128)(2,1)S(1)}, u32[]{:S(2)}, u32[]{:S(2)}) collective-permute-start(s16[48,1024]{1,0:T(8,128)(2,1)S(1)} %get-tuple-element.26), channel_id=1, source_target_pairs={{0,4},{2,6},{4,0},{6,2},{1,5},{3,7},{5,1},{7,3},{8,12},{10,14},{12... | collective-permute-start | bytes 294920 | tf_op jit(solution)/shard_map/ppermute | solution.py:23
  26.2 4.3 %collective-permute-done.2.g2_ref = s16[48,1024]{1,0:T(8,128)(2,1)S(1)} collective-permute-done((s16[48,1024]{1,0:T(8,128)(2,1)S(1)}, s16[48,1024]{1,0:T(8,128)(2,1)S(1)}, u32[]{:S(2)}, u32[]{:S(2)}) %collective-permute-start.2) | collective-permute-done | bytes 98336 | tf_op jit(solution)/shard_map/ppermute | solution.py:23
  30.5 2.6 %collective-permute-done.3.g3_ref = s16[48,1024]{1,0:T(8,128)(2,1)S(1)} collective-permute-done((s16[48,1024]{1,0:T(8,128)(2,1)S(1)}, s16[48,1024]{1,0:T(8,128)(2,1)S(1)}, u32[]{:S(2)}, u32[]{:S(2)}) %collective-permute-start.3) | collective-permute-done | bytes 98336 | tf_op jit(solution)/shard_map/ppermute | solution.py:23
  33.1 0.7 collective-permute-start.4
  33.9 0.9 %collective-permute-done.4.other_ref = f32[32,1024]{1,0:T(8,128)S(1)} collective-permute-done((f32[32,1024]{1,0:T(8,128)S(1)}, f32[32,1024]{1,0:T(8,128)S(1)}, u32[]{:S(2)}, u32[]{:S(2)}) %collective-permute-start.4) | collective-permute-done | bytes 131104 | tf_op jit(solution)/shard_map/ppermute | solution.py:23
  34.8 0.7 shard_map.98.p0
  35.5 1.3 %collective-permute-start.5 = (bf16[16,640]{1,0:T(8,128)(2,1)S(1)}, bf16[16,640]{1,0:T(8,128)(2,1)S(1)}, u32[]{:S(2)}, u32[]{:S(2)}) collective-permute-start(bf16[16,640]{1,0:T(8,128)(2,1)S(1)} %shard_map.98.p0), channel_id=1, source_target_pairs={{0,64},{64,0},{128,192},{192,128},{1,65},{65,1},{129,193},{193,129... | collective-permute-start | bytes 61448 | tf_op jit(solution)/shard_map/ppermute | solution.py:23
  36.8 2.6 %collective-permute-start.6 = (bf16[16,640]{1,0:T(8,128)(2,1)S(1)}, bf16[16,640]{1,0:T(8,128)(2,1)S(1)}, u32[]{:S(2)}, u32[]{:S(2)}) collective-permute-start(bf16[16,640]{1,0:T(8,128)(2,1)S(1)} %shard_map.98.p0), channel_id=1, source_target_pairs={{0,128},{64,192},{128,0},{192,64},{1,129},{65,193},{129,1},{193,65... | collective-permute-start | bytes 61448 | tf_op jit(solution)/shard_map/ppermute | solution.py:23
  39.5 1.4 %collective-permute-done.6.p2 = bf16[16,640]{1,0:T(8,128)(2,1)S(1)} collective-permute-done((bf16[16,640]{1,0:T(8,128)(2,1)S(1)}, bf16[16,640]{1,0:T(8,128)(2,1)S(1)}, u32[]{:S(2)}, u32[]{:S(2)}) %collective-permute-start.6) | collective-permute-done | bytes 20512 | tf_op jit(solution)/shard_map/ppermute | solution.py:23
  41.0 2.3 %collective-permute-done.7.p3 = bf16[16,640]{1,0:T(8,128)(2,1)S(1)} collective-permute-done((bf16[16,640]{1,0:T(8,128)(2,1)S(1)}, bf16[16,640]{1,0:T(8,128)(2,1)S(1)}, u32[]{:S(2)}, u32[]{:S(2)}) %collective-permute-start.7) | collective-permute-done | bytes 20512 | tf_op jit(solution)/shard_map/ppermute | solution.py:23
  43.3 0.3 shard_map.99
  43.6 2.2 %collective-permute-start.11 = (f32[64,256]{1,0:T(8,128)S(1)}, f32[64,256]{1,0:T(8,128)S(1)}, u32[]{:S(2)}, u32[]{:S(2)}) collective-permute-start(f32[64,256]{1,0:T(8,128)S(1)} %get-tuple-element.31), channel_id=1, source_target_pairs={{0,1},{1,0},{2,3},{3,2},{4,5},{5,4},{6,7},{7,6},{8,9},{9,8},{10,11... | collective-permute-start | bytes 196616 | tf_op jit(solution)/shard_map/ppermute | solution.py:23
  45.8 0.9 %collective-permute-done.11 = f32[64,256]{1,0:T(8,128)S(1)} collective-permute-done((f32[64,256]{1,0:T(8,128)S(1)}, f32[64,256]{1,0:T(8,128)S(1)}, u32[]{:S(2)}, u32[]{:S(2)}) %collective-permute-start.11) | collective-permute-done | bytes 65568 | tf_op jit(solution)/shard_map/ppermute | solution.py:23
  46.8 1.5 %collective-permute-start.13 = (f32[64,256]{1,0:T(8,128)S(1)}, f32[64,256]{1,0:T(8,128)S(1)}, u32[]{:S(2)}, u32[]{:S(2)}) collective-permute-start(f32[64,256]{1,0:T(8,128)S(1)} %add.3.a0), channel_id=1, source_target_pairs={{0,4},{2,6},{4,0},{6,2},{1,5},{3,7},{5,1},{7,3},{8,12},{10,14},{12... | collective-permute-start | bytes 196616 | tf_op jit(solution)/shard_map/ppermute | solution.py:23
  48.3 2.3 %collective-permute-start.14 = (f32[64,256]{1,0:T(8,128)S(1)}, f32[64,256]{1,0:T(8,128)S(1)}, u32[]{:S(2)}, u32[]{:S(2)}) collective-permute-start(f32[64,256]{1,0:T(8,128)S(1)} %add.3.a0), channel_id=1, source_target_pairs={{0,6},{2,4},{4,2},{6,0},{1,7},{3,5},{5,3},{7,1},{8,14},{10,12},{12... | collective-permute-start | bytes 196616 | tf_op jit(solution)/shard_map/ppermute | solution.py:23
  50.6 0.8 %collective-permute-done.13.a2 = f32[64,256]{1,0:T(8,128)S(1)} collective-permute-done((f32[64,256]{1,0:T(8,128)S(1)}, f32[64,256]{1,0:T(8,128)S(1)}, u32[]{:S(2)}, u32[]{:S(2)}) %collective-permute-start.13) | collective-permute-done | bytes 65568 | tf_op jit(solution)/shard_map/ppermute | solution.py:23
  51.5 1.5 %collective-permute-done.14.a3 = f32[64,256]{1,0:T(8,128)S(1)} collective-permute-done((f32[64,256]{1,0:T(8,128)S(1)}, f32[64,256]{1,0:T(8,128)S(1)}, u32[]{:S(2)}, u32[]{:S(2)}) %collective-permute-start.14) | collective-permute-done | bytes 65568 | tf_op jit(solution)/shard_map/ppermute | solution.py:23
  53.1 1.1 %collective-permute-start.16 = (f32[16,256]{1,0:T(8,128)S(1)}, f32[16,256]{1,0:T(8,128)S(1)}, u32[]{:S(2)}, u32[]{:S(2)}) collective-permute-start(f32[16,256]{1,0:T(8,128)S(1)} %get-tuple-element.35), channel_id=1, source_target_pairs={{0,128},{64,192},{128,0},{192,64},{1,129},{65,193},{129,1},{193,65... | collective-permute-start | bytes 49160 | tf_op jit(solution)/shard_map/ppermute | solution.py:23
  54.3 2.7 %collective-permute-start.17 = (f32[16,256]{1,0:T(8,128)S(1)}, f32[16,256]{1,0:T(8,128)S(1)}, u32[]{:S(2)}, u32[]{:S(2)}) collective-permute-start(f32[16,256]{1,0:T(8,128)S(1)} %get-tuple-element.36), channel_id=1, source_target_pairs={{0,192},{64,128},{128,64},{192,0},{1,193},{65,129},{129,65},{193,1... | collective-permute-start | bytes 49160 | tf_op jit(solution)/shard_map/ppermute | solution.py:23
  57.0 12.3 %all_to_all.5.slots_ref = f32[8,1,64]{2,1,0:T(1,128)S(1)} all-to-all(f32[8,1,64]{2,1,0:T(1,128)S(1)} %get-tuple-element.37), channel_id=1, replica_groups=mesh['y'=4,'z'=8,'x'=4,'core'=2] {'z'}, dimensions={0} | all-to-all | bytes 4096 | tf_op jit(solution)/shard_map/all_to_all | solution.py:250
  69.4 4.0 %collective-permute-start.18 = (f32[72,256]{1,0:T(8,128)S(1)}, f32[72,256]{1,0:T(8,128)S(1)}, u32[]{:S(2)}, u32[]{:S(2)}) collective-permute-start(f32[72,256]{1,0:T(8,128)S(1)} %shard_map.101.mine_ref), channel_id=1, source_target_pairs={{0,1},{1,0},{2,3},{3,2},{4,5},{5,4},{6,7},{7,6},{8,9},{9,8},{10,11... | collective-permute-start | bytes 221192 | tf_op jit(solution)/shard_map/ppermute | solution.py:23
  73.4 0.9 %collective-permute-done.18.other_ref = f32[72,256]{1,0:T(8,128)S(1)} collective-permute-done((f32[72,256]{1,0:T(8,128)S(1)}, f32[72,256]{1,0:T(8,128)S(1)}, u32[]{:S(2)}, u32[]{:S(2)}) %collective-permute-start.18) | collective-permute-done | bytes 73760 | tf_op jit(solution)/shard_map/ppermute | solution.py:23
  74.3 0.7 shard_map.102
  (30 shorter events, 1.0 us)
Async XLA Ops:
  0.6 20.1 %copy-start.1 = (bf16[64,512]{1,0:T(8,128)(2,1)S(1)}, bf16[64,512]{1,0:T(8,128)(2,1)}, u32[]{:S(2)}) copy-start(bf16[64,512]{1,0:T(8,128)(2,1)} %param.12) | copy-start | bytes 196612
  0.6 33.2 %copy-start.3 = (s32[16]{0:T(128)S(1)}, s32[16]{0:T(128)}, u32[]{:S(2)}) copy-start(s32[16]{0:T(128)} %param.13) | copy-start | bytes 196
  0.7 34.2 %copy-start = (s32[1,1024]{1,0:T(1,128)S(1)}, s32[1,1024]{1,0:T(1,128)}, u32[]{:S(2)}) copy-start(s32[1,1024]{1,0:T(1,128)} %where_ref.1) | copy-start | bytes 12292
  0.7 50.0 %copy-start.2 = (s32[2048]{0:T(1024)S(1)}, s32[2048]{0:T(1024)}, u32[]{:S(2)}) copy-start(s32[2048]{0:T(1024)} %param.14) | copy-start | bytes 24580
  0.7 9.8 %collective-permute-start.8 = (bf16[1,64,512]{2,1,0:T(8,128)(2,1)}, bf16[1,64,512]{2,1,0:T(8,128)(2,1)S(1)}, u32[]{:S(2)}, u32[]{:S(2)}) collective-permute-start(bf16[1,64,512]{2,1,0:T(8,128)(2,1)} %bitcast.5), channel_id=1, source_target_pairs={{0,32},{8,40},{16,48},{24,56},{32,0},{40,8},{48,16},{56,24},{1,33}... | collective-permute-start | bytes 196616 | tf_op jit(solution)/shard_map/ppermute | solution.py:23
  11.3 9.5 %collective-permute-start.9 = (bf16[2,64,512]{2,1,0:T(8,128)(2,1)S(1)}, bf16[2,64,512]{2,1,0:T(8,128)(2,1)S(1)}, u32[]{:S(2)}, u32[]{:S(2)}) collective-permute-start(bf16[2,64,512]{2,1,0:T(8,128)(2,1)S(1)} %pad_maximum_fusion.2), channel_id=1, source_target_pairs={{0,16},{8,24},{16,0},{24,8},{32,48},{40,56},{48,32},{56,40},{1,17}... | collective-permute-start | bytes 393224 | tf_op jit(solution)/shard_map/ppermute | solution.py:23
  17.5 4.4 %collective-permute-start = (f32[64,1024]{1,0:T(8,128)S(1)}, f32[64,1024]{1,0:T(8,128)S(1)}, u32[]{:S(2)}, u32[]{:S(2)}) collective-permute-start(f32[64,1024]{1,0:T(8,128)S(1)} %get-tuple-element.22), channel_id=1, source_target_pairs={{0,1},{1,0},{2,3},{3,2},{4,5},{5,4},{6,7},{7,6},{8,9},{9,8},{10,11... | collective-permute-start | bytes 786440 | tf_op jit(solution)/shard_map/ppermute | solution.py:23
  20.8 18.6 %collective-permute-start.10 = (bf16[4,64,512]{2,1,0:T(8,128)(2,1)S(1)}, bf16[4,64,512]{2,1,0:T(8,128)(2,1)S(1)}, u32[]{:S(2)}, u32[]{:S(2)}) collective-permute-start(bf16[4,64,512]{2,1,0:T(8,128)(2,1)S(1)} %pad_maximum_fusion.1), channel_id=1, source_target_pairs={{0,8},{8,0},{16,24},{24,16},{32,40},{40,32},{48,56},{56,48},{1,9},... | collective-permute-start | bytes 786440 | tf_op jit(solution)/shard_map/ppermute | solution.py:23
  22.1 4.1 %collective-permute-start.1 = (s16[48,1024]{1,0:T(8,128)(2,1)S(1)}, s16[48,1024]{1,0:T(8,128)(2,1)S(1)}, u32[]{:S(2)}, u32[]{:S(2)}) collective-permute-start(s16[48,1024]{1,0:T(8,128)(2,1)S(1)} %get-tuple-element.25), channel_id=1, source_target_pairs={{0,2},{2,0},{4,6},{6,4},{1,3},{3,1},{5,7},{7,5},{8,10},{10,8},{12,... | collective-permute-start | bytes 294920 | tf_op jit(solution)/shard_map/ppermute | solution.py:23
  23.4 7.1 %collective-permute-start.2 = (s16[48,1024]{1,0:T(8,128)(2,1)S(1)}, s16[48,1024]{1,0:T(8,128)(2,1)S(1)}, u32[]{:S(2)}, u32[]{:S(2)}) collective-permute-start(s16[48,1024]{1,0:T(8,128)(2,1)S(1)} %get-tuple-element.26), channel_id=1, source_target_pairs={{0,4},{2,6},{4,0},{6,2},{1,5},{3,7},{5,1},{7,3},{8,12},{10,14},{12... | collective-permute-start | bytes 294920 | tf_op jit(solution)/shard_map/ppermute | solution.py:23
  25.8 7.2 %collective-permute-start.3 = (s16[48,1024]{1,0:T(8,128)(2,1)S(1)}, s16[48,1024]{1,0:T(8,128)(2,1)S(1)}, u32[]{:S(2)}, u32[]{:S(2)}) collective-permute-start(s16[48,1024]{1,0:T(8,128)(2,1)S(1)} %get-tuple-element.27), channel_id=1, source_target_pairs={{0,6},{2,4},{4,2},{6,0},{1,7},{3,5},{5,3},{7,1},{8,14},{10,12},{12... | collective-permute-start | bytes 294920 | tf_op jit(solution)/shard_map/ppermute | solution.py:23
  33.1 1.7 %collective-permute-start.4 = (f32[32,1024]{1,0:T(8,128)S(1)}, f32[32,1024]{1,0:T(8,128)S(1)}, u32[]{:S(2)}, u32[]{:S(2)}) collective-permute-start(f32[32,1024]{1,0:T(8,128)S(1)} %get-tuple-element.29.mine_ref), channel_id=1, source_target_pairs={{0,1},{1,0},{2,3},{3,2},{4,5},{5,4},{6,7},{7,6},{8,9},{9,8},{10,11... | collective-permute-start | bytes 393224 | tf_op jit(solution)/shard_map/ppermute | solution.py:23
  35.5 4.0 %collective-permute-start.5 = (bf16[16,640]{1,0:T(8,128)(2,1)S(1)}, bf16[16,640]{1,0:T(8,128)(2,1)S(1)}, u32[]{:S(2)}, u32[]{:S(2)}) collective-permute-start(bf16[16,640]{1,0:T(8,128)(2,1)S(1)} %shard_map.98.p0), channel_id=1, source_target_pairs={{0,64},{64,0},{128,192},{192,128},{1,65},{65,1},{129,193},{193,129... | collective-permute-start | bytes 61448 | tf_op jit(solution)/shard_map/ppermute | solution.py:23
  36.8 4.1 %collective-permute-start.6 = (bf16[16,640]{1,0:T(8,128)(2,1)S(1)}, bf16[16,640]{1,0:T(8,128)(2,1)S(1)}, u32[]{:S(2)}, u32[]{:S(2)}) collective-permute-start(bf16[16,640]{1,0:T(8,128)(2,1)S(1)} %shard_map.98.p0), channel_id=1, source_target_pairs={{0,128},{64,192},{128,0},{192,64},{1,129},{65,193},{129,1},{193,65... | collective-permute-start | bytes 61448 | tf_op jit(solution)/shard_map/ppermute | solution.py:23
  39.4 3.8 %collective-permute-start.7 = (bf16[16,640]{1,0:T(8,128)(2,1)S(1)}, bf16[16,640]{1,0:T(8,128)(2,1)S(1)}, u32[]{:S(2)}, u32[]{:S(2)}) collective-permute-start(bf16[16,640]{1,0:T(8,128)(2,1)S(1)} %shard_map.98.p0), channel_id=1, source_target_pairs={{0,192},{64,128},{128,64},{192,0},{1,193},{65,129},{129,65},{193,1... | collective-permute-start | bytes 61448 | tf_op jit(solution)/shard_map/ppermute | solution.py:23
  43.6 3.1 %collective-permute-start.11 = (f32[64,256]{1,0:T(8,128)S(1)}, f32[64,256]{1,0:T(8,128)S(1)}, u32[]{:S(2)}, u32[]{:S(2)}) collective-permute-start(f32[64,256]{1,0:T(8,128)S(1)} %get-tuple-element.31), channel_id=1, source_target_pairs={{0,1},{1,0},{2,3},{3,2},{4,5},{5,4},{6,7},{7,6},{8,9},{9,8},{10,11... | collective-permute-start | bytes 196616 | tf_op jit(solution)/shard_map/ppermute | solution.py:23
  46.7 4.0 %collective-permute-start.12 = (f32[64,256]{1,0:T(8,128)S(1)}, f32[64,256]{1,0:T(8,128)S(1)}, u32[]{:S(2)}, u32[]{:S(2)}) collective-permute-start(f32[64,256]{1,0:T(8,128)S(1)} %add.3.a0), channel_id=1, source_target_pairs={{0,2},{2,0},{4,6},{6,4},{1,3},{3,1},{5,7},{7,5},{8,10},{10,8},{12,... | collective-permute-start | bytes 196616 | tf_op jit(solution)/shard_map/ppermute | solution.py:23
  46.8 4.7 %collective-permute-start.13 = (f32[64,256]{1,0:T(8,128)S(1)}, f32[64,256]{1,0:T(8,128)S(1)}, u32[]{:S(2)}, u32[]{:S(2)}) collective-permute-start(f32[64,256]{1,0:T(8,128)S(1)} %add.3.a0), channel_id=1, source_target_pairs={{0,4},{2,6},{4,0},{6,2},{1,5},{3,7},{5,1},{7,3},{8,12},{10,14},{12... | collective-permute-start | bytes 196616 | tf_op jit(solution)/shard_map/ppermute | solution.py:23
  48.3 4.7 %collective-permute-start.14 = (f32[64,256]{1,0:T(8,128)S(1)}, f32[64,256]{1,0:T(8,128)S(1)}, u32[]{:S(2)}, u32[]{:S(2)}) collective-permute-start(f32[64,256]{1,0:T(8,128)S(1)} %add.3.a0), channel_id=1, source_target_pairs={{0,6},{2,4},{4,2},{6,0},{1,7},{3,5},{5,3},{7,1},{8,14},{10,12},{12... | collective-permute-start | bytes 196616 | tf_op jit(solution)/shard_map/ppermute | solution.py:23
  53.1 16.2 %collective-permute-start.15 = (f32[16,256]{1,0:T(8,128)S(1)}, f32[16,256]{1,0:T(8,128)S(1)}, u32[]{:S(2)}, u32[]{:S(2)}) collective-permute-start(f32[16,256]{1,0:T(8,128)S(1)} %get-tuple-element.34), channel_id=1, source_target_pairs={{0,64},{64,0},{128,192},{192,128},{1,65},{65,1},{129,193},{193,129... | collective-permute-start | bytes 49160 | tf_op jit(solution)/shard_map/ppermute | solution.py:23
  53.1 16.2 %collective-permute-start.16 = (f32[16,256]{1,0:T(8,128)S(1)}, f32[16,256]{1,0:T(8,128)S(1)}, u32[]{:S(2)}, u32[]{:S(2)}) collective-permute-start(f32[16,256]{1,0:T(8,128)S(1)} %get-tuple-element.35), channel_id=1, source_target_pairs={{0,128},{64,192},{128,0},{192,64},{1,129},{65,193},{129,1},{193,65... | collective-permute-start | bytes 49160 | tf_op jit(solution)/shard_map/ppermute | solution.py:23
  54.3 15.1 %collective-permute-start.17 = (f32[16,256]{1,0:T(8,128)S(1)}, f32[16,256]{1,0:T(8,128)S(1)}, u32[]{:S(2)}, u32[]{:S(2)}) collective-permute-start(f32[16,256]{1,0:T(8,128)S(1)} %get-tuple-element.36), channel_id=1, source_target_pairs={{0,192},{64,128},{128,64},{192,0},{1,193},{65,129},{129,65},{193,1... | collective-permute-start | bytes 49160 | tf_op jit(solution)/shard_map/ppermute | solution.py:23
  69.4 5.0 %collective-permute-start.18 = (f32[72,256]{1,0:T(8,128)S(1)}, f32[72,256]{1,0:T(8,128)S(1)}, u32[]{:S(2)}, u32[]{:S(2)}) collective-permute-start(f32[72,256]{1,0:T(8,128)S(1)} %shard_map.101.mine_ref), channel_id=1, source_target_pairs={{0,1},{1,0},{2,3},{3,2},{4,5},{5,4},{6,7},{7,6},{8,9},{9,8},{10,11... | collective-permute-start | bytes 221192 | tf_op jit(solution)/shard_map/ppermute | solution.py:23

commit v4 on v3

v4 whole, which is shorter than its diff:
```python
import jax
import jax.numpy as jnp
from jax import lax
from jax.experimental import pallas as pl
from jax.experimental.pallas import tpu as pltpu
from jax.sharding import Mesh
from jax.sharding import PartitionSpec as P

NY, NZ, NX, NC = 4, 8, 4, 2
SIZES = dict(y=NY, z=NZ, x=NX, core=NC)
RANK, TOK, E_DEV, C_DEV, K_DEV, CHOICES = 64, 1024, 16, 64, 512, 2048
ROWS = RANK // (NX * NC)
HALF = RANK // 2
E_ALL, C_ALL = NY * E_DEV, NZ * C_DEV
C_HALF = C_ALL // NC
F32, BF16, I32, I16 = jnp.float32, jnp.bfloat16, jnp.int32, jnp.int16
NT = (((1,), (1,)), ((), ()))
CHUNK = 512
VMEM_LIMIT = 48 * 1024 * 1024


def swap(value, axis, bits):
    return lax.ppermute(value, axis, [(i, i ^ bits) for i in range(SIZES[axis])])


def shaped(*dims, dtype=F32):
    return jax.ShapeDtypeStruct(dims, dtype)


def call(body, outs, *args, scratch=(), after=None, work=0):
    count = len(args)
    specs = [pl.BlockSpec(memory_space=pltpu.VMEM)] * count
    run = body
    if after is not None:
        run = lambda *refs: body(*refs[:count], *refs[count + 1 :])
        specs, args = specs + [pl.BlockSpec(memory_space=pl.ANY)], args + (after,)
    return pl.pallas_call(
        run,
        out_shape=outs,
        in_specs=specs,
        scratch_shapes=scratch,
        compiler_params=pltpu.CompilerParams(vmem_limit_bytes=VMEM_LIMIT),
        cost_estimate=pl.CostEstimate(flops=work, transcendentals=0, bytes_accessed=work // 100) if work else None,
    )(*args)


def project_body(
    x_hbm, y_hbm, w_in_hbm, w_out_hbm, h_hbm, keep_ref, send_ref, h_ref, parts, w_in, w_out, low, out, sems
):
    core = lax.axis_index("core")
    steps = [(y_hbm, w_out, out, k) for k in range(y_hbm.shape[1] // CHUNK)]
    steps += [(x_hbm, w_in, low, k) for k in range(x_hbm.shape[1] // CHUNK)]
    copies = [
        pltpu.make_async_copy(src.at[:, pl.ds(k * CHUNK, CHUNK)], parts.at[n], sems.at[n])
        for n, (src, _, _, k) in enumerate(steps)
    ]
    copy_out = pltpu.make_async_copy(w_out_hbm, w_out, sems.at[len(steps)])
    copy_in = pltpu.make_async_copy(w_in_hbm, w_in, sems.at[len(steps) + 1])
    copy_out.start()
    copies[0].start()
    copy_in.start()
    for copy in copies[1:]:
        copy.start()
    copy_held = pltpu.make_async_copy(h_hbm, h_ref, sems.at[len(steps) + 2])
    copy_held.start()
    copy_out.wait()
    for n, (src, weights, total, k) in enumerate(steps):
        copies[n].wait()
        if src is x_hbm and k == 0:
            copy_in.wait()
        part = lax.dot_general(
            weights[:, k * CHUNK : (k + 1) * CHUNK], parts[n], NT, preferred_element_type=F32
        )
        if k == 0:
            total[...] = part
        else:
            total[...] += part
    copy_held.wait()
    for c in range(NC):
        part = [low[(NC * j + c) * ROWS : (NC * j + c + 1) * ROWS] for j in range(NX)]
        part = jnp.concatenate(part + [out[c * HALF : (c + 1) * HALF]], 0)

        @pl.when(core == c)
        def _():
            keep_ref[...] = part

        @pl.when(core != c)
        def _():
            send_ref[...] = part


def project(x, y, w_in, w_out, held):
    steps = (x.shape[1] + y.shape[1]) // CHUNK
    args = [pltpu.with_memory_space_constraint(a, pltpu.HBM) for a in (x, y, w_in, w_out, held)]
    return pl.pallas_call(
        project_body,
        in_specs=[pl.BlockSpec(memory_space=pltpu.HBM)] * 5,
        out_shape=[shaped(RANK, TOK), shaped(RANK, TOK), shaped(*held.shape, dtype=BF16)],
        scratch_shapes=[
            pltpu.VMEM((steps, TOK, CHUNK), BF16),
            pltpu.VMEM(w_in.shape, BF16),
            pltpu.VMEM(w_out.shape, BF16),
            pltpu.VMEM((RANK, TOK), F32),
            pltpu.VMEM((RANK, TOK), F32),
            pltpu.SemaphoreType.DMA((steps + 3,)),
        ],
        compiler_params=pltpu.CompilerParams(vmem_limit_bytes=VMEM_LIMIT),
        cost_estimate=pl.CostEstimate(
            flops=2 * RANK * x.size + 2 * RANK * y.size, transcendentals=0, bytes_accessed=2 * (x.size + y.size)
        ),
    )(*args)


def coded(value):
    top = jnp.maximum(jnp.max(jnp.abs(value), 0, keepdims=True), 1e-30)
    power = jnp.clip(jnp.floor(jnp.log2(top)) - 13.0, -100.0, 100.0)
    return jnp.round(value / jnp.exp2(power)), power


def spread_body(keep_ref, got_ref, s1_ref, s2_ref, s3_ref, in_ref, out_ref):
    x = lax.axis_index("x")
    out = keep_ref[NX * ROWS :] + got_ref[NX * ROWS :]
    out_ref[...] = out
    out_code, out_power = coded(out)
    line = lax.broadcasted_iota(I32, (ROWS, TOK), 0)
    for d, ref in ((1, s1_ref), (2, s2_ref), (3, s3_ref), (0, None)):
        at = pl.ds(pl.multiple_of((x ^ d) * ROWS, ROWS), ROWS)
        part = keep_ref[at, :] + got_ref[at, :]
        if ref is None:
            in_ref[...] = part
        else:
            code, power = coded(part)
            powers = jnp.where(line == 0, power, out_power)
            ref[...] = jnp.concatenate([code, out_code, powers], 0).astype(I32).astype(I16)


def join_body(first_ref, second_ref, out_ref):
    out_ref[: first_ref.shape[0]] = first_ref[...]
    out_ref[first_ref.shape[0] :] = second_ref[...]


def add_body(in_ref, out_ref, g1_ref, g2_ref, g3_ref, low_ref, half_ref):
    low, half = in_ref[...], out_ref[...]
    for ref in (g1_ref, g2_ref, g3_ref):
        got = ref[...].astype(I32).astype(F32)
        powers = jnp.exp2(got[ROWS + HALF :])
        low = low + got[:ROWS] * powers[:1]
        half = half + got[ROWS : ROWS + HALF] * powers[1:2]
    low_ref[...] = low
    half_ref[...] = half


def parts_of(value):
    high = value.astype(BF16)
    return high, (value - high.astype(F32)).astype(BF16)


def outer_body(in_ref, mine_ref, other_ref, where_ref, goal_ref, p_ref):
    core = lax.axis_index("core")
    low, mine, other = in_ref[...], mine_ref[...], other_ref[...]
    out = jnp.concatenate([jnp.where(core == 0, mine, other), jnp.where(core == 0, other, mine)], 0)
    out_high, out_low = parts_of(out)
    onehot = lax.broadcasted_iota(I32, (E_DEV, TOK), 0) == where_ref[...]
    pairs = [parts_of(jnp.where(onehot, low[i : i + 1], 0.0)) for i in range(ROWS)]
    high = jnp.concatenate([p[0] for p in pairs], 0)
    rest = jnp.concatenate([p[1] for p in pairs], 0)
    dot = lambda u, v: lax.dot_general(u, v, NT, preferred_element_type=F32)
    grads = dot(high, out_high) + (dot(high, out_low) + dot(rest, out_high))
    flat = [grads[i * E_DEV : (i + 1) * E_DEV] for i in range(ROWS)]
    goal = jnp.broadcast_to(goal_ref[...], (E_DEV, 128))
    goal = jnp.where(lax.broadcasted_iota(I32, (E_DEV, 128), 1) < 64, goal >> 4, goal & 15)
    p_ref[...] = jnp.concatenate(flat + [goal.astype(F32)], 1).astype(BF16)


def score_body(p0, p1, p2, p3, first_ref, second_ref, keep_ref, send_ref, goal_ref, held):
    core, z = lax.axis_index("core"), lax.axis_index("z")
    for m, bits in enumerate((0, 4, 2, 6, 1, 5, 3, 7)):
        at = pl.ds(pl.multiple_of((z ^ bits) * C_DEV, C_DEV), C_DEV)
        held[at, :] = (first_ref, second_ref)[m // (NZ // 2)][m % (NZ // 2)]
    ps = [p[...] for p in (p0, p1, p2, p3)]
    left = jnp.concatenate([p[:, :K_DEV] for p in ps], 0)
    score = lax.dot_general(left, held[...], NT, preferred_element_type=F32)
    first, second = score[:, :C_HALF], score[:, C_HALF:]
    keep_ref[...] = jnp.where(core == 0, first, second)
    send_ref[...] = jnp.where(core == 0, second, first)
    goal = jnp.concatenate([p[:, K_DEV:] for p in ps], 0).astype(F32)
    goal_ref[...] = jnp.broadcast_to(goal[:, :1] * 16.0 + goal[:, 64:65], (E_ALL, 128))


def total_body(a0, a1, a2, a3, goal_ref, s0, s1, s2, s3, slots_ref):
    core, y = lax.axis_index("core"), lax.axis_index("y")
    score = (a0[...] + a1[...]) + (a2[...] + a3[...])
    for d, ref in enumerate((s0, s1, s2, s3)):
        ref[...] = score[d * E_DEV : (d + 1) * E_DEV]
    first = ((y * NC + core) * C_HALF).astype(F32)
    goal = goal_ref[...] - first
    lane = lax.broadcasted_iota(I32, (E_ALL, 128), 1).astype(F32)
    slots_ref[...] = jnp.zeros_like(slots_ref)
    for j in range(C_HALF // 128):
        hit = goal == lane + 128.0 * j
        sums = jnp.sum(jnp.where(hit, score[:, 128 * j : 128 * (j + 1)], 0.0), 0, keepdims=True)
        for i in range(128 // C_DEV):
            piece = sums[:, i * C_DEV : (i + 1) * C_DEV]
            at = (core * (NZ // NC) + j * (128 // C_DEV) + i) * NC
            for c in range(NC):
                slots_ref[pl.ds(at + c, 1), 0, :] = piece


def lay_body(mine_ref, other_ref, flag_ref, own_flag_ref, slots_ref, out_ref, total_ref):
    core, y, z = (lax.axis_index(name) for name in ("core", "y", "z"))
    for d in range(NY):
        for part, ref in ((core, mine_ref), (1 - core, other_ref)):
            at = pl.ds(pl.multiple_of((y ^ d) * C_ALL + part * C_HALF, C_HALF), C_HALF)
            out_ref[:, at] = ref[d * E_DEV : (d + 1) * E_DEV, :] * flag_ref[:, at].astype(F32)
    flags = own_flag_ref[pl.ds(y * NZ + z, 1), :].astype(F32)
    total_ref[...] = jnp.sum(slots_ref[...], 0) * flags


def per_device(
    down_matrix_feeds,
    result_slope_matrix,
    feed_sketch_factor,
    result_slope_factor,
    heldout_slope_entries,
    objective_of_sample,
    kept_choice_flags,
    token_sample_position,
):
    far = swap(heldout_slope_entries[None], "z", 4)
    keep, away, held = project(
        down_matrix_feeds,
        result_slope_matrix,
        feed_sketch_factor.T,
        result_slope_factor.T,
        heldout_slope_entries,
    )
    held = jnp.concatenate([held[None], far], 0)
    far = swap(held, "z", 2)

    sent = shaped(2 * ROWS + HALF, TOK, dtype=I16)
    low, half = shaped(ROWS, TOK), shaped(HALF, TOK)
    s1, s2, s3, in_own, out_chip = call(
        spread_body, [sent, sent, sent, low, half], keep, swap(away, "core", 1)
    )
    got = {d: swap(s, "x", d) for d, s in ((2, s2), (1, s1), (3, s3))}
    held = call(join_body, shaped(4, C_DEV, K_DEV, dtype=BF16), held, far, after=in_own)
    far = swap(held, "z", 1)
    in_sum, out_half = call(add_body, [low, half], in_own, out_chip, got[1], got[2], got[3])
    packed = call(
        outer_body,
        shaped(E_DEV, K_DEV + 128, dtype=BF16),
        in_sum,
        out_half,
        swap(out_half, "core", 1),
        token_sample_position,
        objective_of_sample[:, None],
        work=400000000,
    )
    packs = {d: swap(packed, "y", d) for d in (2, 1, 3)}

    side = shaped(E_ALL, C_HALF)
    keep, send, goal = call(
        score_body,
        [side, side, shaped(E_ALL, 128)],
        packed,
        packs[1],
        packs[2],
        packs[3],
        held,
        far,
        scratch=[pltpu.VMEM((C_ALL, K_DEV), BF16)],
    )
    score = keep + swap(send, "core", 1)
    got = {d: swap(score, "x", d) for d in (2, 1, 3)}
    piece = shaped(E_DEV, C_HALF)
    *pieces, slots = call(
        total_body,
        [piece] * NY + [shaped(NZ * NC, 1, C_DEV)],
        score,
        got[1],
        got[2],
        got[3],
        goal,
    )
    got = {d: swap(pieces[d], "y", d) for d in (2, 1, 3)}
    mine, slots = lax.optimization_barrier(
        (jnp.concatenate([pieces[0], got[1], got[2], got[3]], 0), slots)
    )
    sample_affinity, totals = call(
        lay_body,
        [shaped(E_DEV, CHOICES), shaped(1, C_DEV)],
        mine,
        swap(mine, "core", 1),
        kept_choice_flags.reshape(1, CHOICES),
        kept_choice_flags.reshape(NY * NZ, C_DEV),
        lax.all_to_all(slots, ("z", "core"), 0, 0, tiled=True),
    )
    return (sample_affinity, totals[0])


def solution(mesh):
    ex, tp = ("y", "z"), ("x", "core")
    chips = Mesh(mesh.devices.reshape(NY, NZ, NX, NC), ("y", "z", "x", "core"))
    placed = (
        P(ex, tp),
        P(ex, tp),
        P(tp, None),
        P(tp, None),
        P(ex, tp),
        P(ex),
        P(),
        P(ex, None),
    )
    return jax.shard_map(
        per_device, mesh=chips, in_specs=placed, out_specs=(P(ex, None), P(ex)), check_vma=False
    )
```

time: 75.1 us -> 67.8 us (0.903)
  blocking collectives: 12.3 us -> 0 us
  waiting for transfers between devices: 18.3 us -> 23 us
  other arithmetic: 0.95 us -> 0.03 us
  starting transfers between devices: 35.8 us -> 36.6 us
    all_to_all x1 -> x0, blocking collectives: 12.3 us -> none  [per_device(): slots = lax.all_to_all(slots, 'z', 0, 0, tiled=True)]
    all_to_all x0 -> x1, waiting for transfers between devices: none -> 6.87 us  [per_device(): lax.all_to_all(slots, ('z', 'core'), 0, 0, tiled=True)]
    all_to_all x0 -> x1, starting transfers between devices: none -> 4.55 us  [per_device(): lax.all_to_all(slots, ('z', 'core'), 0, 0, tiled=True)]
    ppermute x19, starting transfers between devices: 35.8 us -> 32.1 us  [swap(): lax.ppermute(value, axis, [(i, i ^ bits) for i in range(SIZES[axis])])]
    ppermute x19, waiting for transfers between devices: 18.3 us -> 16.1 us  [swap(): lax.ppermute(value, axis, [(i, i ^ bits) for i in range(SIZES[axis])])]
    concatenate x3 -> x2, other arithmetic: 0.93 us -> 0.02 us  [the longest x1 0.01 us: per_device(): held = jnp.concatenate([held[None], far], 0)]
  transfers between devices with their start and end apart: 19 -> 20, of which waited for: 12 -> 12; matrix products, arithmetic and copies ran while one was open for 0% -> 0% of each run, Pallas kernels for 7% -> 8%
where the time goes in v4:
time: 67.8 us; the launch traced here: 67.7 us
  starting transfers between devices  36.6 us (54%)
  waiting for transfers between devices  23 us (34%)
  Pallas kernels  7.15 us (11%)
  between operations  0.73 us (1%)
    ppermute x19, starting transfers between devices, swap(): lax.ppermute(value, axis, [(i, i ^ bits) for i in range(SIZES[axis])])  32.1 us
    ppermute x19, waiting for transfers between devices, swap(): lax.ppermute(value, axis, [(i, i ^ bits) for i in range(SIZES[axis])])  16.1 us
    all_to_all x1, waiting for transfers between devices, per_device(): lax.all_to_all(slots, ('z', 'core'), 0, 0, tiled=True)  6.87 us
    pallas_call x1, Pallas kernels, project(): pl.pallas_call(project_body, in_specs=[pl.BlockSpec(memory_space=pltpu.HB...  4.76 us
    all_to_all x1, starting transfers between devices, per_device(): lax.all_to_all(slots, ('z', 'core'), 0, 0, tiled=True)  4.55 us
    pallas_call x7, Pallas kernels, call(): pl.pallas_call(run, out_shape=outs, in_specs=specs, scratch_shapes=scratc...  2.38 us
  transfers between devices with their start and end apart: 20, of which 12 were waited for; matrix products, arithmetic and copies ran while one was open for 0% of the time, Pallas kernels for 8%

profile of v4, /device:TPU:1, one launch (start us, length us, event | category | flops | bytes accessed | tf_op | source)
XLA Modules:
  0.0 67.7 jit_solution(14623033681658373523)
XLA Ops:
  0.7 7.8 %collective-permute-start.8 = (bf16[1,64,512]{2,1,0:T(8,128)(2,1)}, bf16[1,64,512]{2,1,0:T(8,128)(2,1)S(1)}, u32[]{:S(2)}, u32[]{:S(2)}) collective-permute-start(bf16[1,64,512]{2,1,0:T(8,128)(2,1)} %bitcast.11), channel_id=1, source_target_pairs={{0,32},{8,40},{16,48},{24,56},{32,0},{40,8},{48,16},{56,24},{1,33}... | collective-permute-start | bytes 196616 | tf_op jit(solution)/shard_map/ppermute | solution.py:23
  8.5 4.8 %shard_map.95 = (f32[64,1024]{1,0:T(8,128)S(1)}, f32[64,1024]{1,0:T(8,128)S(1)}, bf16[64,512]{1,0:T(8,128)(2,1)S(1)}) custom-call(bf16[1024,3584]{1,0:T(8,128)(2,1)} %x_hbm.1, bf16[1024,1024]{1,0:T(8,128)(2,1)} %y_hbm.1, bf16[64,3584]{1,0:T(8,128)(2,1)} %bitcast.9, bf16[64,1024]{1,0:T(8,128)(2,1)} %bitcast.10, bf16[64,512]{1,0:T(8,128)(2,1)} %h_hbm.1), custom_call_target="tpu_custom_call" | custom-call | flops 603979776 | bytes 9437184 | tf_op jit(solution)/shard_map/pallas_call | solution.py:95
  13.3 1.0 %collective-permute-start = (f32[64,1024]{1,0:T(8,128)S(1)}, f32[64,1024]{1,0:T(8,128)S(1)}, u32[]{:S(2)}, u32[]{:S(2)}) collective-permute-start(f32[64,1024]{1,0:T(8,128)S(1)} %get-tuple-element.25), channel_id=1, source_target_pairs={{0,1},{1,0},{2,3},{3,2},{4,5},{5,4},{6,7},{7,6},{8,9},{9,8},{10,11... | collective-permute-start | bytes 786440 | tf_op jit(solution)/shard_map/ppermute | solution.py:23
  14.3 1.3 %collective-permute-start.9 = (bf16[2,64,512]{2,1,0:T(8,128)(2,1)S(1)}, bf16[2,64,512]{2,1,0:T(8,128)(2,1)S(1)}, u32[]{:S(2)}, u32[]{:S(2)}) collective-permute-start(bf16[2,64,512]{2,1,0:T(8,128)(2,1)S(1)} %pad_maximum_fusion.refs_0_), channel_id=1, source_target_pairs={{0,16},{8,24},{16,0},{24,8},{32,48},{40,56},{48,32},{56,40},{1,17}... | collective-permute-start | bytes 393224 | tf_op jit(solution)/shard_map/ppermute | solution.py:23
  15.7 1.3 %collective-permute-start.1 = (s16[48,1024]{1,0:T(8,128)(2,1)S(1)}, s16[48,1024]{1,0:T(8,128)(2,1)S(1)}, u32[]{:S(2)}, u32[]{:S(2)}) collective-permute-start(s16[48,1024]{1,0:T(8,128)(2,1)S(1)} %get-tuple-element.28), channel_id=1, source_target_pairs={{0,2},{2,0},{4,6},{6,4},{1,3},{3,1},{5,7},{7,5},{8,10},{10,8},{12,... | collective-permute-start | bytes 294920 | tf_op jit(solution)/shard_map/ppermute | solution.py:23
  17.0 2.5 %collective-permute-start.2 = (s16[48,1024]{1,0:T(8,128)(2,1)S(1)}, s16[48,1024]{1,0:T(8,128)(2,1)S(1)}, u32[]{:S(2)}, u32[]{:S(2)}) collective-permute-start(s16[48,1024]{1,0:T(8,128)(2,1)S(1)} %get-tuple-element.29), channel_id=1, source_target_pairs={{0,4},{2,6},{4,0},{6,2},{1,5},{3,7},{5,1},{7,3},{8,12},{10,14},{12... | collective-permute-start | bytes 294920 | tf_op jit(solution)/shard_map/ppermute | solution.py:23
  19.7 3.6 %collective-permute-done.9.refs_1_ = bf16[2,64,512]{2,1,0:T(8,128)(2,1)S(1)} collective-permute-done((bf16[2,64,512]{2,1,0:T(8,128)(2,1)S(1)}, bf16[2,64,512]{2,1,0:T(8,128)(2,1)S(1)}, u32[]{:S(2)}, u32[]{:S(2)}) %collective-permute-start.9) | collective-permute-done | bytes 131104 | tf_op jit(solution)/shard_map/ppermute | solution.py:23
  23.4 0.8 %collective-permute-done.2.g2_ref = s16[48,1024]{1,0:T(8,128)(2,1)S(1)} collective-permute-done((s16[48,1024]{1,0:T(8,128)(2,1)S(1)}, s16[48,1024]{1,0:T(8,128)(2,1)S(1)}, u32[]{:S(2)}, u32[]{:S(2)}) %collective-permute-start.2) | collective-permute-done | bytes 98336 | tf_op jit(solution)/shard_map/ppermute | solution.py:23
  24.2 2.6 %collective-permute-done.3.g3_ref = s16[48,1024]{1,0:T(8,128)(2,1)S(1)} collective-permute-done((s16[48,1024]{1,0:T(8,128)(2,1)S(1)}, s16[48,1024]{1,0:T(8,128)(2,1)S(1)}, u32[]{:S(2)}, u32[]{:S(2)}) %collective-permute-start.3) | collective-permute-done | bytes 98336 | tf_op jit(solution)/shard_map/ppermute | solution.py:23
  26.9 0.7 collective-permute-start.4
  27.6 0.9 %collective-permute-done.4.other_ref = f32[32,1024]{1,0:T(8,128)S(1)} collective-permute-done((f32[32,1024]{1,0:T(8,128)S(1)}, f32[32,1024]{1,0:T(8,128)S(1)}, u32[]{:S(2)}, u32[]{:S(2)}) %collective-permute-start.4) | collective-permute-done | bytes 131104 | tf_op jit(solution)/shard_map/ppermute | solution.py:23
  28.5 0.4 shard_map.98.p0
  29.0 1.3 %collective-permute-start.5 = (bf16[16,640]{1,0:T(8,128)(2,1)S(1)}, bf16[16,640]{1,0:T(8,128)(2,1)S(1)}, u32[]{:S(2)}, u32[]{:S(2)}) collective-permute-start(bf16[16,640]{1,0:T(8,128)(2,1)S(1)} %shard_map.98.p0), channel_id=1, source_target_pairs={{0,64},{64,0},{128,192},{192,128},{1,65},{65,1},{129,193},{193,129... | collective-permute-start | bytes 61448 | tf_op jit(solution)/shard_map/ppermute | solution.py:23
  30.3 2.6 %collective-permute-start.6 = (bf16[16,640]{1,0:T(8,128)(2,1)S(1)}, bf16[16,640]{1,0:T(8,128)(2,1)S(1)}, u32[]{:S(2)}, u32[]{:S(2)}) collective-permute-start(bf16[16,640]{1,0:T(8,128)(2,1)S(1)} %shard_map.98.p0), channel_id=1, source_target_pairs={{0,128},{64,192},{128,0},{192,64},{1,129},{65,193},{129,1},{193,65... | collective-permute-start | bytes 61448 | tf_op jit(solution)/shard_map/ppermute | solution.py:23
  33.0 1.5 %collective-permute-done.6.p2 = bf16[16,640]{1,0:T(8,128)(2,1)S(1)} collective-permute-done((bf16[16,640]{1,0:T(8,128)(2,1)S(1)}, bf16[16,640]{1,0:T(8,128)(2,1)S(1)}, u32[]{:S(2)}, u32[]{:S(2)}) %collective-permute-start.6) | collective-permute-done | bytes 20512 | tf_op jit(solution)/shard_map/ppermute | solution.py:23
  34.5 2.3 %collective-permute-done.7.p3 = bf16[16,640]{1,0:T(8,128)(2,1)S(1)} collective-permute-done((bf16[16,640]{1,0:T(8,128)(2,1)S(1)}, bf16[16,640]{1,0:T(8,128)(2,1)S(1)}, u32[]{:S(2)}, u32[]{:S(2)}) %collective-permute-start.7) | collective-permute-done | bytes 20512 | tf_op jit(solution)/shard_map/ppermute | solution.py:23
  36.8 0.3 shard_map.100
  37.1 2.2 %collective-permute-start.11 = (f32[64,256]{1,0:T(8,128)S(1)}, f32[64,256]{1,0:T(8,128)S(1)}, u32[]{:S(2)}, u32[]{:S(2)}) collective-permute-start(f32[64,256]{1,0:T(8,128)S(1)} %get-tuple-element.35), channel_id=1, source_target_pairs={{0,1},{1,0},{2,3},{3,2},{4,5},{5,4},{6,7},{7,6},{8,9},{9,8},{10,11... | collective-permute-start | bytes 196616 | tf_op jit(solution)/shard_map/ppermute | solution.py:23
  39.3 0.9 %collective-permute-done.11 = f32[64,256]{1,0:T(8,128)S(1)} collective-permute-done((f32[64,256]{1,0:T(8,128)S(1)}, f32[64,256]{1,0:T(8,128)S(1)}, u32[]{:S(2)}, u32[]{:S(2)}) %collective-permute-start.11) | collective-permute-done | bytes 65568 | tf_op jit(solution)/shard_map/ppermute | solution.py:23
  40.3 1.5 %collective-permute-start.13 = (f32[64,256]{1,0:T(8,128)S(1)}, f32[64,256]{1,0:T(8,128)S(1)}, u32[]{:S(2)}, u32[]{:S(2)}) collective-permute-start(f32[64,256]{1,0:T(8,128)S(1)} %add.3.a0), channel_id=1, source_target_pairs={{0,4},{2,6},{4,0},{6,2},{1,5},{3,7},{5,1},{7,3},{8,12},{10,14},{12... | collective-permute-start | bytes 196616 | tf_op jit(solution)/shard_map/ppermute | solution.py:23
  41.8 2.4 %collective-permute-start.14 = (f32[64,256]{1,0:T(8,128)S(1)}, f32[64,256]{1,0:T(8,128)S(1)}, u32[]{:S(2)}, u32[]{:S(2)}) collective-permute-start(f32[64,256]{1,0:T(8,128)S(1)} %add.3.a0), channel_id=1, source_target_pairs={{0,6},{2,4},{4,2},{6,0},{1,7},{3,5},{5,3},{7,1},{8,14},{10,12},{12... | collective-permute-start | bytes 196616 | tf_op jit(solution)/shard_map/ppermute | solution.py:23
  44.1 0.9 %collective-permute-done.13.a2 = f32[64,256]{1,0:T(8,128)S(1)} collective-permute-done((f32[64,256]{1,0:T(8,128)S(1)}, f32[64,256]{1,0:T(8,128)S(1)}, u32[]{:S(2)}, u32[]{:S(2)}) %collective-permute-start.13) | collective-permute-done | bytes 65568 | tf_op jit(solution)/shard_map/ppermute | solution.py:23
  45.0 1.5 %collective-permute-done.14.a3 = f32[64,256]{1,0:T(8,128)S(1)} collective-permute-done((f32[64,256]{1,0:T(8,128)S(1)}, f32[64,256]{1,0:T(8,128)S(1)}, u32[]{:S(2)}, u32[]{:S(2)}) %collective-permute-start.14) | collective-permute-done | bytes 65568 | tf_op jit(solution)/shard_map/ppermute | solution.py:23
  46.5 0.7 %shard_map.101 = (f32[16,256]{1,0:T(8,128)S(1)}, f32[16,256]{1,0:T(8,128)S(1)}, f32[16,256]{1,0:T(8,128)S(1)}, f32[16,256]{1,0:T(8,128)S(1)}, f32[16,1,64]{2,1,0:T(1,128)}) custom-call(f32[64,256]{1,0:T(8,128)S(1)} %add.3.a0, f32[64,256]{1,0:T(8,128)S(1)} %collective-permute-done.12.a1, f32[64,256]{1,0:T(8,128)S(1)} %collective-permute-done.13.a2, ...), custom_call_target="tpu_custom_call" | custom-call | tf_op jit(solution)/shard_map/pallas_call | solution.py:37
  47.2 1.1 %collective-permute-start.16 = (f32[16,256]{1,0:T(8,128)S(1)}, f32[16,256]{1,0:T(8,128)S(1)}, u32[]{:S(2)}, u32[]{:S(2)}) collective-permute-start(f32[16,256]{1,0:T(8,128)S(1)} %get-tuple-element.39), channel_id=1, source_target_pairs={{0,128},{64,192},{128,0},{192,64},{1,129},{65,193},{129,1},{193,65... | collective-permute-start | bytes 49160 | tf_op jit(solution)/shard_map/ppermute | solution.py:23
  48.3 2.7 %collective-permute-start.17 = (f32[16,256]{1,0:T(8,128)S(1)}, f32[16,256]{1,0:T(8,128)S(1)}, u32[]{:S(2)}, u32[]{:S(2)}) collective-permute-start(f32[16,256]{1,0:T(8,128)S(1)} %get-tuple-element.40), channel_id=1, source_target_pairs={{0,192},{64,128},{128,64},{192,0},{1,193},{65,129},{129,65},{193,1... | collective-permute-start | bytes 49160 | tf_op jit(solution)/shard_map/ppermute | solution.py:23
  51.1 0.2 collective-permute-done.16
  51.3 0.9 %collective-permute-done.17 = f32[16,256]{1,0:T(8,128)S(1)} collective-permute-done((f32[16,256]{1,0:T(8,128)S(1)}, f32[16,256]{1,0:T(8,128)S(1)}, u32[]{:S(2)}, u32[]{:S(2)}) %collective-permute-start.17) | collective-permute-done | bytes 16416 | tf_op jit(solution)/shard_map/ppermute | solution.py:23
  52.2 3.3 %collective-permute-start.18 = (f32[64,256]{1,0:T(8,128)S(1)}, f32[64,256]{1,0:T(8,128)S(1)}, u32[]{:S(2)}, u32[]{:S(2)}) collective-permute-start(f32[64,256]{1,0:T(8,128)S(1)} %pad_maximum_fusion.1.mine_ref), channel_id=1, source_target_pairs={{0,1},{1,0},{2,3},{3,2},{4,5},{5,4},{6,7},{7,6},{8,9},{9,8},{10,11... | collective-permute-start | bytes 196616 | tf_op jit(solution)/shard_map/ppermute | solution.py:23
  55.5 4.6 %all-to-all-start = ((f32[16,1,64]{2,1,0:T(1,128)}), f32[16,1,64]{2,1,0:T(1,128)S(1)}, u32[]{:S(2)}, u32[]{:S(2)}) async-start(f32[16,1,64]{2,1,0:T(1,128)} %get-tuple-element.43), calls=%async_computation | async-start | bytes 16384 | tf_op jit(solution)/shard_map/all_to_all | solution.py:296
  60.1 6.9 %all-to-all-done.slots_ref = f32[16,1,64]{2,1,0:T(1,128)S(1)} async-done(((f32[16,1,64]{2,1,0:T(1,128)}), f32[16,1,64]{2,1,0:T(1,128)S(1)}, u32[]{:S(2)}, u32[]{:S(2)}) %all-to-all-start) | async-done | bytes 4128 | tf_op jit(solution)/shard_map/all_to_all | solution.py:296
  67.0 0.7 %shard_map.102 = (f32[16,2048]{1,0:T(8,128)}, f32[1,64]{1,0:T(1,128)}) custom-call(f32[64,256]{1,0:T(8,128)S(1)} %pad_maximum_fusion.1.mine_ref, f32[64,256]{1,0:T(8,128)S(1)} %collective-permute-done.18.other_ref, s32[1,2048]{1,0:T(1,128)S(1)} %bitcast.8, s32[32,64]{1,0:T(8,128)S(1)} %reshape.11.own_flag_ref, f32[16,1,64]{2,1,0:T(1,128)S(1)} %all-to-all-done.slots_ref), custom_call_target="tpu_custom_call" | custom-call | tf_op jit(solution)/shard_map/pallas_call | solution.py:37
  (27 shorter events, 0.8 us)
Async XLA Ops:
  0.6 26.9 %copy-start.2 = (s32[16]{0:T(128)S(1)}, s32[16]{0:T(128)}, u32[]{:S(2)}) copy-start(s32[16]{0:T(128)} %param.13) | copy-start | bytes 196
  0.6 27.9 %copy-start.1 = (s32[1,1024]{1,0:T(1,128)S(1)}, s32[1,1024]{1,0:T(1,128)}, u32[]{:S(2)}) copy-start(s32[1,1024]{1,0:T(1,128)} %where_ref.1) | copy-start | bytes 12292
  0.7 59.4 %copy-start = (s32[2048]{0:T(1024)S(1)}, s32[2048]{0:T(1024)}, u32[]{:S(2)}) copy-start(s32[2048]{0:T(1024)} %param.14) | copy-start | bytes 24580
  0.7 13.6 %collective-permute-start.8 = (bf16[1,64,512]{2,1,0:T(8,128)(2,1)}, bf16[1,64,512]{2,1,0:T(8,128)(2,1)S(1)}, u32[]{:S(2)}, u32[]{:S(2)}) collective-permute-start(bf16[1,64,512]{2,1,0:T(8,128)(2,1)} %bitcast.11), channel_id=1, source_target_pairs={{0,32},{8,40},{16,48},{24,56},{32,0},{40,8},{48,16},{56,24},{1,33}... | collective-permute-start | bytes 196616 | tf_op jit(solution)/shard_map/ppermute | solution.py:23
  13.3 2.3 %collective-permute-start = (f32[64,1024]{1,0:T(8,128)S(1)}, f32[64,1024]{1,0:T(8,128)S(1)}, u32[]{:S(2)}, u32[]{:S(2)}) collective-permute-start(f32[64,1024]{1,0:T(8,128)S(1)} %get-tuple-element.25), channel_id=1, source_target_pairs={{0,1},{1,0},{2,3},{3,2},{4,5},{5,4},{6,7},{7,6},{8,9},{9,8},{10,11... | collective-permute-start | bytes 786440 | tf_op jit(solution)/shard_map/ppermute | solution.py:23
  14.3 8.9 %collective-permute-start.9 = (bf16[2,64,512]{2,1,0:T(8,128)(2,1)S(1)}, bf16[2,64,512]{2,1,0:T(8,128)(2,1)S(1)}, u32[]{:S(2)}, u32[]{:S(2)}) collective-permute-start(bf16[2,64,512]{2,1,0:T(8,128)(2,1)S(1)} %pad_maximum_fusion.refs_0_), channel_id=1, source_target_pairs={{0,16},{8,24},{16,0},{24,8},{32,48},{40,56},{48,32},{56,40},{1,17}... | collective-permute-start | bytes 393224 | tf_op jit(solution)/shard_map/ppermute | solution.py:23
  15.7 7.6 %collective-permute-start.1 = (s16[48,1024]{1,0:T(8,128)(2,1)S(1)}, s16[48,1024]{1,0:T(8,128)(2,1)S(1)}, u32[]{:S(2)}, u32[]{:S(2)}) collective-permute-start(s16[48,1024]{1,0:T(8,128)(2,1)S(1)} %get-tuple-element.28), channel_id=1, source_target_pairs={{0,2},{2,0},{4,6},{6,4},{1,3},{3,1},{5,7},{7,5},{8,10},{10,8},{12,... | collective-permute-start | bytes 294920 | tf_op jit(solution)/shard_map/ppermute | solution.py:23
  17.0 7.2 %collective-permute-start.2 = (s16[48,1024]{1,0:T(8,128)(2,1)S(1)}, s16[48,1024]{1,0:T(8,128)(2,1)S(1)}, u32[]{:S(2)}, u32[]{:S(2)}) collective-permute-start(s16[48,1024]{1,0:T(8,128)(2,1)S(1)} %get-tuple-element.29), channel_id=1, source_target_pairs={{0,4},{2,6},{4,0},{6,2},{1,5},{3,7},{5,1},{7,3},{8,12},{10,14},{12... | collective-permute-start | bytes 294920 | tf_op jit(solution)/shard_map/ppermute | solution.py:23
  19.5 7.3 %collective-permute-start.3 = (s16[48,1024]{1,0:T(8,128)(2,1)S(1)}, s16[48,1024]{1,0:T(8,128)(2,1)S(1)}, u32[]{:S(2)}, u32[]{:S(2)}) collective-permute-start(s16[48,1024]{1,0:T(8,128)(2,1)S(1)} %get-tuple-element.30), channel_id=1, source_target_pairs={{0,6},{2,4},{4,2},{6,0},{1,7},{3,5},{5,3},{7,1},{8,14},{10,12},{12... | collective-permute-start | bytes 294920 | tf_op jit(solution)/shard_map/ppermute | solution.py:23
  23.3 13.5 %collective-permute-start.10 = (bf16[4,64,512]{2,1,0:T(8,128)(2,1)S(1)}, bf16[4,64,512]{2,1,0:T(8,128)(2,1)S(1)}, u32[]{:S(2)}, u32[]{:S(2)}) collective-permute-start(bf16[4,64,512]{2,1,0:T(8,128)(2,1)S(1)} %shard_map.99.first_ref), channel_id=1, source_target_pairs={{0,8},{8,0},{16,24},{24,16},{32,40},{40,32},{48,56},{56,48},{1,9},... | collective-permute-start | bytes 786440 | tf_op jit(solution)/shard_map/ppermute | solution.py:23
  26.9 1.6 %collective-permute-start.4 = (f32[32,1024]{1,0:T(8,128)S(1)}, f32[32,1024]{1,0:T(8,128)S(1)}, u32[]{:S(2)}, u32[]{:S(2)}) collective-permute-start(f32[32,1024]{1,0:T(8,128)S(1)} %get-tuple-element.32.mine_ref), channel_id=1, source_target_pairs={{0,1},{1,0},{2,3},{3,2},{4,5},{5,4},{6,7},{7,6},{8,9},{9,8},{10,11... | collective-permute-start | bytes 393224 | tf_op jit(solution)/shard_map/ppermute | solution.py:23
  29.0 4.0 %collective-permute-start.5 = (bf16[16,640]{1,0:T(8,128)(2,1)S(1)}, bf16[16,640]{1,0:T(8,128)(2,1)S(1)}, u32[]{:S(2)}, u32[]{:S(2)}) collective-permute-start(bf16[16,640]{1,0:T(8,128)(2,1)S(1)} %shard_map.98.p0), channel_id=1, source_target_pairs={{0,64},{64,0},{128,192},{192,128},{1,65},{65,1},{129,193},{193,129... | collective-permute-start | bytes 61448 | tf_op jit(solution)/shard_map/ppermute | solution.py:23
  30.3 4.1 %collective-permute-start.6 = (bf16[16,640]{1,0:T(8,128)(2,1)S(1)}, bf16[16,640]{1,0:T(8,128)(2,1)S(1)}, u32[]{:S(2)}, u32[]{:S(2)}) collective-permute-start(bf16[16,640]{1,0:T(8,128)(2,1)S(1)} %shard_map.98.p0), channel_id=1, source_target_pairs={{0,128},{64,192},{128,0},{192,64},{1,129},{65,193},{129,1},{193,65... | collective-permute-start | bytes 61448 | tf_op jit(solution)/shard_map/ppermute | solution.py:23
  32.9 3.8 %collective-permute-start.7 = (bf16[16,640]{1,0:T(8,128)(2,1)S(1)}, bf16[16,640]{1,0:T(8,128)(2,1)S(1)}, u32[]{:S(2)}, u32[]{:S(2)}) collective-permute-start(bf16[16,640]{1,0:T(8,128)(2,1)S(1)} %shard_map.98.p0), channel_id=1, source_target_pairs={{0,192},{64,128},{128,64},{192,0},{1,193},{65,129},{129,65},{193,1... | collective-permute-start | bytes 61448 | tf_op jit(solution)/shard_map/ppermute | solution.py:23
  37.1 3.1 %collective-permute-start.11 = (f32[64,256]{1,0:T(8,128)S(1)}, f32[64,256]{1,0:T(8,128)S(1)}, u32[]{:S(2)}, u32[]{:S(2)}) collective-permute-start(f32[64,256]{1,0:T(8,128)S(1)} %get-tuple-element.35), channel_id=1, source_target_pairs={{0,1},{1,0},{2,3},{3,2},{4,5},{5,4},{6,7},{7,6},{8,9},{9,8},{10,11... | collective-permute-start | bytes 196616 | tf_op jit(solution)/shard_map/ppermute | solution.py:23
  40.2 3.9 %collective-permute-start.12 = (f32[64,256]{1,0:T(8,128)S(1)}, f32[64,256]{1,0:T(8,128)S(1)}, u32[]{:S(2)}, u32[]{:S(2)}) collective-permute-start(f32[64,256]{1,0:T(8,128)S(1)} %add.3.a0), channel_id=1, source_target_pairs={{0,2},{2,0},{4,6},{6,4},{1,3},{3,1},{5,7},{7,5},{8,10},{10,8},{12,... | collective-permute-start | bytes 196616 | tf_op jit(solution)/shard_map/ppermute | solution.py:23
  40.3 4.7 %collective-permute-start.13 = (f32[64,256]{1,0:T(8,128)S(1)}, f32[64,256]{1,0:T(8,128)S(1)}, u32[]{:S(2)}, u32[]{:S(2)}) collective-permute-start(f32[64,256]{1,0:T(8,128)S(1)} %add.3.a0), channel_id=1, source_target_pairs={{0,4},{2,6},{4,0},{6,2},{1,5},{3,7},{5,1},{7,3},{8,12},{10,14},{12... | collective-permute-start | bytes 196616 | tf_op jit(solution)/shard_map/ppermute | solution.py:23
  41.8 4.7 %collective-permute-start.14 = (f32[64,256]{1,0:T(8,128)S(1)}, f32[64,256]{1,0:T(8,128)S(1)}, u32[]{:S(2)}, u32[]{:S(2)}) collective-permute-start(f32[64,256]{1,0:T(8,128)S(1)} %add.3.a0), channel_id=1, source_target_pairs={{0,6},{2,4},{4,2},{6,0},{1,7},{3,5},{5,3},{7,1},{8,14},{10,12},{12... | collective-permute-start | bytes 196616 | tf_op jit(solution)/shard_map/ppermute | solution.py:23
  47.2 3.9 %collective-permute-start.15 = (f32[16,256]{1,0:T(8,128)S(1)}, f32[16,256]{1,0:T(8,128)S(1)}, u32[]{:S(2)}, u32[]{:S(2)}) collective-permute-start(f32[16,256]{1,0:T(8,128)S(1)} %get-tuple-element.38), channel_id=1, source_target_pairs={{0,64},{64,0},{128,192},{192,128},{1,65},{65,1},{129,193},{193,129... | collective-permute-start | bytes 49160 | tf_op jit(solution)/shard_map/ppermute | solution.py:23
  47.2 4.1 %collective-permute-start.16 = (f32[16,256]{1,0:T(8,128)S(1)}, f32[16,256]{1,0:T(8,128)S(1)}, u32[]{:S(2)}, u32[]{:S(2)}) collective-permute-start(f32[16,256]{1,0:T(8,128)S(1)} %get-tuple-element.39), channel_id=1, source_target_pairs={{0,128},{64,192},{128,0},{192,64},{1,129},{65,193},{129,1},{193,65... | collective-permute-start | bytes 49160 | tf_op jit(solution)/shard_map/ppermute | solution.py:23
  48.3 3.9 %collective-permute-start.17 = (f32[16,256]{1,0:T(8,128)S(1)}, f32[16,256]{1,0:T(8,128)S(1)}, u32[]{:S(2)}, u32[]{:S(2)}) collective-permute-start(f32[16,256]{1,0:T(8,128)S(1)} %get-tuple-element.40), channel_id=1, source_target_pairs={{0,192},{64,128},{128,64},{192,0},{1,193},{65,129},{129,65},{193,1... | collective-permute-start | bytes 49160 | tf_op jit(solution)/shard_map/ppermute | solution.py:23
  52.2 14.8 %collective-permute-start.18 = (f32[64,256]{1,0:T(8,128)S(1)}, f32[64,256]{1,0:T(8,128)S(1)}, u32[]{:S(2)}, u32[]{:S(2)}) collective-permute-start(f32[64,256]{1,0:T(8,128)S(1)} %pad_maximum_fusion.1.mine_ref), channel_id=1, source_target_pairs={{0,1},{1,0},{2,3},{3,2},{4,5},{5,4},{6,7},{7,6},{8,9},{9,8},{10,11... | collective-permute-start | bytes 196616 | tf_op jit(solution)/shard_map/ppermute | solution.py:23
  55.5 11.5 %all-to-all-start = ((f32[16,1,64]{2,1,0:T(1,128)}), f32[16,1,64]{2,1,0:T(1,128)S(1)}, u32[]{:S(2)}, u32[]{:S(2)}) async-start(f32[16,1,64]{2,1,0:T(1,128)} %get-tuple-element.43), calls=%async_computation | async-start | bytes 16384 | tf_op jit(solution)/shard_map/all_to_all | solution.py:296

commit v5 on v4

--- a/solution.py
+++ b/solution.py
@@ -174,7 +174,7 @@
 
 def score_body(p0, p1, p2, p3, first_ref, second_ref, keep_ref, send_ref, goal_ref, held):
     core, z = lax.axis_index("core"), lax.axis_index("z")
-    for m, bits in enumerate((0, 4, 2, 6, 1, 5, 3, 7)):
+    for m, bits in enumerate((0, 2, 4, 6, 1, 3, 5, 7)):
         at = pl.ds(pl.multiple_of((z ^ bits) * C_DEV, C_DEV), C_DEV)
         held[at, :] = (first_ref, second_ref)[m // (NZ // 2)][m % (NZ // 2)]
     ps = [p[...] for p in (p0, p1, p2, p3)]
@@ -195,15 +195,14 @@
     first = ((y * NC + core) * C_HALF).astype(F32)
     goal = goal_ref[...] - first
     lane = lax.broadcasted_iota(I32, (E_ALL, 128), 1).astype(F32)
-    slots_ref[...] = jnp.zeros_like(slots_ref)
+    pieces = []
     for j in range(C_HALF // 128):
         hit = goal == lane + 128.0 * j
         sums = jnp.sum(jnp.where(hit, score[:, 128 * j : 128 * (j + 1)], 0.0), 0, keepdims=True)
-        for i in range(128 // C_DEV):
-            piece = sums[:, i * C_DEV : (i + 1) * C_DEV]
-            at = (core * (NZ // NC) + j * (128 // C_DEV) + i) * NC
-            for c in range(NC):
-                slots_ref[pl.ds(at + c, 1), 0, :] = piece
+        pieces += [sums[:, i * C_DEV : (i + 1) * C_DEV] for i in range(128 // C_DEV) for _ in range(NC)]
+    rows = jnp.concatenate(pieces, 0)
+    for c in range(NC):
+        slots_ref[c * len(pieces) : (c + 1) * len(pieces)] = jnp.where(core == c, rows, 0.0)
 
 
 def lay_body(mine_ref, other_ref, flag_ref, own_flag_ref, slots_ref, out_ref, total_ref):
@@ -213,7 +212,7 @@
             at = pl.ds(pl.multiple_of((y ^ d) * C_ALL + part * C_HALF, C_HALF), C_HALF)
             out_ref[:, at] = ref[d * E_DEV : (d + 1) * E_DEV, :] * flag_ref[:, at].astype(F32)
     flags = own_flag_ref[pl.ds(y * NZ + z, 1), :].astype(F32)
-    total_ref[...] = jnp.sum(slots_ref[...], 0) * flags
+    total_ref[...] = jnp.sum(slots_ref[...], 0, keepdims=True) * flags
 
 
 def per_device(
@@ -226,7 +225,7 @@
     kept_choice_flags,
     token_sample_position,
 ):
-    far = swap(heldout_slope_entries[None], "z", 4)
+    far = swap(heldout_slope_entries[None], "z", 2)
     keep, away, held = project(
         down_matrix_feeds,
         result_slope_matrix,
@@ -235,7 +234,7 @@
         heldout_slope_entries,
     )
     held = jnp.concatenate([held[None], far], 0)
-    far = swap(held, "z", 2)
+    far = swap(held, "z", 4)
 
     sent = shaped(2 * ROWS + HALF, TOK, dtype=I16)
     low, half = shaped(ROWS, TOK), shaped(HALF, TOK)
@@ -243,7 +242,7 @@
         spread_body, [sent, sent, sent, low, half], keep, swap(away, "core", 1)
     )
     got = {d: swap(s, "x", d) for d, s in ((2, s2), (1, s1), (3, s3))}
-    held = call(join_body, shaped(4, C_DEV, K_DEV, dtype=BF16), held, far, after=in_own)
+    held = call(join_body, shaped(NZ // 2, C_DEV, K_DEV, dtype=BF16), held, far, after=in_own)
     far = swap(held, "z", 1)
     in_sum, out_half = call(add_body, [low, half], in_own, out_chip, got[1], got[2], got[3])
     packed = call(
@@ -254,7 +253,7 @@
         swap(out_half, "core", 1),
         token_sample_position,
         objective_of_sample[:, None],
-        work=400000000,
+        work=400_000_000,
     )
     packs = {d: swap(packed, "y", d) for d in (2, 1, 3)}
 
@@ -275,7 +274,7 @@
     piece = shaped(E_DEV, C_HALF)
     *pieces, slots = call(
         total_body,
-        [piece] * NY + [shaped(NZ * NC, 1, C_DEV)],
+        [piece] * NY + [shaped(NZ * NC, C_DEV)],
         score,
         got[1],
         got[2],
@@ -283,9 +282,7 @@
         goal,
     )
     got = {d: swap(pieces[d], "y", d) for d in (2, 1, 3)}
-    mine, slots = lax.optimization_barrier(
-        (jnp.concatenate([pieces[0], got[1], got[2], got[3]], 0), slots)
-    )
+    mine = jnp.concatenate([pieces[0], got[1], got[2], got[3]], 0)
     sample_affinity, totals = call(
         lay_body,
         [shaped(E_DEV, CHOICES), shaped(1, C_DEV)],

time: 67.8 us -> 68.9 us (1.016)
  starting transfers between devices: 36.6 us -> 42.1 us
  waiting for transfers between devices: 23 us -> 18.6 us
    ppermute x19, starting transfers between devices: 32.1 us -> 36.4 us  [swap(): lax.ppermute(value, axis, [(i, i ^ bits) for i in range(SIZES[axis])])]
    ppermute x19, waiting for transfers between devices: 16.1 us -> 11.8 us  [swap(): lax.ppermute(value, axis, [(i, i ^ bits) for i in range(SIZES[axis])])]
    all_to_all x1, starting transfers between devices: 4.55 us -> 5.69 us  [per_device(): lax.all_to_all(slots, ('z', 'core'), 0, 0, tiled=True)]
  transfers between devices with their start and end apart: 20 -> 20, of which waited for: 12 -> 10; matrix products, arithmetic and copies ran while one was open for 0% -> 0% of each run, Pallas kernels for 8% -> 8%
where the time goes in v5:
time: 68.9 us; the launch traced here: 68.8 us
  starting transfers between devices  42.1 us (61%)
  waiting for transfers between devices  18.6 us (27%)
  Pallas kernels  7.14 us (10%)
  between operations  0.72 us (1%)
    ppermute x19, starting transfers between devices, swap(): lax.ppermute(value, axis, [(i, i ^ bits) for i in range(SIZES[axis])])  36.4 us
    ppermute x19, waiting for transfers between devices, swap(): lax.ppermute(value, axis, [(i, i ^ bits) for i in range(SIZES[axis])])  11.8 us
    all_to_all x1, waiting for transfers between devices, per_device(): lax.all_to_all(slots, ('z', 'core'), 0, 0, tiled=True)  6.87 us
    all_to_all x1, starting transfers between devices, per_device(): lax.all_to_all(slots, ('z', 'core'), 0, 0, tiled=True)  5.69 us
    pallas_call x1, Pallas kernels, project(): pl.pallas_call(project_body, in_specs=[pl.BlockSpec(memory_space=pltpu.HB...  4.77 us
    pallas_call x7, Pallas kernels, call(): pl.pallas_call(run, out_shape=outs, in_specs=specs, scratch_shapes=scratc...  2.38 us
  transfers between devices with their start and end apart: 20, of which 10 were waited for; matrix products, arithmetic and copies ran while one was open for 0% of the time, Pallas kernels for 8%

profile of v5, /device:TPU:1, one launch (start us, length us, event | category | flops | bytes accessed | tf_op | source)
XLA Modules:
  0.0 68.8 jit_solution(5315925062042254012)
XLA Ops:
  0.7 3.9 %collective-permute-start.8 = (bf16[1,64,512]{2,1,0:T(8,128)(2,1)}, bf16[1,64,512]{2,1,0:T(8,128)(2,1)S(1)}, u32[]{:S(2)}, u32[]{:S(2)}) collective-permute-start(bf16[1,64,512]{2,1,0:T(8,128)(2,1)} %bitcast.16), channel_id=1, source_target_pairs={{0,16},{8,24},{16,0},{24,8},{32,48},{40,56},{48,32},{56,40},{1,17}... | collective-permute-start | bytes 196616 | tf_op jit(solution)/shard_map/ppermute | solution.py:23
  4.6 4.8 %shard_map.95 = (f32[64,1024]{1,0:T(8,128)S(1)}, f32[64,1024]{1,0:T(8,128)S(1)}, bf16[64,512]{1,0:T(8,128)(2,1)S(1)}) custom-call(bf16[1024,3584]{1,0:T(8,128)(2,1)} %x_hbm.1, bf16[1024,1024]{1,0:T(8,128)(2,1)} %y_hbm.1, bf16[64,3584]{1,0:T(8,128)(2,1)} %bitcast.14, bf16[64,1024]{1,0:T(8,128)(2,1)} %bitcast.15, bf16[64,512]{1,0:T(8,128)(2,1)} %h_hbm.1), custom_call_target="tpu_custom_call" | custom-call | flops 603979776 | bytes 9437184 | tf_op jit(solution)/shard_map/pallas_call | solution.py:95
  9.3 1.0 %collective-permute-start = (f32[64,1024]{1,0:T(8,128)S(1)}, f32[64,1024]{1,0:T(8,128)S(1)}, u32[]{:S(2)}, u32[]{:S(2)}) collective-permute-start(f32[64,1024]{1,0:T(8,128)S(1)} %get-tuple-element.23), channel_id=1, source_target_pairs={{0,1},{1,0},{2,3},{3,2},{4,5},{5,4},{6,7},{7,6},{8,9},{9,8},{10,11... | collective-permute-start | bytes 786440 | tf_op jit(solution)/shard_map/ppermute | solution.py:23
  10.4 5.2 %collective-permute-start.9 = (bf16[2,64,512]{2,1,0:T(8,128)(2,1)S(1)}, bf16[2,64,512]{2,1,0:T(8,128)(2,1)S(1)}, u32[]{:S(2)}, u32[]{:S(2)}) collective-permute-start(bf16[2,64,512]{2,1,0:T(8,128)(2,1)S(1)} %pad_maximum_fusion.refs_0_), channel_id=1, source_target_pairs={{0,32},{8,40},{16,48},{24,56},{32,0},{40,8},{48,16},{56,24},{1,33}... | collective-permute-start | bytes 393224 | tf_op jit(solution)/shard_map/ppermute | solution.py:23
  15.7 1.3 %collective-permute-start.1 = (s16[48,1024]{1,0:T(8,128)(2,1)S(1)}, s16[48,1024]{1,0:T(8,128)(2,1)S(1)}, u32[]{:S(2)}, u32[]{:S(2)}) collective-permute-start(s16[48,1024]{1,0:T(8,128)(2,1)S(1)} %get-tuple-element.26), channel_id=1, source_target_pairs={{0,2},{2,0},{4,6},{6,4},{1,3},{3,1},{5,7},{7,5},{8,10},{10,8},{12,... | collective-permute-start | bytes 294920 | tf_op jit(solution)/shard_map/ppermute | solution.py:23
  17.0 2.4 %collective-permute-start.2 = (s16[48,1024]{1,0:T(8,128)(2,1)S(1)}, s16[48,1024]{1,0:T(8,128)(2,1)S(1)}, u32[]{:S(2)}, u32[]{:S(2)}) collective-permute-start(s16[48,1024]{1,0:T(8,128)(2,1)S(1)} %get-tuple-element.27), channel_id=1, source_target_pairs={{0,4},{2,6},{4,0},{6,2},{1,5},{3,7},{5,1},{7,3},{8,12},{10,14},{12... | collective-permute-start | bytes 294920 | tf_op jit(solution)/shard_map/ppermute | solution.py:23
  19.5 0.2 collective-permute-start.3
  19.7 4.5 %collective-permute-start.10 = (bf16[4,64,512]{2,1,0:T(8,128)(2,1)S(1)}, bf16[4,64,512]{2,1,0:T(8,128)(2,1)S(1)}, u32[]{:S(2)}, u32[]{:S(2)}) collective-permute-start(bf16[4,64,512]{2,1,0:T(8,128)(2,1)S(1)} %shard_map.99.first_ref), channel_id=1, source_target_pairs={{0,8},{8,0},{16,24},{24,16},{32,40},{40,32},{48,56},{56,48},{1,9},... | collective-permute-start | bytes 786440 | tf_op jit(solution)/shard_map/ppermute | solution.py:23
  24.2 2.6 %collective-permute-done.3.g3_ref = s16[48,1024]{1,0:T(8,128)(2,1)S(1)} collective-permute-done((s16[48,1024]{1,0:T(8,128)(2,1)S(1)}, s16[48,1024]{1,0:T(8,128)(2,1)S(1)}, u32[]{:S(2)}, u32[]{:S(2)}) %collective-permute-start.3) | collective-permute-done | bytes 98336 | tf_op jit(solution)/shard_map/ppermute | solution.py:23
  26.9 0.7 collective-permute-start.4
  27.6 0.9 %collective-permute-done.4.other_ref = f32[32,1024]{1,0:T(8,128)S(1)} collective-permute-done((f32[32,1024]{1,0:T(8,128)S(1)}, f32[32,1024]{1,0:T(8,128)S(1)}, u32[]{:S(2)}, u32[]{:S(2)}) %collective-permute-start.4) | collective-permute-done | bytes 131104 | tf_op jit(solution)/shard_map/ppermute | solution.py:23
  28.5 0.4 shard_map.98.p0
  29.0 1.3 %collective-permute-start.5 = (bf16[16,640]{1,0:T(8,128)(2,1)S(1)}, bf16[16,640]{1,0:T(8,128)(2,1)S(1)}, u32[]{:S(2)}, u32[]{:S(2)}) collective-permute-start(bf16[16,640]{1,0:T(8,128)(2,1)S(1)} %shard_map.98.p0), channel_id=1, source_target_pairs={{0,64},{64,0},{128,192},{192,128},{1,65},{65,1},{129,193},{193,129... | collective-permute-start | bytes 61448 | tf_op jit(solution)/shard_map/ppermute | solution.py:23
  30.3 2.6 %collective-permute-start.6 = (bf16[16,640]{1,0:T(8,128)(2,1)S(1)}, bf16[16,640]{1,0:T(8,128)(2,1)S(1)}, u32[]{:S(2)}, u32[]{:S(2)}) collective-permute-start(bf16[16,640]{1,0:T(8,128)(2,1)S(1)} %shard_map.98.p0), channel_id=1, source_target_pairs={{0,128},{64,192},{128,0},{192,64},{1,129},{65,193},{129,1},{193,65... | collective-permute-start | bytes 61448 | tf_op jit(solution)/shard_map/ppermute | solution.py:23
  32.9 1.5 %collective-permute-done.6.p2 = bf16[16,640]{1,0:T(8,128)(2,1)S(1)} collective-permute-done((bf16[16,640]{1,0:T(8,128)(2,1)S(1)}, bf16[16,640]{1,0:T(8,128)(2,1)S(1)}, u32[]{:S(2)}, u32[]{:S(2)}) %collective-permute-start.6) | collective-permute-done | bytes 20512 | tf_op jit(solution)/shard_map/ppermute | solution.py:23
  34.5 2.3 %collective-permute-done.7.p3 = bf16[16,640]{1,0:T(8,128)(2,1)S(1)} collective-permute-done((bf16[16,640]{1,0:T(8,128)(2,1)S(1)}, bf16[16,640]{1,0:T(8,128)(2,1)S(1)}, u32[]{:S(2)}, u32[]{:S(2)}) %collective-permute-start.7) | collective-permute-done | bytes 20512 | tf_op jit(solution)/shard_map/ppermute | solution.py:23
  36.8 0.3 shard_map.100
  37.1 2.2 %collective-permute-start.11 = (f32[64,256]{1,0:T(8,128)S(1)}, f32[64,256]{1,0:T(8,128)S(1)}, u32[]{:S(2)}, u32[]{:S(2)}) collective-permute-start(f32[64,256]{1,0:T(8,128)S(1)} %get-tuple-element.33), channel_id=1, source_target_pairs={{0,1},{1,0},{2,3},{3,2},{4,5},{5,4},{6,7},{7,6},{8,9},{9,8},{10,11... | collective-permute-start | bytes 196616 | tf_op jit(solution)/shard_map/ppermute | solution.py:23
  39.3 0.9 %collective-permute-done.11 = f32[64,256]{1,0:T(8,128)S(1)} collective-permute-done((f32[64,256]{1,0:T(8,128)S(1)}, f32[64,256]{1,0:T(8,128)S(1)}, u32[]{:S(2)}, u32[]{:S(2)}) %collective-permute-start.11) | collective-permute-done | bytes 65568 | tf_op jit(solution)/shard_map/ppermute | solution.py:23
  40.3 1.5 %collective-permute-start.13 = (f32[64,256]{1,0:T(8,128)S(1)}, f32[64,256]{1,0:T(8,128)S(1)}, u32[]{:S(2)}, u32[]{:S(2)}) collective-permute-start(f32[64,256]{1,0:T(8,128)S(1)} %add.3.a0), channel_id=1, source_target_pairs={{0,4},{2,6},{4,0},{6,2},{1,5},{3,7},{5,1},{7,3},{8,12},{10,14},{12... | collective-permute-start | bytes 196616 | tf_op jit(solution)/shard_map/ppermute | solution.py:23
  41.8 2.4 %collective-permute-start.14 = (f32[64,256]{1,0:T(8,128)S(1)}, f32[64,256]{1,0:T(8,128)S(1)}, u32[]{:S(2)}, u32[]{:S(2)}) collective-permute-start(f32[64,256]{1,0:T(8,128)S(1)} %add.3.a0), channel_id=1, source_target_pairs={{0,6},{2,4},{4,2},{6,0},{1,7},{3,5},{5,3},{7,1},{8,14},{10,12},{12... | collective-permute-start | bytes 196616 | tf_op jit(solution)/shard_map/ppermute | solution.py:23
  44.1 0.9 %collective-permute-done.13.a2 = f32[64,256]{1,0:T(8,128)S(1)} collective-permute-done((f32[64,256]{1,0:T(8,128)S(1)}, f32[64,256]{1,0:T(8,128)S(1)}, u32[]{:S(2)}, u32[]{:S(2)}) %collective-permute-start.13) | collective-permute-done | bytes 65568 | tf_op jit(solution)/shard_map/ppermute | solution.py:23
  45.0 1.5 %collective-permute-done.14.a3 = f32[64,256]{1,0:T(8,128)S(1)} collective-permute-done((f32[64,256]{1,0:T(8,128)S(1)}, f32[64,256]{1,0:T(8,128)S(1)}, u32[]{:S(2)}, u32[]{:S(2)}) %collective-permute-start.14) | collective-permute-done | bytes 65568 | tf_op jit(solution)/shard_map/ppermute | solution.py:23
  46.5 0.7 %shard_map.101 = (f32[16,256]{1,0:T(8,128)S(1)}, f32[16,256]{1,0:T(8,128)S(1)}, f32[16,256]{1,0:T(8,128)S(1)}, f32[16,256]{1,0:T(8,128)S(1)}, f32[16,64]{1,0:T(8,128)}) custom-call(f32[64,256]{1,0:T(8,128)S(1)} %add.3.a0, f32[64,256]{1,0:T(8,128)S(1)} %collective-permute-done.12.a1, f32[64,256]{1,0:T(8,128)S(1)} %collective-permute-done.13.a2, ...), custom_call_target="tpu_custom_call" | custom-call | tf_op jit(solution)/shard_map/pallas_call | solution.py:37
  47.2 1.1 %collective-permute-start.16 = (f32[16,256]{1,0:T(8,128)S(1)}, f32[16,256]{1,0:T(8,128)S(1)}, u32[]{:S(2)}, u32[]{:S(2)}) collective-permute-start(f32[16,256]{1,0:T(8,128)S(1)} %get-tuple-element.37), channel_id=1, source_target_pairs={{0,128},{64,192},{128,0},{192,64},{1,129},{65,193},{129,1},{193,65... | collective-permute-start | bytes 49160 | tf_op jit(solution)/shard_map/ppermute | solution.py:23
  48.3 2.7 %collective-permute-start.17 = (f32[16,256]{1,0:T(8,128)S(1)}, f32[16,256]{1,0:T(8,128)S(1)}, u32[]{:S(2)}, u32[]{:S(2)}) collective-permute-start(f32[16,256]{1,0:T(8,128)S(1)} %get-tuple-element.38), channel_id=1, source_target_pairs={{0,192},{64,128},{128,64},{192,0},{1,193},{65,129},{129,65},{193,1... | collective-permute-start | bytes 49160 | tf_op jit(solution)/shard_map/ppermute | solution.py:23
  51.1 0.2 collective-permute-done.16
  51.3 0.9 %collective-permute-done.17 = f32[16,256]{1,0:T(8,128)S(1)} collective-permute-done((f32[16,256]{1,0:T(8,128)S(1)}, f32[16,256]{1,0:T(8,128)S(1)}, u32[]{:S(2)}, u32[]{:S(2)}) %collective-permute-start.17) | collective-permute-done | bytes 16416 | tf_op jit(solution)/shard_map/ppermute | solution.py:23
  52.2 3.3 %collective-permute-start.18 = (f32[64,256]{1,0:T(8,128)S(1)}, f32[64,256]{1,0:T(8,128)S(1)}, u32[]{:S(2)}, u32[]{:S(2)}) collective-permute-start(f32[64,256]{1,0:T(8,128)S(1)} %constant_dynamic-update-slice_fusion.mine_ref), channel_id=1, source_target_pairs={{0,1},{1,0},{2,3},{3,2},{4,5},{5,4},{6,7},{7,6},{8,9},{9,8},{10,11... | collective-permute-start | bytes 196616 | tf_op jit(solution)/shard_map/ppermute | solution.py:23
  55.5 5.7 %all-to-all-start = ((f32[16,1,64]{2,1,0:T(1,128)}), f32[16,1,64]{2,1,0:T(1,128)S(1)}, u32[]{:S(2)}, u32[]{:S(2)}) async-start(f32[16,1,64]{2,1,0:T(1,128)} %bitcast.7), calls=%async_computation | async-start | bytes 16384 | tf_op jit(solution)/shard_map/all_to_all | solution.py:293
  61.3 6.9 %all-to-all-done = f32[16,1,64]{2,1,0:T(1,128)S(1)} async-done(((f32[16,1,64]{2,1,0:T(1,128)}), f32[16,1,64]{2,1,0:T(1,128)S(1)}, u32[]{:S(2)}, u32[]{:S(2)}) %all-to-all-start) | async-done | bytes 4128 | tf_op jit(solution)/shard_map/all_to_all | solution.py:293
  68.1 0.7 shard_map.102
  (30 shorter events, 0.6 us)
Async XLA Ops:
  0.6 26.9 %copy-start.2 = (s32[16]{0:T(128)S(1)}, s32[16]{0:T(128)}, u32[]{:S(2)}) copy-start(s32[16]{0:T(128)} %param.13) | copy-start | bytes 196
  0.6 27.9 %copy-start.1 = (s32[1,1024]{1,0:T(1,128)S(1)}, s32[1,1024]{1,0:T(1,128)}, u32[]{:S(2)}) copy-start(s32[1,1024]{1,0:T(1,128)} %where_ref.1) | copy-start | bytes 12292
  0.7 60.5 %copy-start = (s32[2048]{0:T(1024)S(1)}, s32[2048]{0:T(1024)}, u32[]{:S(2)}) copy-start(s32[2048]{0:T(1024)} %param.14) | copy-start | bytes 24580
  0.7 9.7 %collective-permute-start.8 = (bf16[1,64,512]{2,1,0:T(8,128)(2,1)}, bf16[1,64,512]{2,1,0:T(8,128)(2,1)S(1)}, u32[]{:S(2)}, u32[]{:S(2)}) collective-permute-start(bf16[1,64,512]{2,1,0:T(8,128)(2,1)} %bitcast.16), channel_id=1, source_target_pairs={{0,16},{8,24},{16,0},{24,8},{32,48},{40,56},{48,32},{56,40},{1,17}... | collective-permute-start | bytes 196616 | tf_op jit(solution)/shard_map/ppermute | solution.py:23
  9.3 6.3 %collective-permute-start = (f32[64,1024]{1,0:T(8,128)S(1)}, f32[64,1024]{1,0:T(8,128)S(1)}, u32[]{:S(2)}, u32[]{:S(2)}) collective-permute-start(f32[64,1024]{1,0:T(8,128)S(1)} %get-tuple-element.23), channel_id=1, source_target_pairs={{0,1},{1,0},{2,3},{3,2},{4,5},{5,4},{6,7},{7,6},{8,9},{9,8},{10,11... | collective-permute-start | bytes 786440 | tf_op jit(solution)/shard_map/ppermute | solution.py:23
  10.4 9.3 %collective-permute-start.9 = (bf16[2,64,512]{2,1,0:T(8,128)(2,1)S(1)}, bf16[2,64,512]{2,1,0:T(8,128)(2,1)S(1)}, u32[]{:S(2)}, u32[]{:S(2)}) collective-permute-start(bf16[2,64,512]{2,1,0:T(8,128)(2,1)S(1)} %pad_maximum_fusion.refs_0_), channel_id=1, source_target_pairs={{0,32},{8,40},{16,48},{24,56},{32,0},{40,8},{48,16},{56,24},{1,33}... | collective-permute-start | bytes 393224 | tf_op jit(solution)/shard_map/ppermute | solution.py:23
  15.7 8.4 %collective-permute-start.1 = (s16[48,1024]{1,0:T(8,128)(2,1)S(1)}, s16[48,1024]{1,0:T(8,128)(2,1)S(1)}, u32[]{:S(2)}, u32[]{:S(2)}) collective-permute-start(s16[48,1024]{1,0:T(8,128)(2,1)S(1)} %get-tuple-element.26), channel_id=1, source_target_pairs={{0,2},{2,0},{4,6},{6,4},{1,3},{3,1},{5,7},{7,5},{8,10},{10,8},{12,... | collective-permute-start | bytes 294920 | tf_op jit(solution)/shard_map/ppermute | solution.py:23
  17.0 7.2 %collective-permute-start.2 = (s16[48,1024]{1,0:T(8,128)(2,1)S(1)}, s16[48,1024]{1,0:T(8,128)(2,1)S(1)}, u32[]{:S(2)}, u32[]{:S(2)}) collective-permute-start(s16[48,1024]{1,0:T(8,128)(2,1)S(1)} %get-tuple-element.27), channel_id=1, source_target_pairs={{0,4},{2,6},{4,0},{6,2},{1,5},{3,7},{5,1},{7,3},{8,12},{10,14},{12... | collective-permute-start | bytes 294920 | tf_op jit(solution)/shard_map/ppermute | solution.py:23
  19.5 7.3 %collective-permute-start.3 = (s16[48,1024]{1,0:T(8,128)(2,1)S(1)}, s16[48,1024]{1,0:T(8,128)(2,1)S(1)}, u32[]{:S(2)}, u32[]{:S(2)}) collective-permute-start(s16[48,1024]{1,0:T(8,128)(2,1)S(1)} %get-tuple-element.28), channel_id=1, source_target_pairs={{0,6},{2,4},{4,2},{6,0},{1,7},{3,5},{5,3},{7,1},{8,14},{10,12},{12... | collective-permute-start | bytes 294920 | tf_op jit(solution)/shard_map/ppermute | solution.py:23
  19.7 17.1 %collective-permute-start.10 = (bf16[4,64,512]{2,1,0:T(8,128)(2,1)S(1)}, bf16[4,64,512]{2,1,0:T(8,128)(2,1)S(1)}, u32[]{:S(2)}, u32[]{:S(2)}) collective-permute-start(bf16[4,64,512]{2,1,0:T(8,128)(2,1)S(1)} %shard_map.99.first_ref), channel_id=1, source_target_pairs={{0,8},{8,0},{16,24},{24,16},{32,40},{40,32},{48,56},{56,48},{1,9},... | collective-permute-start | bytes 786440 | tf_op jit(solution)/shard_map/ppermute | solution.py:23
  26.9 1.6 %collective-permute-start.4 = (f32[32,1024]{1,0:T(8,128)S(1)}, f32[32,1024]{1,0:T(8,128)S(1)}, u32[]{:S(2)}, u32[]{:S(2)}) collective-permute-start(f32[32,1024]{1,0:T(8,128)S(1)} %get-tuple-element.30.mine_ref), channel_id=1, source_target_pairs={{0,1},{1,0},{2,3},{3,2},{4,5},{5,4},{6,7},{7,6},{8,9},{9,8},{10,11... | collective-permute-start | bytes 393224 | tf_op jit(solution)/shard_map/ppermute | solution.py:23
  29.0 4.0 %collective-permute-start.5 = (bf16[16,640]{1,0:T(8,128)(2,1)S(1)}, bf16[16,640]{1,0:T(8,128)(2,1)S(1)}, u32[]{:S(2)}, u32[]{:S(2)}) collective-permute-start(bf16[16,640]{1,0:T(8,128)(2,1)S(1)} %shard_map.98.p0), channel_id=1, source_target_pairs={{0,64},{64,0},{128,192},{192,128},{1,65},{65,1},{129,193},{193,129... | collective-permute-start | bytes 61448 | tf_op jit(solution)/shard_map/ppermute | solution.py:23
  30.3 4.1 %collective-permute-start.6 = (bf16[16,640]{1,0:T(8,128)(2,1)S(1)}, bf16[16,640]{1,0:T(8,128)(2,1)S(1)}, u32[]{:S(2)}, u32[]{:S(2)}) collective-permute-start(bf16[16,640]{1,0:T(8,128)(2,1)S(1)} %shard_map.98.p0), channel_id=1, source_target_pairs={{0,128},{64,192},{128,0},{192,64},{1,129},{65,193},{129,1},{193,65... | collective-permute-start | bytes 61448 | tf_op jit(solution)/shard_map/ppermute | solution.py:23
  32.9 3.8 %collective-permute-start.7 = (bf16[16,640]{1,0:T(8,128)(2,1)S(1)}, bf16[16,640]{1,0:T(8,128)(2,1)S(1)}, u32[]{:S(2)}, u32[]{:S(2)}) collective-permute-start(bf16[16,640]{1,0:T(8,128)(2,1)S(1)} %shard_map.98.p0), channel_id=1, source_target_pairs={{0,192},{64,128},{128,64},{192,0},{1,193},{65,129},{129,65},{193,1... | collective-permute-start | bytes 61448 | tf_op jit(solution)/shard_map/ppermute | solution.py:23
  37.1 3.1 %collective-permute-start.11 = (f32[64,256]{1,0:T(8,128)S(1)}, f32[64,256]{1,0:T(8,128)S(1)}, u32[]{:S(2)}, u32[]{:S(2)}) collective-permute-start(f32[64,256]{1,0:T(8,128)S(1)} %get-tuple-element.33), channel_id=1, source_target_pairs={{0,1},{1,0},{2,3},{3,2},{4,5},{5,4},{6,7},{7,6},{8,9},{9,8},{10,11... | collective-permute-start | bytes 196616 | tf_op jit(solution)/shard_map/ppermute | solution.py:23
  40.2 3.9 %collective-permute-start.12 = (f32[64,256]{1,0:T(8,128)S(1)}, f32[64,256]{1,0:T(8,128)S(1)}, u32[]{:S(2)}, u32[]{:S(2)}) collective-permute-start(f32[64,256]{1,0:T(8,128)S(1)} %add.3.a0), channel_id=1, source_target_pairs={{0,2},{2,0},{4,6},{6,4},{1,3},{3,1},{5,7},{7,5},{8,10},{10,8},{12,... | collective-permute-start | bytes 196616 | tf_op jit(solution)/shard_map/ppermute | solution.py:23
  40.3 4.7 %collective-permute-start.13 = (f32[64,256]{1,0:T(8,128)S(1)}, f32[64,256]{1,0:T(8,128)S(1)}, u32[]{:S(2)}, u32[]{:S(2)}) collective-permute-start(f32[64,256]{1,0:T(8,128)S(1)} %add.3.a0), channel_id=1, source_target_pairs={{0,4},{2,6},{4,0},{6,2},{1,5},{3,7},{5,1},{7,3},{8,12},{10,14},{12... | collective-permute-start | bytes 196616 | tf_op jit(solution)/shard_map/ppermute | solution.py:23
  41.8 4.7 %collective-permute-start.14 = (f32[64,256]{1,0:T(8,128)S(1)}, f32[64,256]{1,0:T(8,128)S(1)}, u32[]{:S(2)}, u32[]{:S(2)}) collective-permute-start(f32[64,256]{1,0:T(8,128)S(1)} %add.3.a0), channel_id=1, source_target_pairs={{0,6},{2,4},{4,2},{6,0},{1,7},{3,5},{5,3},{7,1},{8,14},{10,12},{12... | collective-permute-start | bytes 196616 | tf_op jit(solution)/shard_map/ppermute | solution.py:23
  47.2 3.9 %collective-permute-start.15 = (f32[16,256]{1,0:T(8,128)S(1)}, f32[16,256]{1,0:T(8,128)S(1)}, u32[]{:S(2)}, u32[]{:S(2)}) collective-permute-start(f32[16,256]{1,0:T(8,128)S(1)} %get-tuple-element.36), channel_id=1, source_target_pairs={{0,64},{64,0},{128,192},{192,128},{1,65},{65,1},{129,193},{193,129... | collective-permute-start | bytes 49160 | tf_op jit(solution)/shard_map/ppermute | solution.py:23
  47.2 4.1 %collective-permute-start.16 = (f32[16,256]{1,0:T(8,128)S(1)}, f32[16,256]{1,0:T(8,128)S(1)}, u32[]{:S(2)}, u32[]{:S(2)}) collective-permute-start(f32[16,256]{1,0:T(8,128)S(1)} %get-tuple-element.37), channel_id=1, source_target_pairs={{0,128},{64,192},{128,0},{192,64},{1,129},{65,193},{129,1},{193,65... | collective-permute-start | bytes 49160 | tf_op jit(solution)/shard_map/ppermute | solution.py:23
  48.3 3.9 %collective-permute-start.17 = (f32[16,256]{1,0:T(8,128)S(1)}, f32[16,256]{1,0:T(8,128)S(1)}, u32[]{:S(2)}, u32[]{:S(2)}) collective-permute-start(f32[16,256]{1,0:T(8,128)S(1)} %get-tuple-element.38), channel_id=1, source_target_pairs={{0,192},{64,128},{128,64},{192,0},{1,193},{65,129},{129,65},{193,1... | collective-permute-start | bytes 49160 | tf_op jit(solution)/shard_map/ppermute | solution.py:23
  52.2 15.9 %collective-permute-start.18 = (f32[64,256]{1,0:T(8,128)S(1)}, f32[64,256]{1,0:T(8,128)S(1)}, u32[]{:S(2)}, u32[]{:S(2)}) collective-permute-start(f32[64,256]{1,0:T(8,128)S(1)} %constant_dynamic-update-slice_fusion.mine_ref), channel_id=1, source_target_pairs={{0,1},{1,0},{2,3},{3,2},{4,5},{5,4},{6,7},{7,6},{8,9},{9,8},{10,11... | collective-permute-start | bytes 196616 | tf_op jit(solution)/shard_map/ppermute | solution.py:23
  55.5 12.6 %all-to-all-start = ((f32[16,1,64]{2,1,0:T(1,128)}), f32[16,1,64]{2,1,0:T(1,128)S(1)}, u32[]{:S(2)}, u32[]{:S(2)}) async-start(f32[16,1,64]{2,1,0:T(1,128)} %bitcast.7), calls=%async_computation | async-start | bytes 16384 | tf_op jit(solution)/shard_map/all_to_all | solution.py:293

commit v6 on v5

--- a/solution.py
+++ b/solution.py
@@ -174,7 +174,7 @@
 
 def score_body(p0, p1, p2, p3, first_ref, second_ref, keep_ref, send_ref, goal_ref, held):
     core, z = lax.axis_index("core"), lax.axis_index("z")
-    for m, bits in enumerate((0, 2, 4, 6, 1, 3, 5, 7)):
+    for m, bits in enumerate((0, 7, 2, 5, 1, 6, 3, 4)):
         at = pl.ds(pl.multiple_of((z ^ bits) * C_DEV, C_DEV), C_DEV)
         held[at, :] = (first_ref, second_ref)[m // (NZ // 2)][m % (NZ // 2)]
     ps = [p[...] for p in (p0, p1, p2, p3)]
@@ -187,11 +187,15 @@
     goal_ref[...] = jnp.broadcast_to(goal[:, :1] * 16.0 + goal[:, 64:65], (E_ALL, 128))
 
 
-def total_body(a0, a1, a2, a3, goal_ref, s0, s1, s2, s3, slots_ref):
-    core, y = lax.axis_index("core"), lax.axis_index("y")
+def sum_body(a0, a1, a2, a3, s0, s1, s2, s3):
     score = (a0[...] + a1[...]) + (a2[...] + a3[...])
     for d, ref in enumerate((s0, s1, s2, s3)):
         ref[...] = score[d * E_DEV : (d + 1) * E_DEV]
+
+
+def total_body(s0, s1, s2, s3, goal_ref, slots_ref):
+    core, y = lax.axis_index("core"), lax.axis_index("y")
+    score = jnp.concatenate([s[...] for s in (s0, s1, s2, s3)], 0)
     first = ((y * NC + core) * C_HALF).astype(F32)
     goal = goal_ref[...] - first
     lane = lax.broadcasted_iota(I32, (E_ALL, 128), 1).astype(F32)
@@ -225,7 +229,7 @@
     kept_choice_flags,
     token_sample_position,
 ):
-    far = swap(heldout_slope_entries[None], "z", 2)
+    far = swap(heldout_slope_entries[None], "z", 7)
     keep, away, held = project(
         down_matrix_feeds,
         result_slope_matrix,
@@ -234,7 +238,7 @@
         heldout_slope_entries,
     )
     held = jnp.concatenate([held[None], far], 0)
-    far = swap(held, "z", 4)
+    far = swap(held, "z", 2)
 
     sent = shaped(2 * ROWS + HALF, TOK, dtype=I16)
     low, half = shaped(ROWS, TOK), shaped(HALF, TOK)
@@ -253,7 +257,7 @@
         swap(out_half, "core", 1),
         token_sample_position,
         objective_of_sample[:, None],
-        work=400_000_000,
+        work=400000000,
     )
     packs = {d: swap(packed, "y", d) for d in (2, 1, 3)}
 
@@ -272,17 +276,11 @@
     score = keep + swap(send, "core", 1)
     got = {d: swap(score, "x", d) for d in (2, 1, 3)}
     piece = shaped(E_DEV, C_HALF)
-    *pieces, slots = call(
-        total_body,
-        [piece] * NY + [shaped(NZ * NC, C_DEV)],
-        score,
-        got[1],
-        got[2],
-        got[3],
-        goal,
-    )
+    pieces = call(sum_body, [piece] * NY, score, got[1], got[2], got[3])
+    slots = call(total_body, shaped(NZ * NC, C_DEV), *pieces, goal)
     got = {d: swap(pieces[d], "y", d) for d in (2, 1, 3)}
     mine = jnp.concatenate([pieces[0], got[1], got[2], got[3]], 0)
+    mine, slots = lax.optimization_barrier((mine, slots))
     sample_affinity, totals = call(
         lay_body,
         [shaped(E_DEV, CHOICES), shaped(1, C_DEV)],

time: 68.9 us -> 65.6 us (0.952)
  starting transfers between devices: 42.1 us -> 35.1 us
  waiting for transfers between devices: 18.6 us -> 22.3 us
    ppermute x19, starting transfers between devices: 36.4 us -> 31.7 us  [swap(): lax.ppermute(value, axis, [(i, i ^ bits) for i in range(SIZES[axis])])]
    ppermute x19, waiting for transfers between devices: 11.8 us -> 15.4 us  [swap(): lax.ppermute(value, axis, [(i, i ^ bits) for i in range(SIZES[axis])])]
    all_to_all x1, starting transfers between devices: 5.69 us -> 3.43 us  [per_device(): lax.all_to_all(slots, ('z', 'core'), 0, 0, tiled=True)]
    pallas_call x7 -> x8, Pallas kernels: 2.38 us -> 2.39 us  [call(): pl.pallas_call(run, out_shape=outs, in_specs=specs, scratch_shapes=scratc...]
  transfers between devices with their start and end apart: 20 -> 20, of which waited for: 10 -> 11; matrix products, arithmetic and copies ran while one was open for 0% -> 0% of each run, Pallas kernels for 8% -> 9%
where the time goes in v6:
time: 65.6 us; the launch traced here: 65.5 us
  starting transfers between devices  35.1 us (54%)
  waiting for transfers between devices  22.3 us (34%)
  Pallas kernels  7.16 us (11%)
  between operations  0.73 us (1%)
    ppermute x19, starting transfers between devices, swap(): lax.ppermute(value, axis, [(i, i ^ bits) for i in range(SIZES[axis])])  31.7 us
    ppermute x19, waiting for transfers between devices, swap(): lax.ppermute(value, axis, [(i, i ^ bits) for i in range(SIZES[axis])])  15.4 us
    all_to_all x1, waiting for transfers between devices, per_device(): lax.all_to_all(slots, ('z', 'core'), 0, 0, tiled=True)  6.87 us
    pallas_call x1, Pallas kernels, project(): pl.pallas_call(project_body, in_specs=[pl.BlockSpec(memory_space=pltpu.HB...  4.77 us
    all_to_all x1, starting transfers between devices, per_device(): lax.all_to_all(slots, ('z', 'core'), 0, 0, tiled=True)  3.43 us
    pallas_call x8, Pallas kernels, call(): pl.pallas_call(run, out_shape=outs, in_specs=specs, scratch_shapes=scratc...  2.39 us
  transfers between devices with their start and end apart: 20, of which 11 were waited for; matrix products, arithmetic and copies ran while one was open for 0% of the time, Pallas kernels for 9%

profile of v6, /device:TPU:1, one launch (start us, length us, event | category | flops | bytes accessed | tf_op | source)
XLA Modules:
  0.0 65.5 jit_solution(7780292821853233707)
XLA Ops:
  0.7 6.5 %collective-permute-start.8 = (bf16[1,64,512]{2,1,0:T(8,128)(2,1)}, bf16[1,64,512]{2,1,0:T(8,128)(2,1)S(1)}, u32[]{:S(2)}, u32[]{:S(2)}) collective-permute-start(bf16[1,64,512]{2,1,0:T(8,128)(2,1)} %bitcast.16), channel_id=1, source_target_pairs={{0,56},{8,48},{16,40},{24,32},{32,24},{40,16},{48,8},{56,0},{1,57}... | collective-permute-start | bytes 196616 | tf_op jit(solution)/shard_map/ppermute | solution.py:23
  7.1 4.8 %shard_map.95 = (f32[64,1024]{1,0:T(8,128)S(1)}, f32[64,1024]{1,0:T(8,128)S(1)}, bf16[64,512]{1,0:T(8,128)(2,1)S(1)}) custom-call(bf16[1024,3584]{1,0:T(8,128)(2,1)} %x_hbm.1, bf16[1024,1024]{1,0:T(8,128)(2,1)} %y_hbm.1, bf16[64,3584]{1,0:T(8,128)(2,1)} %bitcast.14, bf16[64,1024]{1,0:T(8,128)(2,1)} %bitcast.15, bf16[64,512]{1,0:T(8,128)(2,1)} %h_hbm.1), custom_call_target="tpu_custom_call" | custom-call | flops 603979776 | bytes 9437184 | tf_op jit(solution)/shard_map/pallas_call | solution.py:95
  11.9 1.0 %collective-permute-start = (f32[64,1024]{1,0:T(8,128)S(1)}, f32[64,1024]{1,0:T(8,128)S(1)}, u32[]{:S(2)}, u32[]{:S(2)}) collective-permute-start(f32[64,1024]{1,0:T(8,128)S(1)} %get-tuple-element.24), channel_id=1, source_target_pairs={{0,1},{1,0},{2,3},{3,2},{4,5},{5,4},{6,7},{7,6},{8,9},{9,8},{10,11... | collective-permute-start | bytes 786440 | tf_op jit(solution)/shard_map/ppermute | solution.py:23
  13.0 2.2 %collective-permute-start.9 = (bf16[2,64,512]{2,1,0:T(8,128)(2,1)S(1)}, bf16[2,64,512]{2,1,0:T(8,128)(2,1)S(1)}, u32[]{:S(2)}, u32[]{:S(2)}) collective-permute-start(bf16[2,64,512]{2,1,0:T(8,128)(2,1)S(1)} %pad_maximum_fusion.refs_0_), channel_id=1, source_target_pairs={{0,16},{8,24},{16,0},{24,8},{32,48},{40,56},{48,32},{56,40},{1,17}... | collective-permute-start | bytes 393224 | tf_op jit(solution)/shard_map/ppermute | solution.py:23
  15.3 1.3 %collective-permute-start.1 = (s16[48,1024]{1,0:T(8,128)(2,1)S(1)}, s16[48,1024]{1,0:T(8,128)(2,1)S(1)}, u32[]{:S(2)}, u32[]{:S(2)}) collective-permute-start(s16[48,1024]{1,0:T(8,128)(2,1)S(1)} %get-tuple-element.27), channel_id=1, source_target_pairs={{0,2},{2,0},{4,6},{6,4},{1,3},{3,1},{5,7},{7,5},{8,10},{10,8},{12,... | collective-permute-start | bytes 294920 | tf_op jit(solution)/shard_map/ppermute | solution.py:23
  16.6 2.4 %collective-permute-start.2 = (s16[48,1024]{1,0:T(8,128)(2,1)S(1)}, s16[48,1024]{1,0:T(8,128)(2,1)S(1)}, u32[]{:S(2)}, u32[]{:S(2)}) collective-permute-start(s16[48,1024]{1,0:T(8,128)(2,1)S(1)} %get-tuple-element.28), channel_id=1, source_target_pairs={{0,4},{2,6},{4,0},{6,2},{1,5},{3,7},{5,1},{7,3},{8,12},{10,14},{12... | collective-permute-start | bytes 294920 | tf_op jit(solution)/shard_map/ppermute | solution.py:23
  19.0 0.2 collective-permute-start.3
  19.2 2.7 %collective-permute-done.9.refs_1_ = bf16[2,64,512]{2,1,0:T(8,128)(2,1)S(1)} collective-permute-done((bf16[2,64,512]{2,1,0:T(8,128)(2,1)S(1)}, bf16[2,64,512]{2,1,0:T(8,128)(2,1)S(1)}, u32[]{:S(2)}, u32[]{:S(2)}) %collective-permute-start.9) | collective-permute-done | bytes 131104 | tf_op jit(solution)/shard_map/ppermute | solution.py:23
  22.0 1.7 %collective-permute-done.2.g2_ref = s16[48,1024]{1,0:T(8,128)(2,1)S(1)} collective-permute-done((s16[48,1024]{1,0:T(8,128)(2,1)S(1)}, s16[48,1024]{1,0:T(8,128)(2,1)S(1)}, u32[]{:S(2)}, u32[]{:S(2)}) %collective-permute-start.2) | collective-permute-done | bytes 98336 | tf_op jit(solution)/shard_map/ppermute | solution.py:23
  23.8 2.6 %collective-permute-done.3.g3_ref = s16[48,1024]{1,0:T(8,128)(2,1)S(1)} collective-permute-done((s16[48,1024]{1,0:T(8,128)(2,1)S(1)}, s16[48,1024]{1,0:T(8,128)(2,1)S(1)}, u32[]{:S(2)}, u32[]{:S(2)}) %collective-permute-start.3) | collective-permute-done | bytes 98336 | tf_op jit(solution)/shard_map/ppermute | solution.py:23
  26.4 0.7 %collective-permute-start.4 = (f32[32,1024]{1,0:T(8,128)S(1)}, f32[32,1024]{1,0:T(8,128)S(1)}, u32[]{:S(2)}, u32[]{:S(2)}) collective-permute-start(f32[32,1024]{1,0:T(8,128)S(1)} %get-tuple-element.31.mine_ref), channel_id=1, source_target_pairs={{0,1},{1,0},{2,3},{3,2},{4,5},{5,4},{6,7},{7,6},{8,9},{9,8},{10,11... | collective-permute-start | bytes 393224 | tf_op jit(solution)/shard_map/ppermute | solution.py:23
  27.2 0.9 %collective-permute-done.4.other_ref = f32[32,1024]{1,0:T(8,128)S(1)} collective-permute-done((f32[32,1024]{1,0:T(8,128)S(1)}, f32[32,1024]{1,0:T(8,128)S(1)}, u32[]{:S(2)}, u32[]{:S(2)}) %collective-permute-start.4) | collective-permute-done | bytes 131104 | tf_op jit(solution)/shard_map/ppermute | solution.py:23
  28.1 0.4 shard_map.98.p0
  28.5 1.3 %collective-permute-start.5 = (bf16[16,640]{1,0:T(8,128)(2,1)S(1)}, bf16[16,640]{1,0:T(8,128)(2,1)S(1)}, u32[]{:S(2)}, u32[]{:S(2)}) collective-permute-start(bf16[16,640]{1,0:T(8,128)(2,1)S(1)} %shard_map.98.p0), channel_id=1, source_target_pairs={{0,64},{64,0},{128,192},{192,128},{1,65},{65,1},{129,193},{193,129... | collective-permute-start | bytes 61448 | tf_op jit(solution)/shard_map/ppermute | solution.py:23
  29.9 2.6 %collective-permute-start.6 = (bf16[16,640]{1,0:T(8,128)(2,1)S(1)}, bf16[16,640]{1,0:T(8,128)(2,1)S(1)}, u32[]{:S(2)}, u32[]{:S(2)}) collective-permute-start(bf16[16,640]{1,0:T(8,128)(2,1)S(1)} %shard_map.98.p0), channel_id=1, source_target_pairs={{0,128},{64,192},{128,0},{192,64},{1,129},{65,193},{129,1},{193,65... | collective-permute-start | bytes 61448 | tf_op jit(solution)/shard_map/ppermute | solution.py:23
  32.5 1.5 %collective-permute-done.6.p2 = bf16[16,640]{1,0:T(8,128)(2,1)S(1)} collective-permute-done((bf16[16,640]{1,0:T(8,128)(2,1)S(1)}, bf16[16,640]{1,0:T(8,128)(2,1)S(1)}, u32[]{:S(2)}, u32[]{:S(2)}) %collective-permute-start.6) | collective-permute-done | bytes 20512 | tf_op jit(solution)/shard_map/ppermute | solution.py:23
  34.0 2.3 %collective-permute-done.7.p3 = bf16[16,640]{1,0:T(8,128)(2,1)S(1)} collective-permute-done((bf16[16,640]{1,0:T(8,128)(2,1)S(1)}, bf16[16,640]{1,0:T(8,128)(2,1)S(1)}, u32[]{:S(2)}, u32[]{:S(2)}) %collective-permute-start.7) | collective-permute-done | bytes 20512 | tf_op jit(solution)/shard_map/ppermute | solution.py:23
  36.3 0.3 shard_map.100
  36.7 2.2 %collective-permute-start.11 = (f32[64,256]{1,0:T(8,128)S(1)}, f32[64,256]{1,0:T(8,128)S(1)}, u32[]{:S(2)}, u32[]{:S(2)}) collective-permute-start(f32[64,256]{1,0:T(8,128)S(1)} %get-tuple-element.34), channel_id=1, source_target_pairs={{0,1},{1,0},{2,3},{3,2},{4,5},{5,4},{6,7},{7,6},{8,9},{9,8},{10,11... | collective-permute-start | bytes 196616 | tf_op jit(solution)/shard_map/ppermute | solution.py:23
  38.8 0.9 %collective-permute-done.11 = f32[64,256]{1,0:T(8,128)S(1)} collective-permute-done((f32[64,256]{1,0:T(8,128)S(1)}, f32[64,256]{1,0:T(8,128)S(1)}, u32[]{:S(2)}, u32[]{:S(2)}) %collective-permute-start.11) | collective-permute-done | bytes 65568 | tf_op jit(solution)/shard_map/ppermute | solution.py:23
  39.8 1.5 %collective-permute-start.13 = (f32[64,256]{1,0:T(8,128)S(1)}, f32[64,256]{1,0:T(8,128)S(1)}, u32[]{:S(2)}, u32[]{:S(2)}) collective-permute-start(f32[64,256]{1,0:T(8,128)S(1)} %add.3.a0), channel_id=1, source_target_pairs={{0,4},{2,6},{4,0},{6,2},{1,5},{3,7},{5,1},{7,3},{8,12},{10,14},{12... | collective-permute-start | bytes 196616 | tf_op jit(solution)/shard_map/ppermute | solution.py:23
  41.3 2.4 %collective-permute-start.14 = (f32[64,256]{1,0:T(8,128)S(1)}, f32[64,256]{1,0:T(8,128)S(1)}, u32[]{:S(2)}, u32[]{:S(2)}) collective-permute-start(f32[64,256]{1,0:T(8,128)S(1)} %add.3.a0), channel_id=1, source_target_pairs={{0,6},{2,4},{4,2},{6,0},{1,7},{3,5},{5,3},{7,1},{8,14},{10,12},{12... | collective-permute-start | bytes 196616 | tf_op jit(solution)/shard_map/ppermute | solution.py:23
  43.7 0.9 %collective-permute-done.13.a2 = f32[64,256]{1,0:T(8,128)S(1)} collective-permute-done((f32[64,256]{1,0:T(8,128)S(1)}, f32[64,256]{1,0:T(8,128)S(1)}, u32[]{:S(2)}, u32[]{:S(2)}) %collective-permute-start.13) | collective-permute-done | bytes 65568 | tf_op jit(solution)/shard_map/ppermute | solution.py:23
  44.5 1.5 %collective-permute-done.14.a3 = f32[64,256]{1,0:T(8,128)S(1)} collective-permute-done((f32[64,256]{1,0:T(8,128)S(1)}, f32[64,256]{1,0:T(8,128)S(1)}, u32[]{:S(2)}, u32[]{:S(2)}) %collective-permute-start.14) | collective-permute-done | bytes 65568 | tf_op jit(solution)/shard_map/ppermute | solution.py:23
  46.2 1.1 %collective-permute-start.16 = (f32[16,256]{1,0:T(8,128)S(1)}, f32[16,256]{1,0:T(8,128)S(1)}, u32[]{:S(2)}, u32[]{:S(2)}) collective-permute-start(f32[16,256]{1,0:T(8,128)S(1)} %get-tuple-element.37.s2), channel_id=1, source_target_pairs={{0,128},{64,192},{128,0},{192,64},{1,129},{65,193},{129,1},{193,65... | collective-permute-start | bytes 49160 | tf_op jit(solution)/shard_map/ppermute | solution.py:23
  47.3 2.7 %collective-permute-start.17 = (f32[16,256]{1,0:T(8,128)S(1)}, f32[16,256]{1,0:T(8,128)S(1)}, u32[]{:S(2)}, u32[]{:S(2)}) collective-permute-start(f32[16,256]{1,0:T(8,128)S(1)} %get-tuple-element.38.s3), channel_id=1, source_target_pairs={{0,192},{64,128},{128,64},{192,0},{1,193},{65,129},{129,65},{193,1... | collective-permute-start | bytes 49160 | tf_op jit(solution)/shard_map/ppermute | solution.py:23
  50.0 0.7 %shard_map.102 = f32[16,64]{1,0:T(8,128)} custom-call(f32[16,256]{1,0:T(8,128)S(1)} %get-tuple-element.35.s0, f32[16,256]{1,0:T(8,128)S(1)} %get-tuple-element.36.s1, f32[16,256]{1,0:T(8,128)S(1)} %get-tuple-element.37.s2, f32[16,256]{1,0:T(8,128)S(1)} %get-tuple-element.38.s3, f32[64,128]{1,0:T(8,128)S(1)} %get-tuple-element.39.goal_ref), custom_call_target="tpu_custom_call" | custom-call | tf_op jit(solution)/shard_map/pallas_call | solution.py:37
  50.7 0.4 collective-permute-done.17
  51.2 3.3 %collective-permute-start.18 = (f32[64,256]{1,0:T(8,128)S(1)}, f32[64,256]{1,0:T(8,128)S(1)}, u32[]{:S(2)}, u32[]{:S(2)}) collective-permute-start(f32[64,256]{1,0:T(8,128)S(1)} %pad_maximum_fusion.1.mine_ref), channel_id=1, source_target_pairs={{0,1},{1,0},{2,3},{3,2},{4,5},{5,4},{6,7},{7,6},{8,9},{9,8},{10,11... | collective-permute-start | bytes 196616 | tf_op jit(solution)/shard_map/ppermute | solution.py:23
  54.5 3.4 %all-to-all-start = ((f32[16,1,64]{2,1,0:T(1,128)}), f32[16,1,64]{2,1,0:T(1,128)S(1)}, u32[]{:S(2)}, u32[]{:S(2)}) async-start(f32[16,1,64]{2,1,0:T(1,128)} %bitcast.7), calls=%async_computation | async-start | bytes 16384 | tf_op jit(solution)/shard_map/all_to_all | solution.py:291
  58.0 6.9 %all-to-all-done = f32[16,1,64]{2,1,0:T(1,128)S(1)} async-done(((f32[16,1,64]{2,1,0:T(1,128)}), f32[16,1,64]{2,1,0:T(1,128)S(1)}, u32[]{:S(2)}, u32[]{:S(2)}) %all-to-all-start) | async-done | bytes 4128 | tf_op jit(solution)/shard_map/all_to_all | solution.py:291
  64.8 0.7 %shard_map.103 = (f32[16,2048]{1,0:T(8,128)}, f32[1,64]{1,0:T(1,128)}) custom-call(f32[64,256]{1,0:T(8,128)S(1)} %pad_maximum_fusion.1.mine_ref, f32[64,256]{1,0:T(8,128)S(1)} %collective-permute-done.18.other_ref, s32[1,2048]{1,0:T(1,128)S(1)} %bitcast.12, s32[32,64]{1,0:T(8,128)S(1)} %reshape.13.own_flag_ref, f32[16,64]{1,0:T(8,128)S(1)} %bitcast.13), custom_call_target="tpu_custom_call" | custom-call | tf_op jit(solution)/shard_map/pallas_call | solution.py:37
  (28 shorter events, 0.7 us)
Async XLA Ops:
  0.6 26.5 %copy-start.2 = (s32[16]{0:T(128)S(1)}, s32[16]{0:T(128)}, u32[]{:S(2)}) copy-start(s32[16]{0:T(128)} %param.13) | copy-start | bytes 196
  0.6 27.4 %copy-start.1 = (s32[1,1024]{1,0:T(1,128)S(1)}, s32[1,1024]{1,0:T(1,128)}, u32[]{:S(2)}) copy-start(s32[1,1024]{1,0:T(1,128)} %where_ref.1) | copy-start | bytes 12292
  0.7 12.3 %collective-permute-start.8 = (bf16[1,64,512]{2,1,0:T(8,128)(2,1)}, bf16[1,64,512]{2,1,0:T(8,128)(2,1)S(1)}, u32[]{:S(2)}, u32[]{:S(2)}) collective-permute-start(bf16[1,64,512]{2,1,0:T(8,128)(2,1)} %bitcast.16), channel_id=1, source_target_pairs={{0,56},{8,48},{16,40},{24,32},{32,24},{40,16},{48,8},{56,0},{1,57}... | collective-permute-start | bytes 196616 | tf_op jit(solution)/shard_map/ppermute | solution.py:23
  7.1 50.7 %copy-start = (s32[2048]{0:T(1024)S(1)}, s32[2048]{0:T(1024)}, u32[]{:S(2)}) copy-start(s32[2048]{0:T(1024)} %param.14) | copy-start | bytes 24580
  11.9 3.2 %collective-permute-start = (f32[64,1024]{1,0:T(8,128)S(1)}, f32[64,1024]{1,0:T(8,128)S(1)}, u32[]{:S(2)}, u32[]{:S(2)}) collective-permute-start(f32[64,1024]{1,0:T(8,128)S(1)} %get-tuple-element.24), channel_id=1, source_target_pairs={{0,1},{1,0},{2,3},{3,2},{4,5},{5,4},{6,7},{7,6},{8,9},{9,8},{10,11... | collective-permute-start | bytes 786440 | tf_op jit(solution)/shard_map/ppermute | solution.py:23
  13.0 8.9 %collective-permute-start.9 = (bf16[2,64,512]{2,1,0:T(8,128)(2,1)S(1)}, bf16[2,64,512]{2,1,0:T(8,128)(2,1)S(1)}, u32[]{:S(2)}, u32[]{:S(2)}) collective-permute-start(bf16[2,64,512]{2,1,0:T(8,128)(2,1)S(1)} %pad_maximum_fusion.refs_0_), channel_id=1, source_target_pairs={{0,16},{8,24},{16,0},{24,8},{32,48},{40,56},{48,32},{56,40},{1,17}... | collective-permute-start | bytes 393224 | tf_op jit(solution)/shard_map/ppermute | solution.py:23
  15.3 6.7 %collective-permute-start.1 = (s16[48,1024]{1,0:T(8,128)(2,1)S(1)}, s16[48,1024]{1,0:T(8,128)(2,1)S(1)}, u32[]{:S(2)}, u32[]{:S(2)}) collective-permute-start(s16[48,1024]{1,0:T(8,128)(2,1)S(1)} %get-tuple-element.27), channel_id=1, source_target_pairs={{0,2},{2,0},{4,6},{6,4},{1,3},{3,1},{5,7},{7,5},{8,10},{10,8},{12,... | collective-permute-start | bytes 294920 | tf_op jit(solution)/shard_map/ppermute | solution.py:23
  16.6 7.2 %collective-permute-start.2 = (s16[48,1024]{1,0:T(8,128)(2,1)S(1)}, s16[48,1024]{1,0:T(8,128)(2,1)S(1)}, u32[]{:S(2)}, u32[]{:S(2)}) collective-permute-start(s16[48,1024]{1,0:T(8,128)(2,1)S(1)} %get-tuple-element.28), channel_id=1, source_target_pairs={{0,4},{2,6},{4,0},{6,2},{1,5},{3,7},{5,1},{7,3},{8,12},{10,14},{12... | collective-permute-start | bytes 294920 | tf_op jit(solution)/shard_map/ppermute | solution.py:23
  19.0 7.3 %collective-permute-start.3 = (s16[48,1024]{1,0:T(8,128)(2,1)S(1)}, s16[48,1024]{1,0:T(8,128)(2,1)S(1)}, u32[]{:S(2)}, u32[]{:S(2)}) collective-permute-start(s16[48,1024]{1,0:T(8,128)(2,1)S(1)} %get-tuple-element.29), channel_id=1, source_target_pairs={{0,6},{2,4},{4,2},{6,0},{1,7},{3,5},{5,3},{7,1},{8,14},{10,12},{12... | collective-permute-start | bytes 294920 | tf_op jit(solution)/shard_map/ppermute | solution.py:23
  21.9 14.4 %collective-permute-start.10 = (bf16[4,64,512]{2,1,0:T(8,128)(2,1)S(1)}, bf16[4,64,512]{2,1,0:T(8,128)(2,1)S(1)}, u32[]{:S(2)}, u32[]{:S(2)}) collective-permute-start(bf16[4,64,512]{2,1,0:T(8,128)(2,1)S(1)} %shard_map.99.first_ref), channel_id=1, source_target_pairs={{0,8},{8,0},{16,24},{24,16},{32,40},{40,32},{48,56},{56,48},{1,9},... | collective-permute-start | bytes 786440 | tf_op jit(solution)/shard_map/ppermute | solution.py:23
  26.4 1.6 %collective-permute-start.4 = (f32[32,1024]{1,0:T(8,128)S(1)}, f32[32,1024]{1,0:T(8,128)S(1)}, u32[]{:S(2)}, u32[]{:S(2)}) collective-permute-start(f32[32,1024]{1,0:T(8,128)S(1)} %get-tuple-element.31.mine_ref), channel_id=1, source_target_pairs={{0,1},{1,0},{2,3},{3,2},{4,5},{5,4},{6,7},{7,6},{8,9},{9,8},{10,11... | collective-permute-start | bytes 393224 | tf_op jit(solution)/shard_map/ppermute | solution.py:23
  28.5 4.0 %collective-permute-start.5 = (bf16[16,640]{1,0:T(8,128)(2,1)S(1)}, bf16[16,640]{1,0:T(8,128)(2,1)S(1)}, u32[]{:S(2)}, u32[]{:S(2)}) collective-permute-start(bf16[16,640]{1,0:T(8,128)(2,1)S(1)} %shard_map.98.p0), channel_id=1, source_target_pairs={{0,64},{64,0},{128,192},{192,128},{1,65},{65,1},{129,193},{193,129... | collective-permute-start | bytes 61448 | tf_op jit(solution)/shard_map/ppermute | solution.py:23
  29.9 4.1 %collective-permute-start.6 = (bf16[16,640]{1,0:T(8,128)(2,1)S(1)}, bf16[16,640]{1,0:T(8,128)(2,1)S(1)}, u32[]{:S(2)}, u32[]{:S(2)}) collective-permute-start(bf16[16,640]{1,0:T(8,128)(2,1)S(1)} %shard_map.98.p0), channel_id=1, source_target_pairs={{0,128},{64,192},{128,0},{192,64},{1,129},{65,193},{129,1},{193,65... | collective-permute-start | bytes 61448 | tf_op jit(solution)/shard_map/ppermute | solution.py:23
  32.5 3.8 %collective-permute-start.7 = (bf16[16,640]{1,0:T(8,128)(2,1)S(1)}, bf16[16,640]{1,0:T(8,128)(2,1)S(1)}, u32[]{:S(2)}, u32[]{:S(2)}) collective-permute-start(bf16[16,640]{1,0:T(8,128)(2,1)S(1)} %shard_map.98.p0), channel_id=1, source_target_pairs={{0,192},{64,128},{128,64},{192,0},{1,193},{65,129},{129,65},{193,1... | collective-permute-start | bytes 61448 | tf_op jit(solution)/shard_map/ppermute | solution.py:23
  36.7 3.1 %collective-permute-start.11 = (f32[64,256]{1,0:T(8,128)S(1)}, f32[64,256]{1,0:T(8,128)S(1)}, u32[]{:S(2)}, u32[]{:S(2)}) collective-permute-start(f32[64,256]{1,0:T(8,128)S(1)} %get-tuple-element.34), channel_id=1, source_target_pairs={{0,1},{1,0},{2,3},{3,2},{4,5},{5,4},{6,7},{7,6},{8,9},{9,8},{10,11... | collective-permute-start | bytes 196616 | tf_op jit(solution)/shard_map/ppermute | solution.py:23
  39.7 3.9 %collective-permute-start.12 = (f32[64,256]{1,0:T(8,128)S(1)}, f32[64,256]{1,0:T(8,128)S(1)}, u32[]{:S(2)}, u32[]{:S(2)}) collective-permute-start(f32[64,256]{1,0:T(8,128)S(1)} %add.3.a0), channel_id=1, source_target_pairs={{0,2},{2,0},{4,6},{6,4},{1,3},{3,1},{5,7},{7,5},{8,10},{10,8},{12,... | collective-permute-start | bytes 196616 | tf_op jit(solution)/shard_map/ppermute | solution.py:23
  39.8 4.7 %collective-permute-start.13 = (f32[64,256]{1,0:T(8,128)S(1)}, f32[64,256]{1,0:T(8,128)S(1)}, u32[]{:S(2)}, u32[]{:S(2)}) collective-permute-start(f32[64,256]{1,0:T(8,128)S(1)} %add.3.a0), channel_id=1, source_target_pairs={{0,4},{2,6},{4,0},{6,2},{1,5},{3,7},{5,1},{7,3},{8,12},{10,14},{12... | collective-permute-start | bytes 196616 | tf_op jit(solution)/shard_map/ppermute | solution.py:23
  41.3 4.7 %collective-permute-start.14 = (f32[64,256]{1,0:T(8,128)S(1)}, f32[64,256]{1,0:T(8,128)S(1)}, u32[]{:S(2)}, u32[]{:S(2)}) collective-permute-start(f32[64,256]{1,0:T(8,128)S(1)} %add.3.a0), channel_id=1, source_target_pairs={{0,6},{2,4},{4,2},{6,0},{1,7},{3,5},{5,3},{7,1},{8,14},{10,12},{12... | collective-permute-start | bytes 196616 | tf_op jit(solution)/shard_map/ppermute | solution.py:23
  46.1 4.6 %collective-permute-start.15 = (f32[16,256]{1,0:T(8,128)S(1)}, f32[16,256]{1,0:T(8,128)S(1)}, u32[]{:S(2)}, u32[]{:S(2)}) collective-permute-start(f32[16,256]{1,0:T(8,128)S(1)} %get-tuple-element.36.s1), channel_id=1, source_target_pairs={{0,64},{64,0},{128,192},{192,128},{1,65},{65,1},{129,193},{193,129... | collective-permute-start | bytes 49160 | tf_op jit(solution)/shard_map/ppermute | solution.py:23
  46.2 4.5 %collective-permute-start.16 = (f32[16,256]{1,0:T(8,128)S(1)}, f32[16,256]{1,0:T(8,128)S(1)}, u32[]{:S(2)}, u32[]{:S(2)}) collective-permute-start(f32[16,256]{1,0:T(8,128)S(1)} %get-tuple-element.37.s2), channel_id=1, source_target_pairs={{0,128},{64,192},{128,0},{192,64},{1,129},{65,193},{129,1},{193,65... | collective-permute-start | bytes 49160 | tf_op jit(solution)/shard_map/ppermute | solution.py:23
  47.3 3.9 %collective-permute-start.17 = (f32[16,256]{1,0:T(8,128)S(1)}, f32[16,256]{1,0:T(8,128)S(1)}, u32[]{:S(2)}, u32[]{:S(2)}) collective-permute-start(f32[16,256]{1,0:T(8,128)S(1)} %get-tuple-element.38.s3), channel_id=1, source_target_pairs={{0,192},{64,128},{128,64},{192,0},{1,193},{65,129},{129,65},{193,1... | collective-permute-start | bytes 49160 | tf_op jit(solution)/shard_map/ppermute | solution.py:23
  51.2 13.7 %collective-permute-start.18 = (f32[64,256]{1,0:T(8,128)S(1)}, f32[64,256]{1,0:T(8,128)S(1)}, u32[]{:S(2)}, u32[]{:S(2)}) collective-permute-start(f32[64,256]{1,0:T(8,128)S(1)} %pad_maximum_fusion.1.mine_ref), channel_id=1, source_target_pairs={{0,1},{1,0},{2,3},{3,2},{4,5},{5,4},{6,7},{7,6},{8,9},{9,8},{10,11... | collective-permute-start | bytes 196616 | tf_op jit(solution)/shard_map/ppermute | solution.py:23
  54.5 10.4 %all-to-all-start = ((f32[16,1,64]{2,1,0:T(1,128)}), f32[16,1,64]{2,1,0:T(1,128)S(1)}, u32[]{:S(2)}, u32[]{:S(2)}) async-start(f32[16,1,64]{2,1,0:T(1,128)} %bitcast.7), calls=%async_computation | async-start | bytes 16384 | tf_op jit(solution)/shard_map/all_to_all | solution.py:291

commit v7 on v6

--- a/solution.py
+++ b/solution.py
@@ -139,7 +139,7 @@
     out_ref[first_ref.shape[0] :] = second_ref[...]
 
 
-def add_body(in_ref, out_ref, g1_ref, g2_ref, g3_ref, low_ref, half_ref):
+def add_body(in_ref, out_ref, g2_ref, g1_ref, g3_ref, low_ref, half_ref):
     low, half = in_ref[...], out_ref[...]
     for ref in (g1_ref, g2_ref, g3_ref):
         got = ref[...].astype(I32).astype(F32)
@@ -172,7 +172,7 @@
     p_ref[...] = jnp.concatenate(flat + [goal.astype(F32)], 1).astype(BF16)
 
 
-def score_body(p0, p1, p2, p3, first_ref, second_ref, keep_ref, send_ref, goal_ref, held):
+def score_body(p0, p2, p1, p3, first_ref, second_ref, keep_ref, send_ref, goal_ref, held):
     core, z = lax.axis_index("core"), lax.axis_index("z")
     for m, bits in enumerate((0, 7, 2, 5, 1, 6, 3, 4)):
         at = pl.ds(pl.multiple_of((z ^ bits) * C_DEV, C_DEV), C_DEV)
@@ -187,7 +187,7 @@
     goal_ref[...] = jnp.broadcast_to(goal[:, :1] * 16.0 + goal[:, 64:65], (E_ALL, 128))
 
 
-def sum_body(a0, a1, a2, a3, s0, s1, s2, s3):
+def sum_body(a0, a2, a1, a3, s0, s1, s2, s3):
     score = (a0[...] + a1[...]) + (a2[...] + a3[...])
     for d, ref in enumerate((s0, s1, s2, s3)):
         ref[...] = score[d * E_DEV : (d + 1) * E_DEV]
@@ -211,10 +211,10 @@
 
 def lay_body(mine_ref, other_ref, flag_ref, own_flag_ref, slots_ref, out_ref, total_ref):
     core, y, z = (lax.axis_index(name) for name in ("core", "y", "z"))
-    for d in range(NY):
+    for n, d in enumerate((0, 2, 1, 3)):
         for part, ref in ((core, mine_ref), (1 - core, other_ref)):
             at = pl.ds(pl.multiple_of((y ^ d) * C_ALL + part * C_HALF, C_HALF), C_HALF)
-            out_ref[:, at] = ref[d * E_DEV : (d + 1) * E_DEV, :] * flag_ref[:, at].astype(F32)
+            out_ref[:, at] = ref[n * E_DEV : (n + 1) * E_DEV, :] * flag_ref[:, at].astype(F32)
     flags = own_flag_ref[pl.ds(y * NZ + z, 1), :].astype(F32)
     total_ref[...] = jnp.sum(slots_ref[...], 0, keepdims=True) * flags
 
@@ -248,7 +248,7 @@
     got = {d: swap(s, "x", d) for d, s in ((2, s2), (1, s1), (3, s3))}
     held = call(join_body, shaped(NZ // 2, C_DEV, K_DEV, dtype=BF16), held, far, after=in_own)
     far = swap(held, "z", 1)
-    in_sum, out_half = call(add_body, [low, half], in_own, out_chip, got[1], got[2], got[3])
+    in_sum, out_half = call(add_body, [low, half], in_own, out_chip, got[2], got[1], got[3])
     packed = call(
         outer_body,
         shaped(E_DEV, K_DEV + 128, dtype=BF16),
@@ -266,8 +266,8 @@
         score_body,
         [side, side, shaped(E_ALL, 128)],
         packed,
+        packs[2],
         packs[1],
-        packs[2],
         packs[3],
         held,
         far,
@@ -276,10 +276,10 @@
     score = keep + swap(send, "core", 1)
     got = {d: swap(score, "x", d) for d in (2, 1, 3)}
     piece = shaped(E_DEV, C_HALF)
-    pieces = call(sum_body, [piece] * NY, score, got[1], got[2], got[3])
+    pieces = call(sum_body, [piece] * NY, score, got[2], got[1], got[3])
     slots = call(total_body, shaped(NZ * NC, C_DEV), *pieces, goal)
     got = {d: swap(pieces[d], "y", d) for d in (2, 1, 3)}
-    mine = jnp.concatenate([pieces[0], got[1], got[2], got[3]], 0)
+    mine = jnp.concatenate([pieces[0], got[2], got[1], got[3]], 0)
     mine, slots = lax.optimization_barrier((mine, slots))
     sample_affinity, totals = call(
         lay_body,

time: 65.6 us -> 63.4 us (0.966)
  waiting for transfers between devices: 22.3 us -> 20 us
    ppermute x19, waiting for transfers between devices: 15.4 us -> 13.2 us  [swap(): lax.ppermute(value, axis, [(i, i ^ bits) for i in range(SIZES[axis])])]
  transfers between devices with their start and end apart: 20 -> 20, of which waited for: 11 -> 13; matrix products, arithmetic and copies ran while one was open for 0% -> 0% of each run, Pallas kernels for 9% -> 10%
where the time goes in v7:
time: 63.4 us; the launch traced here: 63.3 us
  starting transfers between devices  35.2 us (56%)
  waiting for transfers between devices  20 us (32%)
  Pallas kernels  7.16 us (11%)
  between operations  0.72 us (1%)
    ppermute x19, starting transfers between devices, swap(): lax.ppermute(value, axis, [(i, i ^ bits) for i in range(SIZES[axis])])  31.8 us
    ppermute x19, waiting for transfers between devices, swap(): lax.ppermute(value, axis, [(i, i ^ bits) for i in range(SIZES[axis])])  13.2 us
    all_to_all x1, waiting for transfers between devices, per_device(): lax.all_to_all(slots, ('z', 'core'), 0, 0, tiled=True)  6.87 us
    pallas_call x1, Pallas kernels, project(): pl.pallas_call(project_body, in_specs=[pl.BlockSpec(memory_space=pltpu.HB...  4.77 us
    all_to_all x1, starting transfers between devices, per_device(): lax.all_to_all(slots, ('z', 'core'), 0, 0, tiled=True)  3.4 us
    pallas_call x8, Pallas kernels, call(): pl.pallas_call(run, out_shape=outs, in_specs=specs, scratch_shapes=scratc...  2.39 us
  transfers between devices with their start and end apart: 20, of which 13 were waited for; matrix products, arithmetic and copies ran while one was open for 0% of the time, Pallas kernels for 10%

profile of v7, /device:TPU:1, one launch (start us, length us, event | category | flops | bytes accessed | tf_op | source)
XLA Modules:
  0.0 63.3 jit_solution(2475853874371033467)
XLA Ops:
  0.7 6.5 %collective-permute-start.8 = (bf16[1,64,512]{2,1,0:T(8,128)(2,1)}, bf16[1,64,512]{2,1,0:T(8,128)(2,1)S(1)}, u32[]{:S(2)}, u32[]{:S(2)}) collective-permute-start(bf16[1,64,512]{2,1,0:T(8,128)(2,1)} %bitcast.16), channel_id=1, source_target_pairs={{0,56},{8,48},{16,40},{24,32},{32,24},{40,16},{48,8},{56,0},{1,57}... | collective-permute-start | bytes 196616 | tf_op jit(solution)/shard_map/ppermute | solution.py:23
  7.1 4.8 %shard_map.95 = (f32[64,1024]{1,0:T(8,128)S(1)}, f32[64,1024]{1,0:T(8,128)S(1)}, bf16[64,512]{1,0:T(8,128)(2,1)S(1)}) custom-call(bf16[1024,3584]{1,0:T(8,128)(2,1)} %x_hbm.1, bf16[1024,1024]{1,0:T(8,128)(2,1)} %y_hbm.1, bf16[64,3584]{1,0:T(8,128)(2,1)} %bitcast.14, bf16[64,1024]{1,0:T(8,128)(2,1)} %bitcast.15, bf16[64,512]{1,0:T(8,128)(2,1)} %h_hbm.1), custom_call_target="tpu_custom_call" | custom-call | flops 603979776 | bytes 9437184 | tf_op jit(solution)/shard_map/pallas_call | solution.py:95
  11.9 1.0 %collective-permute-start = (f32[64,1024]{1,0:T(8,128)S(1)}, f32[64,1024]{1,0:T(8,128)S(1)}, u32[]{:S(2)}, u32[]{:S(2)}) collective-permute-start(f32[64,1024]{1,0:T(8,128)S(1)} %get-tuple-element.24), channel_id=1, source_target_pairs={{0,1},{1,0},{2,3},{3,2},{4,5},{5,4},{6,7},{7,6},{8,9},{9,8},{10,11... | collective-permute-start | bytes 786440 | tf_op jit(solution)/shard_map/ppermute | solution.py:23
  13.0 2.2 %collective-permute-start.9 = (bf16[2,64,512]{2,1,0:T(8,128)(2,1)S(1)}, bf16[2,64,512]{2,1,0:T(8,128)(2,1)S(1)}, u32[]{:S(2)}, u32[]{:S(2)}) collective-permute-start(bf16[2,64,512]{2,1,0:T(8,128)(2,1)S(1)} %pad_maximum_fusion.refs_0_), channel_id=1, source_target_pairs={{0,16},{8,24},{16,0},{24,8},{32,48},{40,56},{48,32},{56,40},{1,17}... | collective-permute-start | bytes 393224 | tf_op jit(solution)/shard_map/ppermute | solution.py:23
  15.3 2.8 %collective-permute-start.1 = (s16[48,1024]{1,0:T(8,128)(2,1)S(1)}, s16[48,1024]{1,0:T(8,128)(2,1)S(1)}, u32[]{:S(2)}, u32[]{:S(2)}) collective-permute-start(s16[48,1024]{1,0:T(8,128)(2,1)S(1)} %get-tuple-element.27), channel_id=1, source_target_pairs={{0,4},{2,6},{4,0},{6,2},{1,5},{3,7},{5,1},{7,3},{8,12},{10,14},{12... | collective-permute-start | bytes 294920 | tf_op jit(solution)/shard_map/ppermute | solution.py:23
  18.4 0.6 collective-permute-start.3
  19.0 2.9 %collective-permute-done.9.refs_1_ = bf16[2,64,512]{2,1,0:T(8,128)(2,1)S(1)} collective-permute-done((bf16[2,64,512]{2,1,0:T(8,128)(2,1)S(1)}, bf16[2,64,512]{2,1,0:T(8,128)(2,1)S(1)}, u32[]{:S(2)}, u32[]{:S(2)}) %collective-permute-start.9) | collective-permute-done | bytes 131104 | tf_op jit(solution)/shard_map/ppermute | solution.py:23
  22.0 1.1 %collective-permute-done.2.g1_ref = s16[48,1024]{1,0:T(8,128)(2,1)S(1)} collective-permute-done((s16[48,1024]{1,0:T(8,128)(2,1)S(1)}, s16[48,1024]{1,0:T(8,128)(2,1)S(1)}, u32[]{:S(2)}, u32[]{:S(2)}) %collective-permute-start.2) | collective-permute-done | bytes 98336 | tf_op jit(solution)/shard_map/ppermute | solution.py:23
  23.2 2.1 %collective-permute-start.4 = (f32[32,1024]{1,0:T(8,128)S(1)}, f32[32,1024]{1,0:T(8,128)S(1)}, u32[]{:S(2)}, u32[]{:S(2)}) collective-permute-start(f32[32,1024]{1,0:T(8,128)S(1)} %get-tuple-element.31.mine_ref), channel_id=1, source_target_pairs={{0,1},{1,0},{2,3},{3,2},{4,5},{5,4},{6,7},{7,6},{8,9},{9,8},{10,11... | collective-permute-start | bytes 393224 | tf_op jit(solution)/shard_map/ppermute | solution.py:23
  25.4 0.9 %collective-permute-done.4.other_ref = f32[32,1024]{1,0:T(8,128)S(1)} collective-permute-done((f32[32,1024]{1,0:T(8,128)S(1)}, f32[32,1024]{1,0:T(8,128)S(1)}, u32[]{:S(2)}, u32[]{:S(2)}) %collective-permute-start.4) | collective-permute-done | bytes 131104 | tf_op jit(solution)/shard_map/ppermute | solution.py:23
  26.3 0.4 shard_map.98.p0
  26.7 3.0 %collective-permute-start.5 = (bf16[16,640]{1,0:T(8,128)(2,1)S(1)}, bf16[16,640]{1,0:T(8,128)(2,1)S(1)}, u32[]{:S(2)}, u32[]{:S(2)}) collective-permute-start(bf16[16,640]{1,0:T(8,128)(2,1)S(1)} %shard_map.98.p0), channel_id=1, source_target_pairs={{0,128},{64,192},{128,0},{192,64},{1,129},{65,193},{129,1},{193,65... | collective-permute-start | bytes 61448 | tf_op jit(solution)/shard_map/ppermute | solution.py:23
  29.7 0.4 collective-permute-start.6
  30.1 0.4 collective-permute-start.7
  30.5 0.4 collective-permute-done.5.p2
  30.9 1.4 %collective-permute-done.6.p1 = bf16[16,640]{1,0:T(8,128)(2,1)S(1)} collective-permute-done((bf16[16,640]{1,0:T(8,128)(2,1)S(1)}, bf16[16,640]{1,0:T(8,128)(2,1)S(1)}, u32[]{:S(2)}, u32[]{:S(2)}) %collective-permute-start.6) | collective-permute-done | bytes 20512 | tf_op jit(solution)/shard_map/ppermute | solution.py:23
  32.3 1.6 %collective-permute-done.7.p3 = bf16[16,640]{1,0:T(8,128)(2,1)S(1)} collective-permute-done((bf16[16,640]{1,0:T(8,128)(2,1)S(1)}, bf16[16,640]{1,0:T(8,128)(2,1)S(1)}, u32[]{:S(2)}, u32[]{:S(2)}) %collective-permute-start.7) | collective-permute-done | bytes 20512 | tf_op jit(solution)/shard_map/ppermute | solution.py:23
  34.3 2.2 %collective-permute-start.11 = (f32[64,256]{1,0:T(8,128)S(1)}, f32[64,256]{1,0:T(8,128)S(1)}, u32[]{:S(2)}, u32[]{:S(2)}) collective-permute-start(f32[64,256]{1,0:T(8,128)S(1)} %get-tuple-element.34), channel_id=1, source_target_pairs={{0,1},{1,0},{2,3},{3,2},{4,5},{5,4},{6,7},{7,6},{8,9},{9,8},{10,11... | collective-permute-start | bytes 196616 | tf_op jit(solution)/shard_map/ppermute | solution.py:23
  36.4 0.9 %collective-permute-done.11 = f32[64,256]{1,0:T(8,128)S(1)} collective-permute-done((f32[64,256]{1,0:T(8,128)S(1)}, f32[64,256]{1,0:T(8,128)S(1)}, u32[]{:S(2)}, u32[]{:S(2)}) %collective-permute-start.11) | collective-permute-done | bytes 65568 | tf_op jit(solution)/shard_map/ppermute | solution.py:23
  37.3 1.9 %collective-permute-start.12 = (f32[64,256]{1,0:T(8,128)S(1)}, f32[64,256]{1,0:T(8,128)S(1)}, u32[]{:S(2)}, u32[]{:S(2)}) collective-permute-start(f32[64,256]{1,0:T(8,128)S(1)} %add.3.a0), channel_id=1, source_target_pairs={{0,4},{2,6},{4,0},{6,2},{1,5},{3,7},{5,1},{7,3},{8,12},{10,14},{12... | collective-permute-start | bytes 196616 | tf_op jit(solution)/shard_map/ppermute | solution.py:23
  39.6 1.1 %collective-permute-start.14 = (f32[64,256]{1,0:T(8,128)S(1)}, f32[64,256]{1,0:T(8,128)S(1)}, u32[]{:S(2)}, u32[]{:S(2)}) collective-permute-start(f32[64,256]{1,0:T(8,128)S(1)} %add.3.a0), channel_id=1, source_target_pairs={{0,6},{2,4},{4,2},{6,0},{1,7},{3,5},{5,3},{7,1},{8,14},{10,12},{12... | collective-permute-start | bytes 196616 | tf_op jit(solution)/shard_map/ppermute | solution.py:23
  40.7 1.4 %collective-permute-done.12.a2 = f32[64,256]{1,0:T(8,128)S(1)} collective-permute-done((f32[64,256]{1,0:T(8,128)S(1)}, f32[64,256]{1,0:T(8,128)S(1)}, u32[]{:S(2)}, u32[]{:S(2)}) %collective-permute-start.12) | collective-permute-done | bytes 65568 | tf_op jit(solution)/shard_map/ppermute | solution.py:23
  42.1 1.0 %collective-permute-done.13.a1 = f32[64,256]{1,0:T(8,128)S(1)} collective-permute-done((f32[64,256]{1,0:T(8,128)S(1)}, f32[64,256]{1,0:T(8,128)S(1)}, u32[]{:S(2)}, u32[]{:S(2)}) %collective-permute-start.13) | collective-permute-done | bytes 65568 | tf_op jit(solution)/shard_map/ppermute | solution.py:23
  43.0 1.0 %collective-permute-done.14.a3 = f32[64,256]{1,0:T(8,128)S(1)} collective-permute-done((f32[64,256]{1,0:T(8,128)S(1)}, f32[64,256]{1,0:T(8,128)S(1)}, u32[]{:S(2)}, u32[]{:S(2)}) %collective-permute-start.14) | collective-permute-done | bytes 65568 | tf_op jit(solution)/shard_map/ppermute | solution.py:23
  44.0 0.4 collective-permute-start.15
  44.8 2.6 %collective-permute-start.17 = (f32[16,256]{1,0:T(8,128)S(1)}, f32[16,256]{1,0:T(8,128)S(1)}, u32[]{:S(2)}, u32[]{:S(2)}) collective-permute-start(f32[16,256]{1,0:T(8,128)S(1)} %get-tuple-element.38.s3), channel_id=1, source_target_pairs={{0,192},{64,128},{128,64},{192,0},{1,193},{65,129},{129,65},{193,1... | collective-permute-start | bytes 49160 | tf_op jit(solution)/shard_map/ppermute | solution.py:23
  47.4 0.7 %shard_map.102 = f32[16,64]{1,0:T(8,128)} custom-call(f32[16,256]{1,0:T(8,128)S(1)} %get-tuple-element.35.s0, f32[16,256]{1,0:T(8,128)S(1)} %get-tuple-element.37.s1, f32[16,256]{1,0:T(8,128)S(1)} %get-tuple-element.36.s2, f32[16,256]{1,0:T(8,128)S(1)} %get-tuple-element.38.s3, f32[64,128]{1,0:T(8,128)S(1)} %get-tuple-element.39.goal_ref), custom_call_target="tpu_custom_call" | custom-call | tf_op jit(solution)/shard_map/pallas_call | solution.py:37
  48.2 0.4 collective-permute-done.17
  48.6 3.7 %collective-permute-start.18 = (f32[64,256]{1,0:T(8,128)S(1)}, f32[64,256]{1,0:T(8,128)S(1)}, u32[]{:S(2)}, u32[]{:S(2)}) collective-permute-start(f32[64,256]{1,0:T(8,128)S(1)} %pad_maximum_fusion.1.mine_ref), channel_id=1, source_target_pairs={{0,1},{1,0},{2,3},{3,2},{4,5},{5,4},{6,7},{7,6},{8,9},{9,8},{10,11... | collective-permute-start | bytes 196616 | tf_op jit(solution)/shard_map/ppermute | solution.py:23
  52.2 3.4 %all-to-all-start = ((f32[16,1,64]{2,1,0:T(1,128)}), f32[16,1,64]{2,1,0:T(1,128)S(1)}, u32[]{:S(2)}, u32[]{:S(2)}) async-start(f32[16,1,64]{2,1,0:T(1,128)} %bitcast.7), calls=%async_computation | async-start | bytes 16384 | tf_op jit(solution)/shard_map/all_to_all | solution.py:291
  55.7 6.9 %all-to-all-done = f32[16,1,64]{2,1,0:T(1,128)S(1)} async-done(((f32[16,1,64]{2,1,0:T(1,128)}), f32[16,1,64]{2,1,0:T(1,128)S(1)}, u32[]{:S(2)}, u32[]{:S(2)}) %all-to-all-start) | async-done | bytes 4128 | tf_op jit(solution)/shard_map/all_to_all | solution.py:291
  62.6 0.7 %shard_map.103 = (f32[16,2048]{1,0:T(8,128)}, f32[1,64]{1,0:T(1,128)}) custom-call(f32[64,256]{1,0:T(8,128)S(1)} %pad_maximum_fusion.1.mine_ref, f32[64,256]{1,0:T(8,128)S(1)} %collective-permute-done.18.other_ref, s32[1,2048]{1,0:T(1,128)S(1)} %bitcast.12, s32[32,64]{1,0:T(8,128)S(1)} %reshape.13.own_flag_ref, f32[16,64]{1,0:T(8,128)S(1)} %bitcast.13), custom_call_target="tpu_custom_call" | custom-call | tf_op jit(solution)/shard_map/pallas_call | solution.py:37
  (28 shorter events, 2.0 us)
Async XLA Ops:
  0.6 24.7 %copy-start.2 = (s32[16]{0:T(128)S(1)}, s32[16]{0:T(128)}, u32[]{:S(2)}) copy-start(s32[16]{0:T(128)} %param.13) | copy-start | bytes 196
  0.6 25.6 %copy-start.1 = (s32[1,1024]{1,0:T(1,128)S(1)}, s32[1,1024]{1,0:T(1,128)}, u32[]{:S(2)}) copy-start(s32[1,1024]{1,0:T(1,128)} %where_ref.1) | copy-start | bytes 12292
  0.7 12.3 %collective-permute-start.8 = (bf16[1,64,512]{2,1,0:T(8,128)(2,1)}, bf16[1,64,512]{2,1,0:T(8,128)(2,1)S(1)}, u32[]{:S(2)}, u32[]{:S(2)}) collective-permute-start(bf16[1,64,512]{2,1,0:T(8,128)(2,1)} %bitcast.16), channel_id=1, source_target_pairs={{0,56},{8,48},{16,40},{24,32},{32,24},{40,16},{48,8},{56,0},{1,57}... | collective-permute-start | bytes 196616 | tf_op jit(solution)/shard_map/ppermute | solution.py:23
  7.1 48.5 %copy-start = (s32[2048]{0:T(1024)S(1)}, s32[2048]{0:T(1024)}, u32[]{:S(2)}) copy-start(s32[2048]{0:T(1024)} %param.14) | copy-start | bytes 24580
  11.9 3.2 %collective-permute-start = (f32[64,1024]{1,0:T(8,128)S(1)}, f32[64,1024]{1,0:T(8,128)S(1)}, u32[]{:S(2)}, u32[]{:S(2)}) collective-permute-start(f32[64,1024]{1,0:T(8,128)S(1)} %get-tuple-element.24), channel_id=1, source_target_pairs={{0,1},{1,0},{2,3},{3,2},{4,5},{5,4},{6,7},{7,6},{8,9},{9,8},{10,11... | collective-permute-start | bytes 786440 | tf_op jit(solution)/shard_map/ppermute | solution.py:23
  13.0 8.9 %collective-permute-start.9 = (bf16[2,64,512]{2,1,0:T(8,128)(2,1)S(1)}, bf16[2,64,512]{2,1,0:T(8,128)(2,1)S(1)}, u32[]{:S(2)}, u32[]{:S(2)}) collective-permute-start(bf16[2,64,512]{2,1,0:T(8,128)(2,1)S(1)} %pad_maximum_fusion.refs_0_), channel_id=1, source_target_pairs={{0,16},{8,24},{16,0},{24,8},{32,48},{40,56},{48,32},{56,40},{1,17}... | collective-permute-start | bytes 393224 | tf_op jit(solution)/shard_map/ppermute | solution.py:23
  15.3 6.7 %collective-permute-start.1 = (s16[48,1024]{1,0:T(8,128)(2,1)S(1)}, s16[48,1024]{1,0:T(8,128)(2,1)S(1)}, u32[]{:S(2)}, u32[]{:S(2)}) collective-permute-start(s16[48,1024]{1,0:T(8,128)(2,1)S(1)} %get-tuple-element.27), channel_id=1, source_target_pairs={{0,4},{2,6},{4,0},{6,2},{1,5},{3,7},{5,1},{7,3},{8,12},{10,14},{12... | collective-permute-start | bytes 294920 | tf_op jit(solution)/shard_map/ppermute | solution.py:23
  18.1 5.0 %collective-permute-start.2 = (s16[48,1024]{1,0:T(8,128)(2,1)S(1)}, s16[48,1024]{1,0:T(8,128)(2,1)S(1)}, u32[]{:S(2)}, u32[]{:S(2)}) collective-permute-start(s16[48,1024]{1,0:T(8,128)(2,1)S(1)} %get-tuple-element.28), channel_id=1, source_target_pairs={{0,2},{2,0},{4,6},{6,4},{1,3},{3,1},{5,7},{7,5},{8,10},{10,8},{12,... | collective-permute-start | bytes 294920 | tf_op jit(solution)/shard_map/ppermute | solution.py:23
  18.4 4.7 %collective-permute-start.3 = (s16[48,1024]{1,0:T(8,128)(2,1)S(1)}, s16[48,1024]{1,0:T(8,128)(2,1)S(1)}, u32[]{:S(2)}, u32[]{:S(2)}) collective-permute-start(s16[48,1024]{1,0:T(8,128)(2,1)S(1)} %get-tuple-element.29), channel_id=1, source_target_pairs={{0,6},{2,4},{4,2},{6,0},{1,7},{3,5},{5,3},{7,1},{8,14},{10,12},{12... | collective-permute-start | bytes 294920 | tf_op jit(solution)/shard_map/ppermute | solution.py:23
  21.9 12.0 %collective-permute-start.10 = (bf16[4,64,512]{2,1,0:T(8,128)(2,1)S(1)}, bf16[4,64,512]{2,1,0:T(8,128)(2,1)S(1)}, u32[]{:S(2)}, u32[]{:S(2)}) collective-permute-start(bf16[4,64,512]{2,1,0:T(8,128)(2,1)S(1)} %shard_map.99.first_ref), channel_id=1, source_target_pairs={{0,8},{8,0},{16,24},{24,16},{32,40},{40,32},{48,56},{56,48},{1,9},... | collective-permute-start | bytes 786440 | tf_op jit(solution)/shard_map/ppermute | solution.py:23
  23.2 3.0 %collective-permute-start.4 = (f32[32,1024]{1,0:T(8,128)S(1)}, f32[32,1024]{1,0:T(8,128)S(1)}, u32[]{:S(2)}, u32[]{:S(2)}) collective-permute-start(f32[32,1024]{1,0:T(8,128)S(1)} %get-tuple-element.31.mine_ref), channel_id=1, source_target_pairs={{0,1},{1,0},{2,3},{3,2},{4,5},{5,4},{6,7},{7,6},{8,9},{9,8},{10,11... | collective-permute-start | bytes 393224 | tf_op jit(solution)/shard_map/ppermute | solution.py:23
  26.7 4.2 %collective-permute-start.5 = (bf16[16,640]{1,0:T(8,128)(2,1)S(1)}, bf16[16,640]{1,0:T(8,128)(2,1)S(1)}, u32[]{:S(2)}, u32[]{:S(2)}) collective-permute-start(bf16[16,640]{1,0:T(8,128)(2,1)S(1)} %shard_map.98.p0), channel_id=1, source_target_pairs={{0,128},{64,192},{128,0},{192,64},{1,129},{65,193},{129,1},{193,65... | collective-permute-start | bytes 61448 | tf_op jit(solution)/shard_map/ppermute | solution.py:23
  29.7 2.6 %collective-permute-start.6 = (bf16[16,640]{1,0:T(8,128)(2,1)S(1)}, bf16[16,640]{1,0:T(8,128)(2,1)S(1)}, u32[]{:S(2)}, u32[]{:S(2)}) collective-permute-start(bf16[16,640]{1,0:T(8,128)(2,1)S(1)} %shard_map.98.p0), channel_id=1, source_target_pairs={{0,64},{64,0},{128,192},{192,128},{1,65},{65,1},{129,193},{193,129... | collective-permute-start | bytes 61448 | tf_op jit(solution)/shard_map/ppermute | solution.py:23
  30.1 3.8 %collective-permute-start.7 = (bf16[16,640]{1,0:T(8,128)(2,1)S(1)}, bf16[16,640]{1,0:T(8,128)(2,1)S(1)}, u32[]{:S(2)}, u32[]{:S(2)}) collective-permute-start(bf16[16,640]{1,0:T(8,128)(2,1)S(1)} %shard_map.98.p0), channel_id=1, source_target_pairs={{0,192},{64,128},{128,64},{192,0},{1,193},{65,129},{129,65},{193,1... | collective-permute-start | bytes 61448 | tf_op jit(solution)/shard_map/ppermute | solution.py:23
  34.3 3.1 %collective-permute-start.11 = (f32[64,256]{1,0:T(8,128)S(1)}, f32[64,256]{1,0:T(8,128)S(1)}, u32[]{:S(2)}, u32[]{:S(2)}) collective-permute-start(f32[64,256]{1,0:T(8,128)S(1)} %get-tuple-element.34), channel_id=1, source_target_pairs={{0,1},{1,0},{2,3},{3,2},{4,5},{5,4},{6,7},{7,6},{8,9},{9,8},{10,11... | collective-permute-start | bytes 196616 | tf_op jit(solution)/shard_map/ppermute | solution.py:23
  37.3 4.7 %collective-permute-start.12 = (f32[64,256]{1,0:T(8,128)S(1)}, f32[64,256]{1,0:T(8,128)S(1)}, u32[]{:S(2)}, u32[]{:S(2)}) collective-permute-start(f32[64,256]{1,0:T(8,128)S(1)} %add.3.a0), channel_id=1, source_target_pairs={{0,4},{2,6},{4,0},{6,2},{1,5},{3,7},{5,1},{7,3},{8,12},{10,14},{12... | collective-permute-start | bytes 196616 | tf_op jit(solution)/shard_map/ppermute | solution.py:23
  39.2 3.8 %collective-permute-start.13 = (f32[64,256]{1,0:T(8,128)S(1)}, f32[64,256]{1,0:T(8,128)S(1)}, u32[]{:S(2)}, u32[]{:S(2)}) collective-permute-start(f32[64,256]{1,0:T(8,128)S(1)} %add.3.a0), channel_id=1, source_target_pairs={{0,2},{2,0},{4,6},{6,4},{1,3},{3,1},{5,7},{7,5},{8,10},{10,8},{12,... | collective-permute-start | bytes 196616 | tf_op jit(solution)/shard_map/ppermute | solution.py:23
  39.6 4.5 %collective-permute-start.14 = (f32[64,256]{1,0:T(8,128)S(1)}, f32[64,256]{1,0:T(8,128)S(1)}, u32[]{:S(2)}, u32[]{:S(2)}) collective-permute-start(f32[64,256]{1,0:T(8,128)S(1)} %add.3.a0), channel_id=1, source_target_pairs={{0,6},{2,4},{4,2},{6,0},{1,7},{3,5},{5,3},{7,1},{8,14},{10,12},{12... | collective-permute-start | bytes 196616 | tf_op jit(solution)/shard_map/ppermute | solution.py:23
  44.0 4.2 %collective-permute-start.15 = (f32[16,256]{1,0:T(8,128)S(1)}, f32[16,256]{1,0:T(8,128)S(1)}, u32[]{:S(2)}, u32[]{:S(2)}) collective-permute-start(f32[16,256]{1,0:T(8,128)S(1)} %get-tuple-element.36.s2), channel_id=1, source_target_pairs={{0,128},{64,192},{128,0},{192,64},{1,129},{65,193},{129,1},{193,65... | collective-permute-start | bytes 49160 | tf_op jit(solution)/shard_map/ppermute | solution.py:23
  44.5 3.8 %collective-permute-start.16 = (f32[16,256]{1,0:T(8,128)S(1)}, f32[16,256]{1,0:T(8,128)S(1)}, u32[]{:S(2)}, u32[]{:S(2)}) collective-permute-start(f32[16,256]{1,0:T(8,128)S(1)} %get-tuple-element.37.s1), channel_id=1, source_target_pairs={{0,64},{64,0},{128,192},{192,128},{1,65},{65,1},{129,193},{193,129... | collective-permute-start | bytes 49160 | tf_op jit(solution)/shard_map/ppermute | solution.py:23
  44.8 3.8 %collective-permute-start.17 = (f32[16,256]{1,0:T(8,128)S(1)}, f32[16,256]{1,0:T(8,128)S(1)}, u32[]{:S(2)}, u32[]{:S(2)}) collective-permute-start(f32[16,256]{1,0:T(8,128)S(1)} %get-tuple-element.38.s3), channel_id=1, source_target_pairs={{0,192},{64,128},{128,64},{192,0},{1,193},{65,129},{129,65},{193,1... | collective-permute-start | bytes 49160 | tf_op jit(solution)/shard_map/ppermute | solution.py:23
  48.6 14.0 %collective-permute-start.18 = (f32[64,256]{1,0:T(8,128)S(1)}, f32[64,256]{1,0:T(8,128)S(1)}, u32[]{:S(2)}, u32[]{:S(2)}) collective-permute-start(f32[64,256]{1,0:T(8,128)S(1)} %pad_maximum_fusion.1.mine_ref), channel_id=1, source_target_pairs={{0,1},{1,0},{2,3},{3,2},{4,5},{5,4},{6,7},{7,6},{8,9},{9,8},{10,11... | collective-permute-start | bytes 196616 | tf_op jit(solution)/shard_map/ppermute | solution.py:23
  52.2 10.3 %all-to-all-start = ((f32[16,1,64]{2,1,0:T(1,128)}), f32[16,1,64]{2,1,0:T(1,128)S(1)}, u32[]{:S(2)}, u32[]{:S(2)}) async-start(f32[16,1,64]{2,1,0:T(1,128)} %bitcast.7), calls=%async_computation | async-start | bytes 16384 | tf_op jit(solution)/shard_map/all_to_all | solution.py:291

commit v8 on v7

--- a/solution.py
+++ b/solution.py
@@ -187,8 +187,18 @@
     goal_ref[...] = jnp.broadcast_to(goal[:, :1] * 16.0 + goal[:, 64:65], (E_ALL, 128))
 
 
+def pack_body(keep_ref, got_ref, code_ref):
+    code, power = coded(keep_ref[...] + got_ref[...])
+    power = jnp.broadcast_to(power, (2 * ROWS, C_HALF))
+    code_ref[...] = jnp.concatenate([code, power], 0).astype(I32).astype(I16)
+
+
 def sum_body(a0, a2, a1, a3, s0, s1, s2, s3):
-    score = (a0[...] + a1[...]) + (a2[...] + a3[...])
+    parts = []
+    for ref in (a0, a1, a2, a3):
+        got = ref[...].astype(I32).astype(F32)
+        parts.append(got[:E_ALL] * jnp.exp2(got[E_ALL : E_ALL + 1]))
+    score = (parts[0] + parts[1]) + (parts[2] + parts[3])
     for d, ref in enumerate((s0, s1, s2, s3)):
         ref[...] = score[d * E_DEV : (d + 1) * E_DEV]
 
@@ -273,7 +283,9 @@
         far,
         scratch=[pltpu.VMEM((C_ALL, K_DEV), BF16)],
     )
-    score = keep + swap(send, "core", 1)
+    score = call(
+        pack_body, shaped(E_ALL + 2 * ROWS, C_HALF, dtype=I16), keep, swap(send, "core", 1)
+    )
     got = {d: swap(score, "x", d) for d in (2, 1, 3)}
     piece = shaped(E_DEV, C_HALF)
     pieces = call(sum_body, [piece] * NY, score, got[2], got[1], got[3])

time: 63.4 us -> 63.1 us (level)
    pallas_call x8 -> x9, Pallas kernels: 2.39 us -> 2.45 us  [call(): pl.pallas_call(run, out_shape=outs, in_specs=specs, scratch_shapes=scratc...]
where the time goes in v8:
time: 63.1 us; the launch traced here: 63 us
  starting transfers between devices  35.3 us (56%)
  waiting for transfers between devices  19.6 us (31%)
  Pallas kernels  7.22 us (11%)
  between operations  0.74 us (1%)
    ppermute x19, starting transfers between devices, swap(): lax.ppermute(value, axis, [(i, i ^ bits) for i in range(SIZES[axis])])  31.9 us
    ppermute x19, waiting for transfers between devices, swap(): lax.ppermute(value, axis, [(i, i ^ bits) for i in range(SIZES[axis])])  12.8 us
    all_to_all x1, waiting for transfers between devices, per_device(): lax.all_to_all(slots, ('z', 'core'), 0, 0, tiled=True)  6.81 us
    pallas_call x1, Pallas kernels, project(): pl.pallas_call(project_body, in_specs=[pl.BlockSpec(memory_space=pltpu.HB...  4.77 us
    all_to_all x1, starting transfers between devices, per_device(): lax.all_to_all(slots, ('z', 'core'), 0, 0, tiled=True)  3.37 us
    pallas_call x9, Pallas kernels, call(): pl.pallas_call(run, out_shape=outs, in_specs=specs, scratch_shapes=scratc...  2.45 us
  transfers between devices with their start and end apart: 20, of which 13 were waited for; matrix products, arithmetic and copies ran while one was open for 0% of the time, Pallas kernels for 10%

profile of v8, /device:TPU:1, one launch (start us, length us, event | category | flops | bytes accessed | tf_op | source)
XLA Modules:
  0.0 63.0 jit_solution(17593560135398809387)
XLA Ops:
  0.7 6.5 %collective-permute-start.8 = (bf16[1,64,512]{2,1,0:T(8,128)(2,1)}, bf16[1,64,512]{2,1,0:T(8,128)(2,1)S(1)}, u32[]{:S(2)}, u32[]{:S(2)}) collective-permute-start(bf16[1,64,512]{2,1,0:T(8,128)(2,1)} %bitcast.16), channel_id=1, source_target_pairs={{0,56},{8,48},{16,40},{24,32},{32,24},{40,16},{48,8},{56,0},{1,57}... | collective-permute-start | bytes 196616 | tf_op jit(solution)/shard_map/ppermute | solution.py:23
  7.2 4.8 %shard_map.95 = (f32[64,1024]{1,0:T(8,128)S(1)}, f32[64,1024]{1,0:T(8,128)S(1)}, bf16[64,512]{1,0:T(8,128)(2,1)S(1)}) custom-call(bf16[1024,3584]{1,0:T(8,128)(2,1)} %x_hbm.1, bf16[1024,1024]{1,0:T(8,128)(2,1)} %y_hbm.1, bf16[64,3584]{1,0:T(8,128)(2,1)} %bitcast.14, bf16[64,1024]{1,0:T(8,128)(2,1)} %bitcast.15, bf16[64,512]{1,0:T(8,128)(2,1)} %h_hbm.1), custom_call_target="tpu_custom_call" | custom-call | flops 603979776 | bytes 9437184 | tf_op jit(solution)/shard_map/pallas_call | solution.py:95
  11.9 1.0 %collective-permute-start = (f32[64,1024]{1,0:T(8,128)S(1)}, f32[64,1024]{1,0:T(8,128)S(1)}, u32[]{:S(2)}, u32[]{:S(2)}) collective-permute-start(f32[64,1024]{1,0:T(8,128)S(1)} %get-tuple-element.24), channel_id=1, source_target_pairs={{0,1},{1,0},{2,3},{3,2},{4,5},{5,4},{6,7},{7,6},{8,9},{9,8},{10,11... | collective-permute-start | bytes 786440 | tf_op jit(solution)/shard_map/ppermute | solution.py:23
  13.0 2.2 %collective-permute-start.9 = (bf16[2,64,512]{2,1,0:T(8,128)(2,1)S(1)}, bf16[2,64,512]{2,1,0:T(8,128)(2,1)S(1)}, u32[]{:S(2)}, u32[]{:S(2)}) collective-permute-start(bf16[2,64,512]{2,1,0:T(8,128)(2,1)S(1)} %pad_maximum_fusion.refs_0_), channel_id=1, source_target_pairs={{0,16},{8,24},{16,0},{24,8},{32,48},{40,56},{48,32},{56,40},{1,17}... | collective-permute-start | bytes 393224 | tf_op jit(solution)/shard_map/ppermute | solution.py:23
  15.3 2.8 %collective-permute-start.1 = (s16[48,1024]{1,0:T(8,128)(2,1)S(1)}, s16[48,1024]{1,0:T(8,128)(2,1)S(1)}, u32[]{:S(2)}, u32[]{:S(2)}) collective-permute-start(s16[48,1024]{1,0:T(8,128)(2,1)S(1)} %get-tuple-element.27), channel_id=1, source_target_pairs={{0,4},{2,6},{4,0},{6,2},{1,5},{3,7},{5,1},{7,3},{8,12},{10,14},{12... | collective-permute-start | bytes 294920 | tf_op jit(solution)/shard_map/ppermute | solution.py:23
  18.4 0.5 collective-permute-start.3
  19.0 2.9 %collective-permute-done.9.refs_1_ = bf16[2,64,512]{2,1,0:T(8,128)(2,1)S(1)} collective-permute-done((bf16[2,64,512]{2,1,0:T(8,128)(2,1)S(1)}, bf16[2,64,512]{2,1,0:T(8,128)(2,1)S(1)}, u32[]{:S(2)}, u32[]{:S(2)}) %collective-permute-start.9) | collective-permute-done | bytes 131104 | tf_op jit(solution)/shard_map/ppermute | solution.py:23
  22.0 1.1 %collective-permute-done.2.g1_ref = s16[48,1024]{1,0:T(8,128)(2,1)S(1)} collective-permute-done((s16[48,1024]{1,0:T(8,128)(2,1)S(1)}, s16[48,1024]{1,0:T(8,128)(2,1)S(1)}, u32[]{:S(2)}, u32[]{:S(2)}) %collective-permute-start.2) | collective-permute-done | bytes 98336 | tf_op jit(solution)/shard_map/ppermute | solution.py:23
  23.2 2.1 %collective-permute-start.4 = (f32[32,1024]{1,0:T(8,128)S(1)}, f32[32,1024]{1,0:T(8,128)S(1)}, u32[]{:S(2)}, u32[]{:S(2)}) collective-permute-start(f32[32,1024]{1,0:T(8,128)S(1)} %get-tuple-element.31.mine_ref), channel_id=1, source_target_pairs={{0,1},{1,0},{2,3},{3,2},{4,5},{5,4},{6,7},{7,6},{8,9},{9,8},{10,11... | collective-permute-start | bytes 393224 | tf_op jit(solution)/shard_map/ppermute | solution.py:23
  25.4 0.9 %collective-permute-done.4.other_ref = f32[32,1024]{1,0:T(8,128)S(1)} collective-permute-done((f32[32,1024]{1,0:T(8,128)S(1)}, f32[32,1024]{1,0:T(8,128)S(1)}, u32[]{:S(2)}, u32[]{:S(2)}) %collective-permute-start.4) | collective-permute-done | bytes 131104 | tf_op jit(solution)/shard_map/ppermute | solution.py:23
  26.3 0.4 shard_map.98.p0
  26.7 3.0 %collective-permute-start.5 = (bf16[16,640]{1,0:T(8,128)(2,1)S(1)}, bf16[16,640]{1,0:T(8,128)(2,1)S(1)}, u32[]{:S(2)}, u32[]{:S(2)}) collective-permute-start(bf16[16,640]{1,0:T(8,128)(2,1)S(1)} %shard_map.98.p0), channel_id=1, source_target_pairs={{0,128},{64,192},{128,0},{192,64},{1,129},{65,193},{129,1},{193,65... | collective-permute-start | bytes 61448 | tf_op jit(solution)/shard_map/ppermute | solution.py:23
  29.7 0.4 collective-permute-start.6
  30.1 0.4 collective-permute-start.7
  30.5 0.4 collective-permute-done.5.p2
  30.9 1.4 %collective-permute-done.6.p1 = bf16[16,640]{1,0:T(8,128)(2,1)S(1)} collective-permute-done((bf16[16,640]{1,0:T(8,128)(2,1)S(1)}, bf16[16,640]{1,0:T(8,128)(2,1)S(1)}, u32[]{:S(2)}, u32[]{:S(2)}) %collective-permute-start.6) | collective-permute-done | bytes 20512 | tf_op jit(solution)/shard_map/ppermute | solution.py:23
  32.3 1.6 %collective-permute-done.7.p3 = bf16[16,640]{1,0:T(8,128)(2,1)S(1)} collective-permute-done((bf16[16,640]{1,0:T(8,128)(2,1)S(1)}, bf16[16,640]{1,0:T(8,128)(2,1)S(1)}, u32[]{:S(2)}, u32[]{:S(2)}) %collective-permute-start.7) | collective-permute-done | bytes 20512 | tf_op jit(solution)/shard_map/ppermute | solution.py:23
  34.3 2.2 %collective-permute-start.11 = (f32[64,256]{1,0:T(8,128)S(1)}, f32[64,256]{1,0:T(8,128)S(1)}, u32[]{:S(2)}, u32[]{:S(2)}) collective-permute-start(f32[64,256]{1,0:T(8,128)S(1)} %get-tuple-element.34), channel_id=1, source_target_pairs={{0,1},{1,0},{2,3},{3,2},{4,5},{5,4},{6,7},{7,6},{8,9},{9,8},{10,11... | collective-permute-start | bytes 196616 | tf_op jit(solution)/shard_map/ppermute | solution.py:23
  36.4 0.9 %collective-permute-done.11.got_ref = f32[64,256]{1,0:T(8,128)S(1)} collective-permute-done((f32[64,256]{1,0:T(8,128)S(1)}, f32[64,256]{1,0:T(8,128)S(1)}, u32[]{:S(2)}, u32[]{:S(2)}) %collective-permute-start.11) | collective-permute-done | bytes 65568 | tf_op jit(solution)/shard_map/ppermute | solution.py:23
  37.4 1.9 %collective-permute-start.12 = (s16[80,256]{1,0:T(8,128)(2,1)S(1)}, s16[80,256]{1,0:T(8,128)(2,1)S(1)}, u32[]{:S(2)}, u32[]{:S(2)}) collective-permute-start(s16[80,256]{1,0:T(8,128)(2,1)S(1)} %shard_map.101.a0), channel_id=1, source_target_pairs={{0,4},{2,6},{4,0},{6,2},{1,5},{3,7},{5,1},{7,3},{8,12},{10,14},{12... | collective-permute-start | bytes 122888 | tf_op jit(solution)/shard_map/ppermute | solution.py:23
  39.6 1.1 %collective-permute-start.14 = (s16[80,256]{1,0:T(8,128)(2,1)S(1)}, s16[80,256]{1,0:T(8,128)(2,1)S(1)}, u32[]{:S(2)}, u32[]{:S(2)}) collective-permute-start(s16[80,256]{1,0:T(8,128)(2,1)S(1)} %shard_map.101.a0), channel_id=1, source_target_pairs={{0,6},{2,4},{4,2},{6,0},{1,7},{3,5},{5,3},{7,1},{8,14},{10,12},{12... | collective-permute-start | bytes 122888 | tf_op jit(solution)/shard_map/ppermute | solution.py:23
  40.7 1.1 %collective-permute-done.12.a2 = s16[80,256]{1,0:T(8,128)(2,1)S(1)} collective-permute-done((s16[80,256]{1,0:T(8,128)(2,1)S(1)}, s16[80,256]{1,0:T(8,128)(2,1)S(1)}, u32[]{:S(2)}, u32[]{:S(2)}) %collective-permute-start.12) | collective-permute-done | bytes 40992 | tf_op jit(solution)/shard_map/ppermute | solution.py:23
  41.8 0.7 %collective-permute-done.13.a1 = s16[80,256]{1,0:T(8,128)(2,1)S(1)} collective-permute-done((s16[80,256]{1,0:T(8,128)(2,1)S(1)}, s16[80,256]{1,0:T(8,128)(2,1)S(1)}, u32[]{:S(2)}, u32[]{:S(2)}) %collective-permute-start.13) | collective-permute-done | bytes 40992 | tf_op jit(solution)/shard_map/ppermute | solution.py:23
  42.5 1.1 %collective-permute-done.14.a3 = s16[80,256]{1,0:T(8,128)(2,1)S(1)} collective-permute-done((s16[80,256]{1,0:T(8,128)(2,1)S(1)}, s16[80,256]{1,0:T(8,128)(2,1)S(1)}, u32[]{:S(2)}, u32[]{:S(2)}) %collective-permute-start.14) | collective-permute-done | bytes 40992 | tf_op jit(solution)/shard_map/ppermute | solution.py:23
  43.7 0.4 collective-permute-start.15
  44.5 2.6 %collective-permute-start.17 = (f32[16,256]{1,0:T(8,128)S(1)}, f32[16,256]{1,0:T(8,128)S(1)}, u32[]{:S(2)}, u32[]{:S(2)}) collective-permute-start(f32[16,256]{1,0:T(8,128)S(1)} %get-tuple-element.38.s3), channel_id=1, source_target_pairs={{0,192},{64,128},{128,64},{192,0},{1,193},{65,129},{129,65},{193,1... | collective-permute-start | bytes 49160 | tf_op jit(solution)/shard_map/ppermute | solution.py:23
  47.0 0.7 %shard_map.103 = f32[16,64]{1,0:T(8,128)} custom-call(f32[16,256]{1,0:T(8,128)S(1)} %get-tuple-element.35.s0, f32[16,256]{1,0:T(8,128)S(1)} %get-tuple-element.37.s1, f32[16,256]{1,0:T(8,128)S(1)} %get-tuple-element.36.s2, f32[16,256]{1,0:T(8,128)S(1)} %get-tuple-element.38.s3, f32[64,128]{1,0:T(8,128)S(1)} %get-tuple-element.39.goal_ref), custom_call_target="tpu_custom_call" | custom-call | tf_op jit(solution)/shard_map/pallas_call | solution.py:37
  47.9 0.4 collective-permute-done.17
  48.3 3.8 %collective-permute-start.18 = (f32[64,256]{1,0:T(8,128)S(1)}, f32[64,256]{1,0:T(8,128)S(1)}, u32[]{:S(2)}, u32[]{:S(2)}) collective-permute-start(f32[64,256]{1,0:T(8,128)S(1)} %pad_maximum_fusion.1.mine_ref), channel_id=1, source_target_pairs={{0,1},{1,0},{2,3},{3,2},{4,5},{5,4},{6,7},{7,6},{8,9},{9,8},{10,11... | collective-permute-start | bytes 196616 | tf_op jit(solution)/shard_map/ppermute | solution.py:23
  52.0 3.4 %all-to-all-start = ((f32[16,1,64]{2,1,0:T(1,128)}), f32[16,1,64]{2,1,0:T(1,128)S(1)}, u32[]{:S(2)}, u32[]{:S(2)}) async-start(f32[16,1,64]{2,1,0:T(1,128)} %bitcast.7), calls=%async_computation | async-start | bytes 16384 | tf_op jit(solution)/shard_map/all_to_all | solution.py:303
  55.5 6.8 %all-to-all-done = f32[16,1,64]{2,1,0:T(1,128)S(1)} async-done(((f32[16,1,64]{2,1,0:T(1,128)}), f32[16,1,64]{2,1,0:T(1,128)S(1)}, u32[]{:S(2)}, u32[]{:S(2)}) %all-to-all-start) | async-done | bytes 4128 | tf_op jit(solution)/shard_map/all_to_all | solution.py:303
  62.3 0.7 %shard_map.104 = (f32[16,2048]{1,0:T(8,128)}, f32[1,64]{1,0:T(1,128)}) custom-call(f32[64,256]{1,0:T(8,128)S(1)} %pad_maximum_fusion.1.mine_ref, f32[64,256]{1,0:T(8,128)S(1)} %collective-permute-done.18.other_ref, s32[1,2048]{1,0:T(1,128)S(1)} %bitcast.12, s32[32,64]{1,0:T(8,128)S(1)} %reshape.13.own_flag_ref, f32[16,64]{1,0:T(8,128)S(1)} %bitcast.13), custom_call_target="tpu_custom_call" | custom-call | tf_op jit(solution)/shard_map/pallas_call | solution.py:37
  (28 shorter events, 2.0 us)
Async XLA Ops:
  0.6 24.7 %copy-start.2 = (s32[16]{0:T(128)S(1)}, s32[16]{0:T(128)}, u32[]{:S(2)}) copy-start(s32[16]{0:T(128)} %param.13) | copy-start | bytes 196
  0.6 25.6 %copy-start.1 = (s32[1,1024]{1,0:T(1,128)S(1)}, s32[1,1024]{1,0:T(1,128)}, u32[]{:S(2)}) copy-start(s32[1,1024]{1,0:T(1,128)} %where_ref.1) | copy-start | bytes 12292
  0.7 54.8 %copy-start = (s32[2048]{0:T(1024)S(1)}, s32[2048]{0:T(1024)}, u32[]{:S(2)}) copy-start(s32[2048]{0:T(1024)} %param.14) | copy-start | bytes 24580
  0.7 12.3 %collective-permute-start.8 = (bf16[1,64,512]{2,1,0:T(8,128)(2,1)}, bf16[1,64,512]{2,1,0:T(8,128)(2,1)S(1)}, u32[]{:S(2)}, u32[]{:S(2)}) collective-permute-start(bf16[1,64,512]{2,1,0:T(8,128)(2,1)} %bitcast.16), channel_id=1, source_target_pairs={{0,56},{8,48},{16,40},{24,32},{32,24},{40,16},{48,8},{56,0},{1,57}... | collective-permute-start | bytes 196616 | tf_op jit(solution)/shard_map/ppermute | solution.py:23
  11.9 3.2 %collective-permute-start = (f32[64,1024]{1,0:T(8,128)S(1)}, f32[64,1024]{1,0:T(8,128)S(1)}, u32[]{:S(2)}, u32[]{:S(2)}) collective-permute-start(f32[64,1024]{1,0:T(8,128)S(1)} %get-tuple-element.24), channel_id=1, source_target_pairs={{0,1},{1,0},{2,3},{3,2},{4,5},{5,4},{6,7},{7,6},{8,9},{9,8},{10,11... | collective-permute-start | bytes 786440 | tf_op jit(solution)/shard_map/ppermute | solution.py:23
  13.0 8.9 %collective-permute-start.9 = (bf16[2,64,512]{2,1,0:T(8,128)(2,1)S(1)}, bf16[2,64,512]{2,1,0:T(8,128)(2,1)S(1)}, u32[]{:S(2)}, u32[]{:S(2)}) collective-permute-start(bf16[2,64,512]{2,1,0:T(8,128)(2,1)S(1)} %pad_maximum_fusion.refs_0_), channel_id=1, source_target_pairs={{0,16},{8,24},{16,0},{24,8},{32,48},{40,56},{48,32},{56,40},{1,17}... | collective-permute-start | bytes 393224 | tf_op jit(solution)/shard_map/ppermute | solution.py:23
  15.3 6.7 %collective-permute-start.1 = (s16[48,1024]{1,0:T(8,128)(2,1)S(1)}, s16[48,1024]{1,0:T(8,128)(2,1)S(1)}, u32[]{:S(2)}, u32[]{:S(2)}) collective-permute-start(s16[48,1024]{1,0:T(8,128)(2,1)S(1)} %get-tuple-element.27), channel_id=1, source_target_pairs={{0,4},{2,6},{4,0},{6,2},{1,5},{3,7},{5,1},{7,3},{8,12},{10,14},{12... | collective-permute-start | bytes 294920 | tf_op jit(solution)/shard_map/ppermute | solution.py:23
  18.1 5.0 %collective-permute-start.2 = (s16[48,1024]{1,0:T(8,128)(2,1)S(1)}, s16[48,1024]{1,0:T(8,128)(2,1)S(1)}, u32[]{:S(2)}, u32[]{:S(2)}) collective-permute-start(s16[48,1024]{1,0:T(8,128)(2,1)S(1)} %get-tuple-element.28), channel_id=1, source_target_pairs={{0,2},{2,0},{4,6},{6,4},{1,3},{3,1},{5,7},{7,5},{8,10},{10,8},{12,... | collective-permute-start | bytes 294920 | tf_op jit(solution)/shard_map/ppermute | solution.py:23
  18.4 4.7 %collective-permute-start.3 = (s16[48,1024]{1,0:T(8,128)(2,1)S(1)}, s16[48,1024]{1,0:T(8,128)(2,1)S(1)}, u32[]{:S(2)}, u32[]{:S(2)}) collective-permute-start(s16[48,1024]{1,0:T(8,128)(2,1)S(1)} %get-tuple-element.29), channel_id=1, source_target_pairs={{0,6},{2,4},{4,2},{6,0},{1,7},{3,5},{5,3},{7,1},{8,14},{10,12},{12... | collective-permute-start | bytes 294920 | tf_op jit(solution)/shard_map/ppermute | solution.py:23
  21.9 12.0 %collective-permute-start.10 = (bf16[4,64,512]{2,1,0:T(8,128)(2,1)S(1)}, bf16[4,64,512]{2,1,0:T(8,128)(2,1)S(1)}, u32[]{:S(2)}, u32[]{:S(2)}) collective-permute-start(bf16[4,64,512]{2,1,0:T(8,128)(2,1)S(1)} %shard_map.99.first_ref), channel_id=1, source_target_pairs={{0,8},{8,0},{16,24},{24,16},{32,40},{40,32},{48,56},{56,48},{1,9},... | collective-permute-start | bytes 786440 | tf_op jit(solution)/shard_map/ppermute | solution.py:23
  23.2 3.0 %collective-permute-start.4 = (f32[32,1024]{1,0:T(8,128)S(1)}, f32[32,1024]{1,0:T(8,128)S(1)}, u32[]{:S(2)}, u32[]{:S(2)}) collective-permute-start(f32[32,1024]{1,0:T(8,128)S(1)} %get-tuple-element.31.mine_ref), channel_id=1, source_target_pairs={{0,1},{1,0},{2,3},{3,2},{4,5},{5,4},{6,7},{7,6},{8,9},{9,8},{10,11... | collective-permute-start | bytes 393224 | tf_op jit(solution)/shard_map/ppermute | solution.py:23
  26.7 4.2 %collective-permute-start.5 = (bf16[16,640]{1,0:T(8,128)(2,1)S(1)}, bf16[16,640]{1,0:T(8,128)(2,1)S(1)}, u32[]{:S(2)}, u32[]{:S(2)}) collective-permute-start(bf16[16,640]{1,0:T(8,128)(2,1)S(1)} %shard_map.98.p0), channel_id=1, source_target_pairs={{0,128},{64,192},{128,0},{192,64},{1,129},{65,193},{129,1},{193,65... | collective-permute-start | bytes 61448 | tf_op jit(solution)/shard_map/ppermute | solution.py:23
  29.7 2.6 %collective-permute-start.6 = (bf16[16,640]{1,0:T(8,128)(2,1)S(1)}, bf16[16,640]{1,0:T(8,128)(2,1)S(1)}, u32[]{:S(2)}, u32[]{:S(2)}) collective-permute-start(bf16[16,640]{1,0:T(8,128)(2,1)S(1)} %shard_map.98.p0), channel_id=1, source_target_pairs={{0,64},{64,0},{128,192},{192,128},{1,65},{65,1},{129,193},{193,129... | collective-permute-start | bytes 61448 | tf_op jit(solution)/shard_map/ppermute | solution.py:23
  30.1 3.8 %collective-permute-start.7 = (bf16[16,640]{1,0:T(8,128)(2,1)S(1)}, bf16[16,640]{1,0:T(8,128)(2,1)S(1)}, u32[]{:S(2)}, u32[]{:S(2)}) collective-permute-start(bf16[16,640]{1,0:T(8,128)(2,1)S(1)} %shard_map.98.p0), channel_id=1, source_target_pairs={{0,192},{64,128},{128,64},{192,0},{1,193},{65,129},{129,65},{193,1... | collective-permute-start | bytes 61448 | tf_op jit(solution)/shard_map/ppermute | solution.py:23
  34.3 3.1 %collective-permute-start.11 = (f32[64,256]{1,0:T(8,128)S(1)}, f32[64,256]{1,0:T(8,128)S(1)}, u32[]{:S(2)}, u32[]{:S(2)}) collective-permute-start(f32[64,256]{1,0:T(8,128)S(1)} %get-tuple-element.34), channel_id=1, source_target_pairs={{0,1},{1,0},{2,3},{3,2},{4,5},{5,4},{6,7},{7,6},{8,9},{9,8},{10,11... | collective-permute-start | bytes 196616 | tf_op jit(solution)/shard_map/ppermute | solution.py:23
  37.4 4.4 %collective-permute-start.12 = (s16[80,256]{1,0:T(8,128)(2,1)S(1)}, s16[80,256]{1,0:T(8,128)(2,1)S(1)}, u32[]{:S(2)}, u32[]{:S(2)}) collective-permute-start(s16[80,256]{1,0:T(8,128)(2,1)S(1)} %shard_map.101.a0), channel_id=1, source_target_pairs={{0,4},{2,6},{4,0},{6,2},{1,5},{3,7},{5,1},{7,3},{8,12},{10,14},{12... | collective-permute-start | bytes 122888 | tf_op jit(solution)/shard_map/ppermute | solution.py:23
  39.3 3.2 %collective-permute-start.13 = (s16[80,256]{1,0:T(8,128)(2,1)S(1)}, s16[80,256]{1,0:T(8,128)(2,1)S(1)}, u32[]{:S(2)}, u32[]{:S(2)}) collective-permute-start(s16[80,256]{1,0:T(8,128)(2,1)S(1)} %shard_map.101.a0), channel_id=1, source_target_pairs={{0,2},{2,0},{4,6},{6,4},{1,3},{3,1},{5,7},{7,5},{8,10},{10,8},{12,... | collective-permute-start | bytes 122888 | tf_op jit(solution)/shard_map/ppermute | solution.py:23
  39.6 4.1 %collective-permute-start.14 = (s16[80,256]{1,0:T(8,128)(2,1)S(1)}, s16[80,256]{1,0:T(8,128)(2,1)S(1)}, u32[]{:S(2)}, u32[]{:S(2)}) collective-permute-start(s16[80,256]{1,0:T(8,128)(2,1)S(1)} %shard_map.101.a0), channel_id=1, source_target_pairs={{0,6},{2,4},{4,2},{6,0},{1,7},{3,5},{5,3},{7,1},{8,14},{10,12},{12... | collective-permute-start | bytes 122888 | tf_op jit(solution)/shard_map/ppermute | solution.py:23
  43.7 4.2 %collective-permute-start.15 = (f32[16,256]{1,0:T(8,128)S(1)}, f32[16,256]{1,0:T(8,128)S(1)}, u32[]{:S(2)}, u32[]{:S(2)}) collective-permute-start(f32[16,256]{1,0:T(8,128)S(1)} %get-tuple-element.36.s2), channel_id=1, source_target_pairs={{0,128},{64,192},{128,0},{192,64},{1,129},{65,193},{129,1},{193,65... | collective-permute-start | bytes 49160 | tf_op jit(solution)/shard_map/ppermute | solution.py:23
  44.1 3.7 %collective-permute-start.16 = (f32[16,256]{1,0:T(8,128)S(1)}, f32[16,256]{1,0:T(8,128)S(1)}, u32[]{:S(2)}, u32[]{:S(2)}) collective-permute-start(f32[16,256]{1,0:T(8,128)S(1)} %get-tuple-element.37.s1), channel_id=1, source_target_pairs={{0,64},{64,0},{128,192},{192,128},{1,65},{65,1},{129,193},{193,129... | collective-permute-start | bytes 49160 | tf_op jit(solution)/shard_map/ppermute | solution.py:23
  44.5 3.8 %collective-permute-start.17 = (f32[16,256]{1,0:T(8,128)S(1)}, f32[16,256]{1,0:T(8,128)S(1)}, u32[]{:S(2)}, u32[]{:S(2)}) collective-permute-start(f32[16,256]{1,0:T(8,128)S(1)} %get-tuple-element.38.s3), channel_id=1, source_target_pairs={{0,192},{64,128},{128,64},{192,0},{1,193},{65,129},{129,65},{193,1... | collective-permute-start | bytes 49160 | tf_op jit(solution)/shard_map/ppermute | solution.py:23
  48.3 14.0 %collective-permute-start.18 = (f32[64,256]{1,0:T(8,128)S(1)}, f32[64,256]{1,0:T(8,128)S(1)}, u32[]{:S(2)}, u32[]{:S(2)}) collective-permute-start(f32[64,256]{1,0:T(8,128)S(1)} %pad_maximum_fusion.1.mine_ref), channel_id=1, source_target_pairs={{0,1},{1,0},{2,3},{3,2},{4,5},{5,4},{6,7},{7,6},{8,9},{9,8},{10,11... | collective-permute-start | bytes 196616 | tf_op jit(solution)/shard_map/ppermute | solution.py:23
  52.0 10.3 %all-to-all-start = ((f32[16,1,64]{2,1,0:T(1,128)}), f32[16,1,64]{2,1,0:T(1,128)S(1)}, u32[]{:S(2)}, u32[]{:S(2)}) async-start(f32[16,1,64]{2,1,0:T(1,128)} %bitcast.7), calls=%async_computation | async-start | bytes 16384 | tf_op jit(solution)/shard_map/all_to_all | solution.py:303

commit v9 on v8

--- a/solution.py
+++ b/solution.py
@@ -111,10 +111,21 @@
     )(*args)
 
 
+def factors(power):
+    half = jnp.floor(power * 0.5)
+    return jnp.exp2(half), jnp.exp2(power - half)
+
+
 def coded(value):
-    top = jnp.maximum(jnp.max(jnp.abs(value), 0, keepdims=True), 1e-30)
-    power = jnp.clip(jnp.floor(jnp.log2(top)) - 13.0, -100.0, 100.0)
-    return jnp.round(value / jnp.exp2(power)), power
+    top = jnp.maximum(jnp.max(jnp.abs(value), 0, keepdims=True), 1e-37)
+    power = jnp.floor(jnp.log2(top)) - 13.0
+    first, second = factors(power)
+    return jnp.round(value / first / second), power
+
+
+def decoded(code, power):
+    first, second = factors(power)
+    return code * first * second
 
 
 def spread_body(keep_ref, got_ref, s1_ref, s2_ref, s3_ref, in_ref, out_ref):
@@ -143,9 +154,9 @@
     low, half = in_ref[...], out_ref[...]
     for ref in (g1_ref, g2_ref, g3_ref):
         got = ref[...].astype(I32).astype(F32)
-        powers = jnp.exp2(got[ROWS + HALF :])
-        low = low + got[:ROWS] * powers[:1]
-        half = half + got[ROWS : ROWS + HALF] * powers[1:2]
+        powers = got[ROWS + HALF :]
+        low = low + decoded(got[:ROWS], powers[:1])
+        half = half + decoded(got[ROWS : ROWS + HALF], powers[1:2])
     low_ref[...] = low
     half_ref[...] = half
 
@@ -197,7 +208,7 @@
     parts = []
     for ref in (a0, a1, a2, a3):
         got = ref[...].astype(I32).astype(F32)
-        parts.append(got[:E_ALL] * jnp.exp2(got[E_ALL : E_ALL + 1]))
+        parts.append(decoded(got[:E_ALL], got[E_ALL : E_ALL + 1]))
     score = (parts[0] + parts[1]) + (parts[2] + parts[3])
     for d, ref in enumerate((s0, s1, s2, s3)):
         ref[...] = score[d * E_DEV : (d + 1) * E_DEV]

time: 63.1 us -> 63.2 us (level)
  no operation moved by 1% of the time
where the time goes in v9:
time: 63.2 us; the launch traced here: 63.1 us
  starting transfers between devices  35.3 us (56%)
  waiting for transfers between devices  19.6 us (31%)
  Pallas kernels  7.29 us (12%)
  between operations  0.74 us (1%)
    ppermute x19, starting transfers between devices, swap(): lax.ppermute(value, axis, [(i, i ^ bits) for i in range(SIZES[axis])])  31.9 us
    ppermute x19, waiting for transfers between devices, swap(): lax.ppermute(value, axis, [(i, i ^ bits) for i in range(SIZES[axis])])  12.8 us
    all_to_all x1, waiting for transfers between devices, per_device(): lax.all_to_all(slots, ('z', 'core'), 0, 0, tiled=True)  6.8 us
    pallas_call x1, Pallas kernels, project(): pl.pallas_call(project_body, in_specs=[pl.BlockSpec(memory_space=pltpu.HB...  4.77 us
    all_to_all x1, starting transfers between devices, per_device(): lax.all_to_all(slots, ('z', 'core'), 0, 0, tiled=True)  3.37 us
    pallas_call x9, Pallas kernels, call(): pl.pallas_call(run, out_shape=outs, in_specs=specs, scratch_shapes=scratc...  2.52 us
  transfers between devices with their start and end apart: 20, of which 13 were waited for; matrix products, arithmetic and copies ran while one was open for 0% of the time, Pallas kernels for 10%

profile of v9, /device:TPU:1, one launch (start us, length us, event | category | flops | bytes accessed | tf_op | source)
XLA Modules:
  0.0 63.1 jit_solution(13743934994442589040)
XLA Ops:
  0.7 6.5 %collective-permute-start.8 = (bf16[1,64,512]{2,1,0:T(8,128)(2,1)}, bf16[1,64,512]{2,1,0:T(8,128)(2,1)S(1)}, u32[]{:S(2)}, u32[]{:S(2)}) collective-permute-start(bf16[1,64,512]{2,1,0:T(8,128)(2,1)} %bitcast.16), channel_id=1, source_target_pairs={{0,56},{8,48},{16,40},{24,32},{32,24},{40,16},{48,8},{56,0},{1,57}... | collective-permute-start | bytes 196616 | tf_op jit(solution)/shard_map/ppermute | solution.py:23
  7.2 4.8 %shard_map.95 = (f32[64,1024]{1,0:T(8,128)S(1)}, f32[64,1024]{1,0:T(8,128)S(1)}, bf16[64,512]{1,0:T(8,128)(2,1)S(1)}) custom-call(bf16[1024,3584]{1,0:T(8,128)(2,1)} %x_hbm.1, bf16[1024,1024]{1,0:T(8,128)(2,1)} %y_hbm.1, bf16[64,3584]{1,0:T(8,128)(2,1)} %bitcast.14, bf16[64,1024]{1,0:T(8,128)(2,1)} %bitcast.15, bf16[64,512]{1,0:T(8,128)(2,1)} %h_hbm.1), custom_call_target="tpu_custom_call" | custom-call | flops 603979776 | bytes 9437184 | tf_op jit(solution)/shard_map/pallas_call | solution.py:95
  11.9 1.0 %collective-permute-start = (f32[64,1024]{1,0:T(8,128)S(1)}, f32[64,1024]{1,0:T(8,128)S(1)}, u32[]{:S(2)}, u32[]{:S(2)}) collective-permute-start(f32[64,1024]{1,0:T(8,128)S(1)} %get-tuple-element.24), channel_id=1, source_target_pairs={{0,1},{1,0},{2,3},{3,2},{4,5},{5,4},{6,7},{7,6},{8,9},{9,8},{10,11... | collective-permute-start | bytes 786440 | tf_op jit(solution)/shard_map/ppermute | solution.py:23
  13.0 2.2 %collective-permute-start.9 = (bf16[2,64,512]{2,1,0:T(8,128)(2,1)S(1)}, bf16[2,64,512]{2,1,0:T(8,128)(2,1)S(1)}, u32[]{:S(2)}, u32[]{:S(2)}) collective-permute-start(bf16[2,64,512]{2,1,0:T(8,128)(2,1)S(1)} %pad_maximum_fusion.refs_0_), channel_id=1, source_target_pairs={{0,16},{8,24},{16,0},{24,8},{32,48},{40,56},{48,32},{56,40},{1,17}... | collective-permute-start | bytes 393224 | tf_op jit(solution)/shard_map/ppermute | solution.py:23
  15.3 2.8 %collective-permute-start.1 = (s16[48,1024]{1,0:T(8,128)(2,1)S(1)}, s16[48,1024]{1,0:T(8,128)(2,1)S(1)}, u32[]{:S(2)}, u32[]{:S(2)}) collective-permute-start(s16[48,1024]{1,0:T(8,128)(2,1)S(1)} %get-tuple-element.27), channel_id=1, source_target_pairs={{0,4},{2,6},{4,0},{6,2},{1,5},{3,7},{5,1},{7,3},{8,12},{10,14},{12... | collective-permute-start | bytes 294920 | tf_op jit(solution)/shard_map/ppermute | solution.py:23
  18.5 0.5 collective-permute-start.3
  19.0 2.9 %collective-permute-done.9.refs_1_ = bf16[2,64,512]{2,1,0:T(8,128)(2,1)S(1)} collective-permute-done((bf16[2,64,512]{2,1,0:T(8,128)(2,1)S(1)}, bf16[2,64,512]{2,1,0:T(8,128)(2,1)S(1)}, u32[]{:S(2)}, u32[]{:S(2)}) %collective-permute-start.9) | collective-permute-done | bytes 131104 | tf_op jit(solution)/shard_map/ppermute | solution.py:23
  22.0 1.1 %collective-permute-done.2.g1_ref = s16[48,1024]{1,0:T(8,128)(2,1)S(1)} collective-permute-done((s16[48,1024]{1,0:T(8,128)(2,1)S(1)}, s16[48,1024]{1,0:T(8,128)(2,1)S(1)}, u32[]{:S(2)}, u32[]{:S(2)}) %collective-permute-start.2) | collective-permute-done | bytes 98336 | tf_op jit(solution)/shard_map/ppermute | solution.py:23
  23.3 2.1 %collective-permute-start.4 = (f32[32,1024]{1,0:T(8,128)S(1)}, f32[32,1024]{1,0:T(8,128)S(1)}, u32[]{:S(2)}, u32[]{:S(2)}) collective-permute-start(f32[32,1024]{1,0:T(8,128)S(1)} %get-tuple-element.31.mine_ref), channel_id=1, source_target_pairs={{0,1},{1,0},{2,3},{3,2},{4,5},{5,4},{6,7},{7,6},{8,9},{9,8},{10,11... | collective-permute-start | bytes 393224 | tf_op jit(solution)/shard_map/ppermute | solution.py:23
  25.4 0.9 %collective-permute-done.4.other_ref = f32[32,1024]{1,0:T(8,128)S(1)} collective-permute-done((f32[32,1024]{1,0:T(8,128)S(1)}, f32[32,1024]{1,0:T(8,128)S(1)}, u32[]{:S(2)}, u32[]{:S(2)}) %collective-permute-start.4) | collective-permute-done | bytes 131104 | tf_op jit(solution)/shard_map/ppermute | solution.py:23
  26.3 0.4 shard_map.98.p0
  26.8 3.0 %collective-permute-start.5 = (bf16[16,640]{1,0:T(8,128)(2,1)S(1)}, bf16[16,640]{1,0:T(8,128)(2,1)S(1)}, u32[]{:S(2)}, u32[]{:S(2)}) collective-permute-start(bf16[16,640]{1,0:T(8,128)(2,1)S(1)} %shard_map.98.p0), channel_id=1, source_target_pairs={{0,128},{64,192},{128,0},{192,64},{1,129},{65,193},{129,1},{193,65... | collective-permute-start | bytes 61448 | tf_op jit(solution)/shard_map/ppermute | solution.py:23
  29.8 0.4 collective-permute-start.6
  30.2 0.4 collective-permute-start.7
  30.5 0.4 collective-permute-done.5.p2
  31.0 1.4 %collective-permute-done.6.p1 = bf16[16,640]{1,0:T(8,128)(2,1)S(1)} collective-permute-done((bf16[16,640]{1,0:T(8,128)(2,1)S(1)}, bf16[16,640]{1,0:T(8,128)(2,1)S(1)}, u32[]{:S(2)}, u32[]{:S(2)}) %collective-permute-start.6) | collective-permute-done | bytes 20512 | tf_op jit(solution)/shard_map/ppermute | solution.py:23
  32.4 1.6 %collective-permute-done.7.p3 = bf16[16,640]{1,0:T(8,128)(2,1)S(1)} collective-permute-done((bf16[16,640]{1,0:T(8,128)(2,1)S(1)}, bf16[16,640]{1,0:T(8,128)(2,1)S(1)}, u32[]{:S(2)}, u32[]{:S(2)}) %collective-permute-start.7) | collective-permute-done | bytes 20512 | tf_op jit(solution)/shard_map/ppermute | solution.py:23
  34.3 2.2 %collective-permute-start.11 = (f32[64,256]{1,0:T(8,128)S(1)}, f32[64,256]{1,0:T(8,128)S(1)}, u32[]{:S(2)}, u32[]{:S(2)}) collective-permute-start(f32[64,256]{1,0:T(8,128)S(1)} %get-tuple-element.34), channel_id=1, source_target_pairs={{0,1},{1,0},{2,3},{3,2},{4,5},{5,4},{6,7},{7,6},{8,9},{9,8},{10,11... | collective-permute-start | bytes 196616 | tf_op jit(solution)/shard_map/ppermute | solution.py:23
  36.5 0.9 %collective-permute-done.11.got_ref = f32[64,256]{1,0:T(8,128)S(1)} collective-permute-done((f32[64,256]{1,0:T(8,128)S(1)}, f32[64,256]{1,0:T(8,128)S(1)}, u32[]{:S(2)}, u32[]{:S(2)}) %collective-permute-start.11) | collective-permute-done | bytes 65568 | tf_op jit(solution)/shard_map/ppermute | solution.py:23
  37.4 1.9 %collective-permute-start.12 = (s16[80,256]{1,0:T(8,128)(2,1)S(1)}, s16[80,256]{1,0:T(8,128)(2,1)S(1)}, u32[]{:S(2)}, u32[]{:S(2)}) collective-permute-start(s16[80,256]{1,0:T(8,128)(2,1)S(1)} %shard_map.101.a0), channel_id=1, source_target_pairs={{0,4},{2,6},{4,0},{6,2},{1,5},{3,7},{5,1},{7,3},{8,12},{10,14},{12... | collective-permute-start | bytes 122888 | tf_op jit(solution)/shard_map/ppermute | solution.py:23
  39.7 1.1 %collective-permute-start.14 = (s16[80,256]{1,0:T(8,128)(2,1)S(1)}, s16[80,256]{1,0:T(8,128)(2,1)S(1)}, u32[]{:S(2)}, u32[]{:S(2)}) collective-permute-start(s16[80,256]{1,0:T(8,128)(2,1)S(1)} %shard_map.101.a0), channel_id=1, source_target_pairs={{0,6},{2,4},{4,2},{6,0},{1,7},{3,5},{5,3},{7,1},{8,14},{10,12},{12... | collective-permute-start | bytes 122888 | tf_op jit(solution)/shard_map/ppermute | solution.py:23
  40.8 1.1 %collective-permute-done.12.a2 = s16[80,256]{1,0:T(8,128)(2,1)S(1)} collective-permute-done((s16[80,256]{1,0:T(8,128)(2,1)S(1)}, s16[80,256]{1,0:T(8,128)(2,1)S(1)}, u32[]{:S(2)}, u32[]{:S(2)}) %collective-permute-start.12) | collective-permute-done | bytes 40992 | tf_op jit(solution)/shard_map/ppermute | solution.py:23
  41.9 0.7 %collective-permute-done.13.a1 = s16[80,256]{1,0:T(8,128)(2,1)S(1)} collective-permute-done((s16[80,256]{1,0:T(8,128)(2,1)S(1)}, s16[80,256]{1,0:T(8,128)(2,1)S(1)}, u32[]{:S(2)}, u32[]{:S(2)}) %collective-permute-start.13) | collective-permute-done | bytes 40992 | tf_op jit(solution)/shard_map/ppermute | solution.py:23
  42.6 1.1 %collective-permute-done.14.a3 = s16[80,256]{1,0:T(8,128)(2,1)S(1)} collective-permute-done((s16[80,256]{1,0:T(8,128)(2,1)S(1)}, s16[80,256]{1,0:T(8,128)(2,1)S(1)}, u32[]{:S(2)}, u32[]{:S(2)}) %collective-permute-start.14) | collective-permute-done | bytes 40992 | tf_op jit(solution)/shard_map/ppermute | solution.py:23
  43.8 0.4 collective-permute-start.15
  44.5 2.6 %collective-permute-start.17 = (f32[16,256]{1,0:T(8,128)S(1)}, f32[16,256]{1,0:T(8,128)S(1)}, u32[]{:S(2)}, u32[]{:S(2)}) collective-permute-start(f32[16,256]{1,0:T(8,128)S(1)} %get-tuple-element.38.s3), channel_id=1, source_target_pairs={{0,192},{64,128},{128,64},{192,0},{1,193},{65,129},{129,65},{193,1... | collective-permute-start | bytes 49160 | tf_op jit(solution)/shard_map/ppermute | solution.py:23
  47.1 0.7 %shard_map.103 = f32[16,64]{1,0:T(8,128)} custom-call(f32[16,256]{1,0:T(8,128)S(1)} %get-tuple-element.35.s0, f32[16,256]{1,0:T(8,128)S(1)} %get-tuple-element.37.s1, f32[16,256]{1,0:T(8,128)S(1)} %get-tuple-element.36.s2, f32[16,256]{1,0:T(8,128)S(1)} %get-tuple-element.38.s3, f32[64,128]{1,0:T(8,128)S(1)} %get-tuple-element.39.goal_ref), custom_call_target="tpu_custom_call" | custom-call | tf_op jit(solution)/shard_map/pallas_call | solution.py:37
  48.0 0.4 collective-permute-done.17
  48.4 3.8 %collective-permute-start.18 = (f32[64,256]{1,0:T(8,128)S(1)}, f32[64,256]{1,0:T(8,128)S(1)}, u32[]{:S(2)}, u32[]{:S(2)}) collective-permute-start(f32[64,256]{1,0:T(8,128)S(1)} %pad_maximum_fusion.1.mine_ref), channel_id=1, source_target_pairs={{0,1},{1,0},{2,3},{3,2},{4,5},{5,4},{6,7},{7,6},{8,9},{9,8},{10,11... | collective-permute-start | bytes 196616 | tf_op jit(solution)/shard_map/ppermute | solution.py:23
  52.1 3.4 %all-to-all-start = ((f32[16,1,64]{2,1,0:T(1,128)}), f32[16,1,64]{2,1,0:T(1,128)S(1)}, u32[]{:S(2)}, u32[]{:S(2)}) async-start(f32[16,1,64]{2,1,0:T(1,128)} %bitcast.7), calls=%async_computation | async-start | bytes 16384 | tf_op jit(solution)/shard_map/all_to_all | solution.py:314
  55.6 6.8 %all-to-all-done = f32[16,1,64]{2,1,0:T(1,128)S(1)} async-done(((f32[16,1,64]{2,1,0:T(1,128)}), f32[16,1,64]{2,1,0:T(1,128)S(1)}, u32[]{:S(2)}, u32[]{:S(2)}) %all-to-all-start) | async-done | bytes 4128 | tf_op jit(solution)/shard_map/all_to_all | solution.py:314
  62.4 0.7 %shard_map.104 = (f32[16,2048]{1,0:T(8,128)}, f32[1,64]{1,0:T(1,128)}) custom-call(f32[64,256]{1,0:T(8,128)S(1)} %pad_maximum_fusion.1.mine_ref, f32[64,256]{1,0:T(8,128)S(1)} %collective-permute-done.18.other_ref, s32[1,2048]{1,0:T(1,128)S(1)} %bitcast.12, s32[32,64]{1,0:T(8,128)S(1)} %reshape.13.own_flag_ref, f32[16,64]{1,0:T(8,128)S(1)} %bitcast.13), custom_call_target="tpu_custom_call" | custom-call | tf_op jit(solution)/shard_map/pallas_call | solution.py:37
  (28 shorter events, 2.1 us)
Async XLA Ops:
  0.6 24.7 %copy-start.2 = (s32[16]{0:T(128)S(1)}, s32[16]{0:T(128)}, u32[]{:S(2)}) copy-start(s32[16]{0:T(128)} %param.13) | copy-start | bytes 196
  0.6 25.7 %copy-start.1 = (s32[1,1024]{1,0:T(1,128)S(1)}, s32[1,1024]{1,0:T(1,128)}, u32[]{:S(2)}) copy-start(s32[1,1024]{1,0:T(1,128)} %where_ref.1) | copy-start | bytes 12292
  0.7 54.9 %copy-start = (s32[2048]{0:T(1024)S(1)}, s32[2048]{0:T(1024)}, u32[]{:S(2)}) copy-start(s32[2048]{0:T(1024)} %param.14) | copy-start | bytes 24580
  0.7 12.3 %collective-permute-start.8 = (bf16[1,64,512]{2,1,0:T(8,128)(2,1)}, bf16[1,64,512]{2,1,0:T(8,128)(2,1)S(1)}, u32[]{:S(2)}, u32[]{:S(2)}) collective-permute-start(bf16[1,64,512]{2,1,0:T(8,128)(2,1)} %bitcast.16), channel_id=1, source_target_pairs={{0,56},{8,48},{16,40},{24,32},{32,24},{40,16},{48,8},{56,0},{1,57}... | collective-permute-start | bytes 196616 | tf_op jit(solution)/shard_map/ppermute | solution.py:23
  11.9 3.2 %collective-permute-start = (f32[64,1024]{1,0:T(8,128)S(1)}, f32[64,1024]{1,0:T(8,128)S(1)}, u32[]{:S(2)}, u32[]{:S(2)}) collective-permute-start(f32[64,1024]{1,0:T(8,128)S(1)} %get-tuple-element.24), channel_id=1, source_target_pairs={{0,1},{1,0},{2,3},{3,2},{4,5},{5,4},{6,7},{7,6},{8,9},{9,8},{10,11... | collective-permute-start | bytes 786440 | tf_op jit(solution)/shard_map/ppermute | solution.py:23
  13.0 8.9 %collective-permute-start.9 = (bf16[2,64,512]{2,1,0:T(8,128)(2,1)S(1)}, bf16[2,64,512]{2,1,0:T(8,128)(2,1)S(1)}, u32[]{:S(2)}, u32[]{:S(2)}) collective-permute-start(bf16[2,64,512]{2,1,0:T(8,128)(2,1)S(1)} %pad_maximum_fusion.refs_0_), channel_id=1, source_target_pairs={{0,16},{8,24},{16,0},{24,8},{32,48},{40,56},{48,32},{56,40},{1,17}... | collective-permute-start | bytes 393224 | tf_op jit(solution)/shard_map/ppermute | solution.py:23
  15.3 6.7 %collective-permute-start.1 = (s16[48,1024]{1,0:T(8,128)(2,1)S(1)}, s16[48,1024]{1,0:T(8,128)(2,1)S(1)}, u32[]{:S(2)}, u32[]{:S(2)}) collective-permute-start(s16[48,1024]{1,0:T(8,128)(2,1)S(1)} %get-tuple-element.27), channel_id=1, source_target_pairs={{0,4},{2,6},{4,0},{6,2},{1,5},{3,7},{5,1},{7,3},{8,12},{10,14},{12... | collective-permute-start | bytes 294920 | tf_op jit(solution)/shard_map/ppermute | solution.py:23
  18.1 5.0 %collective-permute-start.2 = (s16[48,1024]{1,0:T(8,128)(2,1)S(1)}, s16[48,1024]{1,0:T(8,128)(2,1)S(1)}, u32[]{:S(2)}, u32[]{:S(2)}) collective-permute-start(s16[48,1024]{1,0:T(8,128)(2,1)S(1)} %get-tuple-element.28), channel_id=1, source_target_pairs={{0,2},{2,0},{4,6},{6,4},{1,3},{3,1},{5,7},{7,5},{8,10},{10,8},{12,... | collective-permute-start | bytes 294920 | tf_op jit(solution)/shard_map/ppermute | solution.py:23
  18.5 4.7 %collective-permute-start.3 = (s16[48,1024]{1,0:T(8,128)(2,1)S(1)}, s16[48,1024]{1,0:T(8,128)(2,1)S(1)}, u32[]{:S(2)}, u32[]{:S(2)}) collective-permute-start(s16[48,1024]{1,0:T(8,128)(2,1)S(1)} %get-tuple-element.29), channel_id=1, source_target_pairs={{0,6},{2,4},{4,2},{6,0},{1,7},{3,5},{5,3},{7,1},{8,14},{10,12},{12... | collective-permute-start | bytes 294920 | tf_op jit(solution)/shard_map/ppermute | solution.py:23
  21.9 12.1 %collective-permute-start.10 = (bf16[4,64,512]{2,1,0:T(8,128)(2,1)S(1)}, bf16[4,64,512]{2,1,0:T(8,128)(2,1)S(1)}, u32[]{:S(2)}, u32[]{:S(2)}) collective-permute-start(bf16[4,64,512]{2,1,0:T(8,128)(2,1)S(1)} %shard_map.99.first_ref), channel_id=1, source_target_pairs={{0,8},{8,0},{16,24},{24,16},{32,40},{40,32},{48,56},{56,48},{1,9},... | collective-permute-start | bytes 786440 | tf_op jit(solution)/shard_map/ppermute | solution.py:23
  23.3 3.0 %collective-permute-start.4 = (f32[32,1024]{1,0:T(8,128)S(1)}, f32[32,1024]{1,0:T(8,128)S(1)}, u32[]{:S(2)}, u32[]{:S(2)}) collective-permute-start(f32[32,1024]{1,0:T(8,128)S(1)} %get-tuple-element.31.mine_ref), channel_id=1, source_target_pairs={{0,1},{1,0},{2,3},{3,2},{4,5},{5,4},{6,7},{7,6},{8,9},{9,8},{10,11... | collective-permute-start | bytes 393224 | tf_op jit(solution)/shard_map/ppermute | solution.py:23
  26.8 4.2 %collective-permute-start.5 = (bf16[16,640]{1,0:T(8,128)(2,1)S(1)}, bf16[16,640]{1,0:T(8,128)(2,1)S(1)}, u32[]{:S(2)}, u32[]{:S(2)}) collective-permute-start(bf16[16,640]{1,0:T(8,128)(2,1)S(1)} %shard_map.98.p0), channel_id=1, source_target_pairs={{0,128},{64,192},{128,0},{192,64},{1,129},{65,193},{129,1},{193,65... | collective-permute-start | bytes 61448 | tf_op jit(solution)/shard_map/ppermute | solution.py:23
  29.8 2.6 %collective-permute-start.6 = (bf16[16,640]{1,0:T(8,128)(2,1)S(1)}, bf16[16,640]{1,0:T(8,128)(2,1)S(1)}, u32[]{:S(2)}, u32[]{:S(2)}) collective-permute-start(bf16[16,640]{1,0:T(8,128)(2,1)S(1)} %shard_map.98.p0), channel_id=1, source_target_pairs={{0,64},{64,0},{128,192},{192,128},{1,65},{65,1},{129,193},{193,129... | collective-permute-start | bytes 61448 | tf_op jit(solution)/shard_map/ppermute | solution.py:23
  30.2 3.8 %collective-permute-start.7 = (bf16[16,640]{1,0:T(8,128)(2,1)S(1)}, bf16[16,640]{1,0:T(8,128)(2,1)S(1)}, u32[]{:S(2)}, u32[]{:S(2)}) collective-permute-start(bf16[16,640]{1,0:T(8,128)(2,1)S(1)} %shard_map.98.p0), channel_id=1, source_target_pairs={{0,192},{64,128},{128,64},{192,0},{1,193},{65,129},{129,65},{193,1... | collective-permute-start | bytes 61448 | tf_op jit(solution)/shard_map/ppermute | solution.py:23
  34.3 3.1 %collective-permute-start.11 = (f32[64,256]{1,0:T(8,128)S(1)}, f32[64,256]{1,0:T(8,128)S(1)}, u32[]{:S(2)}, u32[]{:S(2)}) collective-permute-start(f32[64,256]{1,0:T(8,128)S(1)} %get-tuple-element.34), channel_id=1, source_target_pairs={{0,1},{1,0},{2,3},{3,2},{4,5},{5,4},{6,7},{7,6},{8,9},{9,8},{10,11... | collective-permute-start | bytes 196616 | tf_op jit(solution)/shard_map/ppermute | solution.py:23
  37.4 4.4 %collective-permute-start.12 = (s16[80,256]{1,0:T(8,128)(2,1)S(1)}, s16[80,256]{1,0:T(8,128)(2,1)S(1)}, u32[]{:S(2)}, u32[]{:S(2)}) collective-permute-start(s16[80,256]{1,0:T(8,128)(2,1)S(1)} %shard_map.101.a0), channel_id=1, source_target_pairs={{0,4},{2,6},{4,0},{6,2},{1,5},{3,7},{5,1},{7,3},{8,12},{10,14},{12... | collective-permute-start | bytes 122888 | tf_op jit(solution)/shard_map/ppermute | solution.py:23
  39.3 3.2 %collective-permute-start.13 = (s16[80,256]{1,0:T(8,128)(2,1)S(1)}, s16[80,256]{1,0:T(8,128)(2,1)S(1)}, u32[]{:S(2)}, u32[]{:S(2)}) collective-permute-start(s16[80,256]{1,0:T(8,128)(2,1)S(1)} %shard_map.101.a0), channel_id=1, source_target_pairs={{0,2},{2,0},{4,6},{6,4},{1,3},{3,1},{5,7},{7,5},{8,10},{10,8},{12,... | collective-permute-start | bytes 122888 | tf_op jit(solution)/shard_map/ppermute | solution.py:23
  39.7 4.1 %collective-permute-start.14 = (s16[80,256]{1,0:T(8,128)(2,1)S(1)}, s16[80,256]{1,0:T(8,128)(2,1)S(1)}, u32[]{:S(2)}, u32[]{:S(2)}) collective-permute-start(s16[80,256]{1,0:T(8,128)(2,1)S(1)} %shard_map.101.a0), channel_id=1, source_target_pairs={{0,6},{2,4},{4,2},{6,0},{1,7},{3,5},{5,3},{7,1},{8,14},{10,12},{12... | collective-permute-start | bytes 122888 | tf_op jit(solution)/shard_map/ppermute | solution.py:23
  43.8 4.2 %collective-permute-start.15 = (f32[16,256]{1,0:T(8,128)S(1)}, f32[16,256]{1,0:T(8,128)S(1)}, u32[]{:S(2)}, u32[]{:S(2)}) collective-permute-start(f32[16,256]{1,0:T(8,128)S(1)} %get-tuple-element.36.s2), channel_id=1, source_target_pairs={{0,128},{64,192},{128,0},{192,64},{1,129},{65,193},{129,1},{193,65... | collective-permute-start | bytes 49160 | tf_op jit(solution)/shard_map/ppermute | solution.py:23
  44.2 3.7 %collective-permute-start.16 = (f32[16,256]{1,0:T(8,128)S(1)}, f32[16,256]{1,0:T(8,128)S(1)}, u32[]{:S(2)}, u32[]{:S(2)}) collective-permute-start(f32[16,256]{1,0:T(8,128)S(1)} %get-tuple-element.37.s1), channel_id=1, source_target_pairs={{0,64},{64,0},{128,192},{192,128},{1,65},{65,1},{129,193},{193,129... | collective-permute-start | bytes 49160 | tf_op jit(solution)/shard_map/ppermute | solution.py:23
  44.5 3.8 %collective-permute-start.17 = (f32[16,256]{1,0:T(8,128)S(1)}, f32[16,256]{1,0:T(8,128)S(1)}, u32[]{:S(2)}, u32[]{:S(2)}) collective-permute-start(f32[16,256]{1,0:T(8,128)S(1)} %get-tuple-element.38.s3), channel_id=1, source_target_pairs={{0,192},{64,128},{128,64},{192,0},{1,193},{65,129},{129,65},{193,1... | collective-permute-start | bytes 49160 | tf_op jit(solution)/shard_map/ppermute | solution.py:23
  48.4 14.0 %collective-permute-start.18 = (f32[64,256]{1,0:T(8,128)S(1)}, f32[64,256]{1,0:T(8,128)S(1)}, u32[]{:S(2)}, u32[]{:S(2)}) collective-permute-start(f32[64,256]{1,0:T(8,128)S(1)} %pad_maximum_fusion.1.mine_ref), channel_id=1, source_target_pairs={{0,1},{1,0},{2,3},{3,2},{4,5},{5,4},{6,7},{7,6},{8,9},{9,8},{10,11... | collective-permute-start | bytes 196616 | tf_op jit(solution)/shard_map/ppermute | solution.py:23
  52.1 10.3 %all-to-all-start = ((f32[16,1,64]{2,1,0:T(1,128)}), f32[16,1,64]{2,1,0:T(1,128)S(1)}, u32[]{:S(2)}, u32[]{:S(2)}) async-start(f32[16,1,64]{2,1,0:T(1,128)} %bitcast.7), calls=%async_computation | async-start | bytes 16384 | tf_op jit(solution)/shard_map/all_to_all | solution.py:314

commit v10 on v9

--- a/solution.py
+++ b/solution.py
@@ -230,12 +230,16 @@
         slots_ref[c * len(pieces) : (c + 1) * len(pieces)] = jnp.where(core == c, rows, 0.0)
 
 
-def lay_body(mine_ref, other_ref, flag_ref, own_flag_ref, slots_ref, out_ref, total_ref):
-    core, y, z = (lax.axis_index(name) for name in ("core", "y", "z"))
+def lay_body(mine_ref, other_ref, flag_ref, out_ref):
+    core, y = lax.axis_index("core"), lax.axis_index("y")
     for n, d in enumerate((0, 2, 1, 3)):
         for part, ref in ((core, mine_ref), (1 - core, other_ref)):
             at = pl.ds(pl.multiple_of((y ^ d) * C_ALL + part * C_HALF, C_HALF), C_HALF)
             out_ref[:, at] = ref[n * E_DEV : (n + 1) * E_DEV, :] * flag_ref[:, at].astype(F32)
+
+
+def finish_body(slots_ref, own_flag_ref, total_ref):
+    y, z = lax.axis_index("y"), lax.axis_index("z")
     flags = own_flag_ref[pl.ds(y * NZ + z, 1), :].astype(F32)
     total_ref[...] = jnp.sum(slots_ref[...], 0, keepdims=True) * flags
 
@@ -304,14 +308,19 @@
     got = {d: swap(pieces[d], "y", d) for d in (2, 1, 3)}
     mine = jnp.concatenate([pieces[0], got[2], got[1], got[3]], 0)
     mine, slots = lax.optimization_barrier((mine, slots))
-    sample_affinity, totals = call(
+    sample_affinity = call(
         lay_body,
-        [shaped(E_DEV, CHOICES), shaped(1, C_DEV)],
+        shaped(E_DEV, CHOICES),
         mine,
         swap(mine, "core", 1),
         kept_choice_flags.reshape(1, CHOICES),
+    )
+    totals = call(
+        finish_body,
+        shaped(1, C_DEV),
+        lax.all_to_all(slots, ("z", "core"), 0, 0, tiled=True),
         kept_choice_flags.reshape(NY * NZ, C_DEV),
-        lax.all_to_all(slots, ("z", "core"), 0, 0, tiled=True),
+        after=sample_affinity,
     )
     return (sample_affinity, totals[0])
 

time: 63.2 us -> 64 us (1.013)
  local copies, waits for them, and re-layouts: 0.17 us -> 1.07 us
    unnamed x6 -> x8, local copies, waits for them, and re-layouts: 0.01 us -> 0.92 us
    pallas_call x9 -> x10, Pallas kernels: 2.52 us -> 3.03 us  [call(): pl.pallas_call(run, out_shape=outs, in_specs=specs, scratch_shapes=scratc...]
  transfers between devices with their start and end apart: 20 -> 20, of which waited for: 13 -> 13; matrix products, arithmetic and copies ran while one was open for 0% -> 0% of each run, Pallas kernels for 10% -> 11%
where the time goes in v10:
time: 64 us; the launch traced here: 63.9 us
  starting transfers between devices  35.3 us (55%)
  waiting for transfers between devices  19 us (30%)
  Pallas kernels  7.8 us (12%)
  local copies, waits for them, and re-layouts  1.07 us (2%)
  between operations  0.75 us (1%)
    ppermute x19, starting transfers between devices, swap(): lax.ppermute(value, axis, [(i, i ^ bits) for i in range(SIZES[axis])])  31.9 us
    ppermute x19, waiting for transfers between devices, swap(): lax.ppermute(value, axis, [(i, i ^ bits) for i in range(SIZES[axis])])  12.8 us
    all_to_all x1, waiting for transfers between devices, per_device(): lax.all_to_all(slots, ('z', 'core'), 0, 0, tiled=True)  6.18 us
    pallas_call x1, Pallas kernels, project(): pl.pallas_call(project_body, in_specs=[pl.BlockSpec(memory_space=pltpu.HB...  4.77 us
    all_to_all x1, starting transfers between devices, per_device(): lax.all_to_all(slots, ('z', 'core'), 0, 0, tiled=True)  3.37 us
    pallas_call x10, Pallas kernels, call(): pl.pallas_call(run, out_shape=outs, in_specs=specs, scratch_shapes=scratc...  3.03 us
  transfers between devices with their start and end apart: 20, of which 13 were waited for; matrix products, arithmetic and copies ran while one was open for 0% of the time, Pallas kernels for 11%

profile of v10, /device:TPU:1, one launch (start us, length us, event | category | flops | bytes accessed | tf_op | source)
XLA Modules:
  0.0 63.9 jit_solution(3499263124761260267)
XLA Ops:
  0.7 6.5 %collective-permute-start.8 = (bf16[1,64,512]{2,1,0:T(8,128)(2,1)}, bf16[1,64,512]{2,1,0:T(8,128)(2,1)S(1)}, u32[]{:S(2)}, u32[]{:S(2)}) collective-permute-start(bf16[1,64,512]{2,1,0:T(8,128)(2,1)} %bitcast.16), channel_id=1, source_target_pairs={{0,56},{8,48},{16,40},{24,32},{32,24},{40,16},{48,8},{56,0},{1,57}... | collective-permute-start | bytes 196616 | tf_op jit(solution)/shard_map/ppermute | solution.py:23
  7.2 4.8 %shard_map.95 = (f32[64,1024]{1,0:T(8,128)S(1)}, f32[64,1024]{1,0:T(8,128)S(1)}, bf16[64,512]{1,0:T(8,128)(2,1)S(1)}) custom-call(bf16[1024,3584]{1,0:T(8,128)(2,1)} %x_hbm.1, bf16[1024,1024]{1,0:T(8,128)(2,1)} %y_hbm.1, bf16[64,3584]{1,0:T(8,128)(2,1)} %bitcast.14, bf16[64,1024]{1,0:T(8,128)(2,1)} %bitcast.15, bf16[64,512]{1,0:T(8,128)(2,1)} %h_hbm.1), custom_call_target="tpu_custom_call" | custom-call | flops 603979776 | bytes 9437184 | tf_op jit(solution)/shard_map/pallas_call | solution.py:95
  11.9 1.0 %collective-permute-start = (f32[64,1024]{1,0:T(8,128)S(1)}, f32[64,1024]{1,0:T(8,128)S(1)}, u32[]{:S(2)}, u32[]{:S(2)}) collective-permute-start(f32[64,1024]{1,0:T(8,128)S(1)} %get-tuple-element.22), channel_id=1, source_target_pairs={{0,1},{1,0},{2,3},{3,2},{4,5},{5,4},{6,7},{7,6},{8,9},{9,8},{10,11... | collective-permute-start | bytes 786440 | tf_op jit(solution)/shard_map/ppermute | solution.py:23
  13.0 2.2 %collective-permute-start.9 = (bf16[2,64,512]{2,1,0:T(8,128)(2,1)S(1)}, bf16[2,64,512]{2,1,0:T(8,128)(2,1)S(1)}, u32[]{:S(2)}, u32[]{:S(2)}) collective-permute-start(bf16[2,64,512]{2,1,0:T(8,128)(2,1)S(1)} %pad_maximum_fusion.refs_0_), channel_id=1, source_target_pairs={{0,16},{8,24},{16,0},{24,8},{32,48},{40,56},{48,32},{56,40},{1,17}... | collective-permute-start | bytes 393224 | tf_op jit(solution)/shard_map/ppermute | solution.py:23
  15.3 2.8 %collective-permute-start.1 = (s16[48,1024]{1,0:T(8,128)(2,1)S(1)}, s16[48,1024]{1,0:T(8,128)(2,1)S(1)}, u32[]{:S(2)}, u32[]{:S(2)}) collective-permute-start(s16[48,1024]{1,0:T(8,128)(2,1)S(1)} %get-tuple-element.25), channel_id=1, source_target_pairs={{0,4},{2,6},{4,0},{6,2},{1,5},{3,7},{5,1},{7,3},{8,12},{10,14},{12... | collective-permute-start | bytes 294920 | tf_op jit(solution)/shard_map/ppermute | solution.py:23
  18.5 0.5 collective-permute-start.3
  19.0 2.9 %collective-permute-done.9.refs_1_ = bf16[2,64,512]{2,1,0:T(8,128)(2,1)S(1)} collective-permute-done((bf16[2,64,512]{2,1,0:T(8,128)(2,1)S(1)}, bf16[2,64,512]{2,1,0:T(8,128)(2,1)S(1)}, u32[]{:S(2)}, u32[]{:S(2)}) %collective-permute-start.9) | collective-permute-done | bytes 131104 | tf_op jit(solution)/shard_map/ppermute | solution.py:23
  22.0 1.1 %collective-permute-done.2.g1_ref = s16[48,1024]{1,0:T(8,128)(2,1)S(1)} collective-permute-done((s16[48,1024]{1,0:T(8,128)(2,1)S(1)}, s16[48,1024]{1,0:T(8,128)(2,1)S(1)}, u32[]{:S(2)}, u32[]{:S(2)}) %collective-permute-start.2) | collective-permute-done | bytes 98336 | tf_op jit(solution)/shard_map/ppermute | solution.py:23
  23.3 2.1 %collective-permute-start.4 = (f32[32,1024]{1,0:T(8,128)S(1)}, f32[32,1024]{1,0:T(8,128)S(1)}, u32[]{:S(2)}, u32[]{:S(2)}) collective-permute-start(f32[32,1024]{1,0:T(8,128)S(1)} %get-tuple-element.29.mine_ref), channel_id=1, source_target_pairs={{0,1},{1,0},{2,3},{3,2},{4,5},{5,4},{6,7},{7,6},{8,9},{9,8},{10,11... | collective-permute-start | bytes 393224 | tf_op jit(solution)/shard_map/ppermute | solution.py:23
  25.4 0.9 %collective-permute-done.4.other_ref = f32[32,1024]{1,0:T(8,128)S(1)} collective-permute-done((f32[32,1024]{1,0:T(8,128)S(1)}, f32[32,1024]{1,0:T(8,128)S(1)}, u32[]{:S(2)}, u32[]{:S(2)}) %collective-permute-start.4) | collective-permute-done | bytes 131104 | tf_op jit(solution)/shard_map/ppermute | solution.py:23
  26.3 0.4 shard_map.98.p0
  26.8 3.0 %collective-permute-start.5 = (bf16[16,640]{1,0:T(8,128)(2,1)S(1)}, bf16[16,640]{1,0:T(8,128)(2,1)S(1)}, u32[]{:S(2)}, u32[]{:S(2)}) collective-permute-start(bf16[16,640]{1,0:T(8,128)(2,1)S(1)} %shard_map.98.p0), channel_id=1, source_target_pairs={{0,128},{64,192},{128,0},{192,64},{1,129},{65,193},{129,1},{193,65... | collective-permute-start | bytes 61448 | tf_op jit(solution)/shard_map/ppermute | solution.py:23
  29.8 0.4 collective-permute-start.6
  30.5 0.4 collective-permute-done.5.p2
  31.0 1.4 %collective-permute-done.6.p1 = bf16[16,640]{1,0:T(8,128)(2,1)S(1)} collective-permute-done((bf16[16,640]{1,0:T(8,128)(2,1)S(1)}, bf16[16,640]{1,0:T(8,128)(2,1)S(1)}, u32[]{:S(2)}, u32[]{:S(2)}) %collective-permute-start.6) | collective-permute-done | bytes 20512 | tf_op jit(solution)/shard_map/ppermute | solution.py:23
  32.4 1.6 %collective-permute-done.7.p3 = bf16[16,640]{1,0:T(8,128)(2,1)S(1)} collective-permute-done((bf16[16,640]{1,0:T(8,128)(2,1)S(1)}, bf16[16,640]{1,0:T(8,128)(2,1)S(1)}, u32[]{:S(2)}, u32[]{:S(2)}) %collective-permute-start.7) | collective-permute-done | bytes 20512 | tf_op jit(solution)/shard_map/ppermute | solution.py:23
  34.3 2.2 %collective-permute-start.11 = (f32[64,256]{1,0:T(8,128)S(1)}, f32[64,256]{1,0:T(8,128)S(1)}, u32[]{:S(2)}, u32[]{:S(2)}) collective-permute-start(f32[64,256]{1,0:T(8,128)S(1)} %get-tuple-element.32), channel_id=1, source_target_pairs={{0,1},{1,0},{2,3},{3,2},{4,5},{5,4},{6,7},{7,6},{8,9},{9,8},{10,11... | collective-permute-start | bytes 196616 | tf_op jit(solution)/shard_map/ppermute | solution.py:23
  36.5 0.9 %collective-permute-done.11.got_ref = f32[64,256]{1,0:T(8,128)S(1)} collective-permute-done((f32[64,256]{1,0:T(8,128)S(1)}, f32[64,256]{1,0:T(8,128)S(1)}, u32[]{:S(2)}, u32[]{:S(2)}) %collective-permute-start.11) | collective-permute-done | bytes 65568 | tf_op jit(solution)/shard_map/ppermute | solution.py:23
  37.4 1.9 %collective-permute-start.12 = (s16[80,256]{1,0:T(8,128)(2,1)S(1)}, s16[80,256]{1,0:T(8,128)(2,1)S(1)}, u32[]{:S(2)}, u32[]{:S(2)}) collective-permute-start(s16[80,256]{1,0:T(8,128)(2,1)S(1)} %shard_map.101.a0), channel_id=1, source_target_pairs={{0,4},{2,6},{4,0},{6,2},{1,5},{3,7},{5,1},{7,3},{8,12},{10,14},{12... | collective-permute-start | bytes 122888 | tf_op jit(solution)/shard_map/ppermute | solution.py:23
  39.7 1.1 %collective-permute-start.14 = (s16[80,256]{1,0:T(8,128)(2,1)S(1)}, s16[80,256]{1,0:T(8,128)(2,1)S(1)}, u32[]{:S(2)}, u32[]{:S(2)}) collective-permute-start(s16[80,256]{1,0:T(8,128)(2,1)S(1)} %shard_map.101.a0), channel_id=1, source_target_pairs={{0,6},{2,4},{4,2},{6,0},{1,7},{3,5},{5,3},{7,1},{8,14},{10,12},{12... | collective-permute-start | bytes 122888 | tf_op jit(solution)/shard_map/ppermute | solution.py:23
  40.8 1.1 %collective-permute-done.12.a2 = s16[80,256]{1,0:T(8,128)(2,1)S(1)} collective-permute-done((s16[80,256]{1,0:T(8,128)(2,1)S(1)}, s16[80,256]{1,0:T(8,128)(2,1)S(1)}, u32[]{:S(2)}, u32[]{:S(2)}) %collective-permute-start.12) | collective-permute-done | bytes 40992 | tf_op jit(solution)/shard_map/ppermute | solution.py:23
  41.9 0.7 %collective-permute-done.13.a1 = s16[80,256]{1,0:T(8,128)(2,1)S(1)} collective-permute-done((s16[80,256]{1,0:T(8,128)(2,1)S(1)}, s16[80,256]{1,0:T(8,128)(2,1)S(1)}, u32[]{:S(2)}, u32[]{:S(2)}) %collective-permute-start.13) | collective-permute-done | bytes 40992 | tf_op jit(solution)/shard_map/ppermute | solution.py:23
  42.6 1.1 %collective-permute-done.14.a3 = s16[80,256]{1,0:T(8,128)(2,1)S(1)} collective-permute-done((s16[80,256]{1,0:T(8,128)(2,1)S(1)}, s16[80,256]{1,0:T(8,128)(2,1)S(1)}, u32[]{:S(2)}, u32[]{:S(2)}) %collective-permute-start.14) | collective-permute-done | bytes 40992 | tf_op jit(solution)/shard_map/ppermute | solution.py:23
  43.8 0.4 collective-permute-start.15
  44.5 2.6 %collective-permute-start.17 = (f32[16,256]{1,0:T(8,128)S(1)}, f32[16,256]{1,0:T(8,128)S(1)}, u32[]{:S(2)}, u32[]{:S(2)}) collective-permute-start(f32[16,256]{1,0:T(8,128)S(1)} %get-tuple-element.36.s3), channel_id=1, source_target_pairs={{0,192},{64,128},{128,64},{192,0},{1,193},{65,129},{129,65},{193,1... | collective-permute-start | bytes 49160 | tf_op jit(solution)/shard_map/ppermute | solution.py:23
  47.1 0.7 %shard_map.103 = f32[16,64]{1,0:T(8,128)} custom-call(f32[16,256]{1,0:T(8,128)S(1)} %get-tuple-element.33.s0, f32[16,256]{1,0:T(8,128)S(1)} %get-tuple-element.35.s1, f32[16,256]{1,0:T(8,128)S(1)} %get-tuple-element.34.s2, f32[16,256]{1,0:T(8,128)S(1)} %get-tuple-element.36.s3, f32[64,128]{1,0:T(8,128)S(1)} %get-tuple-element.37.goal_ref), custom_call_target="tpu_custom_call" | custom-call | tf_op jit(solution)/shard_map/pallas_call | solution.py:37
  48.4 3.8 %collective-permute-start.18 = (f32[64,256]{1,0:T(8,128)S(1)}, f32[64,256]{1,0:T(8,128)S(1)}, u32[]{:S(2)}, u32[]{:S(2)}) collective-permute-start(f32[64,256]{1,0:T(8,128)S(1)} %pad_maximum_fusion.1.mine_ref), channel_id=1, source_target_pairs={{0,1},{1,0},{2,3},{3,2},{4,5},{5,4},{6,7},{7,6},{8,9},{9,8},{10,11... | collective-permute-start | bytes 196616 | tf_op jit(solution)/shard_map/ppermute | solution.py:23
  52.1 3.4 %all-to-all-start = ((f32[16,1,64]{2,1,0:T(1,128)}), f32[16,1,64]{2,1,0:T(1,128)S(1)}, u32[]{:S(2)}, u32[]{:S(2)}) async-start(f32[16,1,64]{2,1,0:T(1,128)} %bitcast.7), calls=%async_computation | async-start | bytes 16384 | tf_op jit(solution)/shard_map/all_to_all | solution.py:321
  55.6 0.7 %shard_map.104.refs_2_ = f32[16,2048]{1,0:T(8,128)} custom-call(f32[64,256]{1,0:T(8,128)S(1)} %pad_maximum_fusion.1.mine_ref, f32[64,256]{1,0:T(8,128)S(1)} %collective-permute-done.18.other_ref, s32[1,2048]{1,0:T(1,128)S(1)} %bitcast.12), custom_call_target="tpu_custom_call" | custom-call | tf_op jit(solution)/shard_map/pallas_call | solution.py:37
  56.3 6.2 %all-to-all-done = f32[16,1,64]{2,1,0:T(1,128)S(1)} async-done(((f32[16,1,64]{2,1,0:T(1,128)}), f32[16,1,64]{2,1,0:T(1,128)S(1)}, u32[]{:S(2)}, u32[]{:S(2)}) %all-to-all-start) | async-done | bytes 4128 | tf_op jit(solution)/shard_map/all_to_all | solution.py:321
  62.5 0.9 %copy-done = f32[16,2048]{1,0:T(8,128)S(1)} copy-done((f32[16,2048]{1,0:T(8,128)S(1)}, f32[16,2048]{1,0:T(8,128)}, u32[]{:S(2)}) %copy-start) | copy-done | bytes 131096
  63.4 0.5 shard_map.105
  (31 shorter events, 2.9 us)
Async XLA Ops:
  0.6 24.7 %copy-start.3 = (s32[16]{0:T(128)S(1)}, s32[16]{0:T(128)}, u32[]{:S(2)}) copy-start(s32[16]{0:T(128)} %param.13) | copy-start | bytes 196
  0.6 25.7 %copy-start.2 = (s32[1,1024]{1,0:T(1,128)S(1)}, s32[1,1024]{1,0:T(1,128)}, u32[]{:S(2)}) copy-start(s32[1,1024]{1,0:T(1,128)} %where_ref.1) | copy-start | bytes 12292
  0.7 54.9 %copy-start.1 = (s32[2048]{0:T(1024)S(1)}, s32[2048]{0:T(1024)}, u32[]{:S(2)}) copy-start(s32[2048]{0:T(1024)} %param.14) | copy-start | bytes 24580
  0.7 12.3 %collective-permute-start.8 = (bf16[1,64,512]{2,1,0:T(8,128)(2,1)}, bf16[1,64,512]{2,1,0:T(8,128)(2,1)S(1)}, u32[]{:S(2)}, u32[]{:S(2)}) collective-permute-start(bf16[1,64,512]{2,1,0:T(8,128)(2,1)} %bitcast.16), channel_id=1, source_target_pairs={{0,56},{8,48},{16,40},{24,32},{32,24},{40,16},{48,8},{56,0},{1,57}... | collective-permute-start | bytes 196616 | tf_op jit(solution)/shard_map/ppermute | solution.py:23
  11.9 3.2 %collective-permute-start = (f32[64,1024]{1,0:T(8,128)S(1)}, f32[64,1024]{1,0:T(8,128)S(1)}, u32[]{:S(2)}, u32[]{:S(2)}) collective-permute-start(f32[64,1024]{1,0:T(8,128)S(1)} %get-tuple-element.22), channel_id=1, source_target_pairs={{0,1},{1,0},{2,3},{3,2},{4,5},{5,4},{6,7},{7,6},{8,9},{9,8},{10,11... | collective-permute-start | bytes 786440 | tf_op jit(solution)/shard_map/ppermute | solution.py:23
  13.0 8.9 %collective-permute-start.9 = (bf16[2,64,512]{2,1,0:T(8,128)(2,1)S(1)}, bf16[2,64,512]{2,1,0:T(8,128)(2,1)S(1)}, u32[]{:S(2)}, u32[]{:S(2)}) collective-permute-start(bf16[2,64,512]{2,1,0:T(8,128)(2,1)S(1)} %pad_maximum_fusion.refs_0_), channel_id=1, source_target_pairs={{0,16},{8,24},{16,0},{24,8},{32,48},{40,56},{48,32},{56,40},{1,17}... | collective-permute-start | bytes 393224 | tf_op jit(solution)/shard_map/ppermute | solution.py:23
  15.3 6.7 %collective-permute-start.1 = (s16[48,1024]{1,0:T(8,128)(2,1)S(1)}, s16[48,1024]{1,0:T(8,128)(2,1)S(1)}, u32[]{:S(2)}, u32[]{:S(2)}) collective-permute-start(s16[48,1024]{1,0:T(8,128)(2,1)S(1)} %get-tuple-element.25), channel_id=1, source_target_pairs={{0,4},{2,6},{4,0},{6,2},{1,5},{3,7},{5,1},{7,3},{8,12},{10,14},{12... | collective-permute-start | bytes 294920 | tf_op jit(solution)/shard_map/ppermute | solution.py:23
  18.1 5.0 %collective-permute-start.2 = (s16[48,1024]{1,0:T(8,128)(2,1)S(1)}, s16[48,1024]{1,0:T(8,128)(2,1)S(1)}, u32[]{:S(2)}, u32[]{:S(2)}) collective-permute-start(s16[48,1024]{1,0:T(8,128)(2,1)S(1)} %get-tuple-element.26), channel_id=1, source_target_pairs={{0,2},{2,0},{4,6},{6,4},{1,3},{3,1},{5,7},{7,5},{8,10},{10,8},{12,... | collective-permute-start | bytes 294920 | tf_op jit(solution)/shard_map/ppermute | solution.py:23
  18.5 4.7 %collective-permute-start.3 = (s16[48,1024]{1,0:T(8,128)(2,1)S(1)}, s16[48,1024]{1,0:T(8,128)(2,1)S(1)}, u32[]{:S(2)}, u32[]{:S(2)}) collective-permute-start(s16[48,1024]{1,0:T(8,128)(2,1)S(1)} %get-tuple-element.27), channel_id=1, source_target_pairs={{0,6},{2,4},{4,2},{6,0},{1,7},{3,5},{5,3},{7,1},{8,14},{10,12},{12... | collective-permute-start | bytes 294920 | tf_op jit(solution)/shard_map/ppermute | solution.py:23
  21.9 12.1 %collective-permute-start.10 = (bf16[4,64,512]{2,1,0:T(8,128)(2,1)S(1)}, bf16[4,64,512]{2,1,0:T(8,128)(2,1)S(1)}, u32[]{:S(2)}, u32[]{:S(2)}) collective-permute-start(bf16[4,64,512]{2,1,0:T(8,128)(2,1)S(1)} %shard_map.99.first_ref), channel_id=1, source_target_pairs={{0,8},{8,0},{16,24},{24,16},{32,40},{40,32},{48,56},{56,48},{1,9},... | collective-permute-start | bytes 786440 | tf_op jit(solution)/shard_map/ppermute | solution.py:23
  23.3 3.0 %collective-permute-start.4 = (f32[32,1024]{1,0:T(8,128)S(1)}, f32[32,1024]{1,0:T(8,128)S(1)}, u32[]{:S(2)}, u32[]{:S(2)}) collective-permute-start(f32[32,1024]{1,0:T(8,128)S(1)} %get-tuple-element.29.mine_ref), channel_id=1, source_target_pairs={{0,1},{1,0},{2,3},{3,2},{4,5},{5,4},{6,7},{7,6},{8,9},{9,8},{10,11... | collective-permute-start | bytes 393224 | tf_op jit(solution)/shard_map/ppermute | solution.py:23
  26.8 4.2 %collective-permute-start.5 = (bf16[16,640]{1,0:T(8,128)(2,1)S(1)}, bf16[16,640]{1,0:T(8,128)(2,1)S(1)}, u32[]{:S(2)}, u32[]{:S(2)}) collective-permute-start(bf16[16,640]{1,0:T(8,128)(2,1)S(1)} %shard_map.98.p0), channel_id=1, source_target_pairs={{0,128},{64,192},{128,0},{192,64},{1,129},{65,193},{129,1},{193,65... | collective-permute-start | bytes 61448 | tf_op jit(solution)/shard_map/ppermute | solution.py:23
  29.8 2.6 %collective-permute-start.6 = (bf16[16,640]{1,0:T(8,128)(2,1)S(1)}, bf16[16,640]{1,0:T(8,128)(2,1)S(1)}, u32[]{:S(2)}, u32[]{:S(2)}) collective-permute-start(bf16[16,640]{1,0:T(8,128)(2,1)S(1)} %shard_map.98.p0), channel_id=1, source_target_pairs={{0,64},{64,0},{128,192},{192,128},{1,65},{65,1},{129,193},{193,129... | collective-permute-start | bytes 61448 | tf_op jit(solution)/shard_map/ppermute | solution.py:23
  30.2 3.8 %collective-permute-start.7 = (bf16[16,640]{1,0:T(8,128)(2,1)S(1)}, bf16[16,640]{1,0:T(8,128)(2,1)S(1)}, u32[]{:S(2)}, u32[]{:S(2)}) collective-permute-start(bf16[16,640]{1,0:T(8,128)(2,1)S(1)} %shard_map.98.p0), channel_id=1, source_target_pairs={{0,192},{64,128},{128,64},{192,0},{1,193},{65,129},{129,65},{193,1... | collective-permute-start | bytes 61448 | tf_op jit(solution)/shard_map/ppermute | solution.py:23
  34.3 3.1 %collective-permute-start.11 = (f32[64,256]{1,0:T(8,128)S(1)}, f32[64,256]{1,0:T(8,128)S(1)}, u32[]{:S(2)}, u32[]{:S(2)}) collective-permute-start(f32[64,256]{1,0:T(8,128)S(1)} %get-tuple-element.32), channel_id=1, source_target_pairs={{0,1},{1,0},{2,3},{3,2},{4,5},{5,4},{6,7},{7,6},{8,9},{9,8},{10,11... | collective-permute-start | bytes 196616 | tf_op jit(solution)/shard_map/ppermute | solution.py:23
  37.4 4.4 %collective-permute-start.12 = (s16[80,256]{1,0:T(8,128)(2,1)S(1)}, s16[80,256]{1,0:T(8,128)(2,1)S(1)}, u32[]{:S(2)}, u32[]{:S(2)}) collective-permute-start(s16[80,256]{1,0:T(8,128)(2,1)S(1)} %shard_map.101.a0), channel_id=1, source_target_pairs={{0,4},{2,6},{4,0},{6,2},{1,5},{3,7},{5,1},{7,3},{8,12},{10,14},{12... | collective-permute-start | bytes 122888 | tf_op jit(solution)/shard_map/ppermute | solution.py:23
  39.3 3.2 %collective-permute-start.13 = (s16[80,256]{1,0:T(8,128)(2,1)S(1)}, s16[80,256]{1,0:T(8,128)(2,1)S(1)}, u32[]{:S(2)}, u32[]{:S(2)}) collective-permute-start(s16[80,256]{1,0:T(8,128)(2,1)S(1)} %shard_map.101.a0), channel_id=1, source_target_pairs={{0,2},{2,0},{4,6},{6,4},{1,3},{3,1},{5,7},{7,5},{8,10},{10,8},{12,... | collective-permute-start | bytes 122888 | tf_op jit(solution)/shard_map/ppermute | solution.py:23
  39.7 4.1 %collective-permute-start.14 = (s16[80,256]{1,0:T(8,128)(2,1)S(1)}, s16[80,256]{1,0:T(8,128)(2,1)S(1)}, u32[]{:S(2)}, u32[]{:S(2)}) collective-permute-start(s16[80,256]{1,0:T(8,128)(2,1)S(1)} %shard_map.101.a0), channel_id=1, source_target_pairs={{0,6},{2,4},{4,2},{6,0},{1,7},{3,5},{5,3},{7,1},{8,14},{10,12},{12... | collective-permute-start | bytes 122888 | tf_op jit(solution)/shard_map/ppermute | solution.py:23
  43.8 4.2 %collective-permute-start.15 = (f32[16,256]{1,0:T(8,128)S(1)}, f32[16,256]{1,0:T(8,128)S(1)}, u32[]{:S(2)}, u32[]{:S(2)}) collective-permute-start(f32[16,256]{1,0:T(8,128)S(1)} %get-tuple-element.34.s2), channel_id=1, source_target_pairs={{0,128},{64,192},{128,0},{192,64},{1,129},{65,193},{129,1},{193,65... | collective-permute-start | bytes 49160 | tf_op jit(solution)/shard_map/ppermute | solution.py:23
  44.2 3.7 %collective-permute-start.16 = (f32[16,256]{1,0:T(8,128)S(1)}, f32[16,256]{1,0:T(8,128)S(1)}, u32[]{:S(2)}, u32[]{:S(2)}) collective-permute-start(f32[16,256]{1,0:T(8,128)S(1)} %get-tuple-element.35.s1), channel_id=1, source_target_pairs={{0,64},{64,0},{128,192},{192,128},{1,65},{65,1},{129,193},{193,129... | collective-permute-start | bytes 49160 | tf_op jit(solution)/shard_map/ppermute | solution.py:23
  44.5 3.8 %collective-permute-start.17 = (f32[16,256]{1,0:T(8,128)S(1)}, f32[16,256]{1,0:T(8,128)S(1)}, u32[]{:S(2)}, u32[]{:S(2)}) collective-permute-start(f32[16,256]{1,0:T(8,128)S(1)} %get-tuple-element.36.s3), channel_id=1, source_target_pairs={{0,192},{64,128},{128,64},{192,0},{1,193},{65,129},{129,65},{193,1... | collective-permute-start | bytes 49160 | tf_op jit(solution)/shard_map/ppermute | solution.py:23
  48.4 7.2 %collective-permute-start.18 = (f32[64,256]{1,0:T(8,128)S(1)}, f32[64,256]{1,0:T(8,128)S(1)}, u32[]{:S(2)}, u32[]{:S(2)}) collective-permute-start(f32[64,256]{1,0:T(8,128)S(1)} %pad_maximum_fusion.1.mine_ref), channel_id=1, source_target_pairs={{0,1},{1,0},{2,3},{3,2},{4,5},{5,4},{6,7},{7,6},{8,9},{9,8},{10,11... | collective-permute-start | bytes 196616 | tf_op jit(solution)/shard_map/ppermute | solution.py:23
  52.1 10.3 %all-to-all-start = ((f32[16,1,64]{2,1,0:T(1,128)}), f32[16,1,64]{2,1,0:T(1,128)S(1)}, u32[]{:S(2)}, u32[]{:S(2)}) async-start(f32[16,1,64]{2,1,0:T(1,128)} %bitcast.7), calls=%async_computation | async-start | bytes 16384 | tf_op jit(solution)/shard_map/all_to_all | solution.py:321
  62.5 0.9 %copy-start = (f32[16,2048]{1,0:T(8,128)S(1)}, f32[16,2048]{1,0:T(8,128)}, u32[]{:S(2)}) copy-start(f32[16,2048]{1,0:T(8,128)} %shard_map.104.refs_2_) | copy-start | bytes 393220
